TPU v7x, 32 devices: a whole 2x2x4 slice. The times are simulated.
32 devices in a mesh: dp: 16 (over z, y, core), tensor: 2 (over x).
Axes of the slice: x: 2, y: 2, z: 4, core: 2. Of those that a mesh axis runs over, the one named last changes fastest.
Arguments:
- block_input: bfloat16 [16384, 768], P(('dp', 'tensor')), may hold values from -6 to 6
- segment_index: int32 [16384], P('dp'), may hold values from 0 to 1, as said below
- output_cotangent: bfloat16 [16384, 768], P(('dp', 'tensor')), may hold values from -6 to 6
- triple_weight: bfloat16 [768, 3, 768], P(None, None, 'tensor')
- merge_weight: bfloat16 [768, 768], P(None, 'tensor'), may hold values from -0.21875 to 0.21875
- expand_weight: bfloat16 [768, 3072], P(None, 'tensor')
- contract_weight: bfloat16 [768, 3072], P(None, 'tensor'), may hold values from -0.109375 to 0.109375
- norm_gains: float32 [3, 768], replicated, may hold values from 0.25 to 1.75
- norm_biases: float32 [3, 768], replicated, may hold values from -3 to 3
- hidden_gain: float32 [3072], replicated, may hold values from 0.25 to 1.75
- hidden_bias: float32 [3072], replicated, may hold values from -3 to 3
Outputs:
- layer_output: bfloat16 [16384, 768], P(('dp', 'tensor'))
- input_gradient: bfloat16 [16384, 768], P(('dp', 'tensor'))
- triple_gradient: float32 [768, 3, 768], P('dp', None, 'tensor')
- merge_gradient: float32 [768, 768], P('dp', 'tensor')
- expand_gradient: float32 [768, 3072], P('dp', 'tensor')
- contract_gradient: float32 [768, 3072], P('dp', 'tensor')
- gains_gradient: float32 [3, 768], replicated
- biases_gradient: float32 [3, 768], replicated
- hidden_gain_gradient: float32 [3072], replicated
- hidden_bias_gradient: float32 [3072], replicated
Inputs may be any that keep to these rules, and one draw needn't show every extreme that they name: `segment_index`: the 1024 tokens of one dp index are aligned runs of 1024 tokens; each run is one sequence or 2 sequences of 512 tokens. Within one dp index equal values mark one sequence and values never fall.
All inputs are finite; a program needn't handle non-finite values.
Results may differ from a plain program's by a relative error of at most 0.019.
Values may be sent and summed in bfloat16 or wider, within the bound.
No kernel may reach another device: no remote copies, remote signals or barrier semaphores. Data moves between devices by JAX's collectives and lax.ppermute only.
A program may use at most 192 MiB of HBM per device.

v0:
```python
from functools import partial

import jax
import jax.numpy as jnp
from jax import lax
from jax.sharding import PartitionSpec as P

HEAD = 64


epsilon = 1e-05


def local_norm(values, norm_gain, norm_bias):
    centered = values - jnp.mean(values, axis=-1, keepdims=True)
    inverse = lax.rsqrt(jnp.mean(centered * centered, axis=-1, keepdims=True) + epsilon)
    normed = centered * inverse
    return (normed, inverse, normed * norm_gain + norm_bias)


def local_norm_back(upstream, normed, inverse, norm_gain):
    scaled = upstream * norm_gain
    return inverse * (
        scaled
        - jnp.mean(scaled, axis=-1, keepdims=True)
        - normed * jnp.mean(scaled * normed, axis=-1, keepdims=True)
    )


def row_sums(values):
    return lax.psum(values, "tensor")


def split_norm(values, full_width, norm_gain, norm_bias):
    means = row_sums(jnp.sum(values, axis=-1)) / full_width
    centered = values - means[:, None]
    variance = row_sums(jnp.sum(centered * centered, axis=-1)) / full_width
    inverse = lax.rsqrt(variance + epsilon)[:, None]
    normed = centered * inverse
    return (normed, inverse, normed * norm_gain + norm_bias)


def split_norm_back(upstream, normed, inverse, norm_gain, full_width):
    scaled = upstream * norm_gain
    totals, crossed = lax.psum(
        (jnp.sum(scaled, axis=-1), jnp.sum(scaled * normed, axis=-1)), "tensor"
    )
    return inverse * (
        scaled - totals[:, None] / full_width - normed * crossed[:, None] / full_width
    )


def masked_scores(query_rows, key_rows, segment, first_row, last_row):
    positions = lax.iota(jnp.int32, last_row)
    scores = (
        jnp.einsum("qhd,khd->hqk", query_rows, key_rows, preferred_element_type=jnp.float32) * 0.125
    )
    allowed = (segment[first_row:last_row, None] == segment[None, :last_row]) & (
        positions[None, :] <= positions[first_row:last_row, None]
    )
    return jnp.where(allowed[None], scores, -1e30)


def split_packed(packed, head_count):
    token_count = packed.shape[0]
    queries = packed[:, 0].reshape(token_count, head_count, HEAD)
    keys_all = packed[:, 1].reshape(token_count, head_count, HEAD)
    values_all = packed[:, 2].reshape(token_count, head_count, HEAD)
    return (token_count, queries, keys_all, values_all)


def attend_forward(packed, segment, head_count):
    token_count, queries, keys_all, values_all = split_packed(packed, head_count)
    block_rows = min(512, token_count)
    outputs = []
    log_sums = []
    for block_number in range(token_count // block_rows):
        first_row = block_number * block_rows
        last_row = first_row + block_rows
        scores = masked_scores(
            queries[first_row:last_row], keys_all[:last_row], segment, first_row, last_row
        )
        maxima = jnp.max(scores, axis=-1, keepdims=True)
        weights = jnp.exp(scores - maxima)
        totals = jnp.sum(weights, axis=-1, keepdims=True)
        shares_low = (weights / totals).astype(jnp.bfloat16)
        outputs.append(
            jnp.einsum(
                "hqk,khd->qhd",
                shares_low,
                values_all[:last_row],
                preferred_element_type=jnp.float32,
            )
        )
        log_sums.append((maxima + jnp.log(totals))[..., 0])
    attended = jnp.concatenate(outputs, axis=0).reshape(token_count, head_count * HEAD)
    return (attended, jnp.concatenate(log_sums, axis=1))


def attend_backward(packed, segment, log_sums, attended_grad, head_count):
    token_count, queries, keys_all, values_all = split_packed(packed, head_count)
    block_rows = min(512, token_count)
    upstream = attended_grad.reshape(token_count, head_count, HEAD)
    key_grads = jnp.zeros((token_count, head_count, HEAD), jnp.float32)
    value_grads = jnp.zeros((token_count, head_count, HEAD), jnp.float32)
    query_grads = []
    for block_number in range(token_count // block_rows):
        first_row = block_number * block_rows
        last_row = first_row + block_rows
        query_rows = queries[first_row:last_row]
        scores = masked_scores(query_rows, keys_all[:last_row], segment, first_row, last_row)
        shares = jnp.exp(scores - log_sums[:, first_row:last_row, None])
        shares_low = shares.astype(jnp.bfloat16)
        upstream_rows = upstream[first_row:last_row]
        value_grads = value_grads.at[:last_row].add(
            jnp.einsum(
                "hqk,qhd->khd", shares_low, upstream_rows, preferred_element_type=jnp.float32
            )
        )
        share_grads = jnp.einsum(
            "qhd,khd->hqk", upstream_rows, values_all[:last_row], preferred_element_type=jnp.float32
        )
        centre = jnp.sum(shares * share_grads, axis=-1, keepdims=True)
        score_grads = (shares * (share_grads - centre)).astype(jnp.bfloat16)
        query_grads.append(
            jnp.einsum(
                "hqk,khd->qhd", score_grads, keys_all[:last_row], preferred_element_type=jnp.float32
            )
            * 0.125
        )
        key_grads = key_grads.at[:last_row].add(
            jnp.einsum("hqk,qhd->khd", score_grads, query_rows, preferred_element_type=jnp.float32)
            * 0.125
        )
    stacked = jnp.stack([jnp.concatenate(query_grads, axis=0), key_grads, value_grads], axis=1)
    return stacked.reshape(token_count, 3, head_count * HEAD).astype(jnp.bfloat16)


def reduce_grads(grads):
    return (
        lax.psum_scatter(grads[0], "dp", scatter_dimension=0, tiled=True),
        lax.psum_scatter(grads[1], "dp", scatter_dimension=0, tiled=True),
        lax.psum_scatter(grads[2], "dp", scatter_dimension=0, tiled=True),
        lax.psum_scatter(grads[3], "dp", scatter_dimension=0, tiled=True),
    )


def place_into(piece, full_width, shard_index):
    return lax.dynamic_update_slice_in_dim(
        jnp.zeros((full_width,), jnp.float32), piece, shard_index * piece.shape[0], 0
    )


def body(
    block_input,
    segment_index,
    output_cotangent,
    triple_weight,
    merge_weight,
    expand_weight,
    contract_weight,
    norm_gains,
    norm_biases,
    hidden_gain,
    hidden_bias,
):
    row_count = block_input.shape[0]
    model_width = block_input.shape[1]
    local_width = triple_weight.shape[2]
    hidden_local = expand_weight.shape[1]
    hidden_width = hidden_gain.shape[0]
    head_count = local_width // HEAD
    shard_index = lax.axis_index("tensor")
    inner_gain = lax.dynamic_slice_in_dim(norm_gains[1], shard_index * local_width, local_width)
    inner_bias = lax.dynamic_slice_in_dim(norm_biases[1], shard_index * local_width, local_width)
    wide_gain = lax.dynamic_slice_in_dim(hidden_gain, shard_index * hidden_local, hidden_local)
    wide_bias = lax.dynamic_slice_in_dim(hidden_bias, shard_index * hidden_local, hidden_local)
    inputs = block_input.astype(jnp.float32)
    first_normed, first_inverse, first_out = local_norm(inputs, norm_gains[0], norm_biases[0])
    first_rows = lax.all_gather(first_out.astype(jnp.bfloat16), "tensor", axis=0, tiled=True)
    packed = jnp.einsum(
        "gd,dcf->gcf", first_rows, triple_weight, preferred_element_type=jnp.float32
    ).astype(jnp.bfloat16)
    attended, log_sums = attend_forward(packed, segment_index, head_count)
    inner_normed, inner_inverse, inner_out = split_norm(
        attended, model_width, inner_gain, inner_bias
    )
    inner_low = inner_out.astype(jnp.bfloat16)
    piece = inner_low
    merged = lax.psum_scatter(
        jnp.einsum("gi,oi->go", piece, merge_weight, preferred_element_type=jnp.float32).astype(
            jnp.bfloat16
        ),
        "tensor",
        scatter_dimension=0,
        tiled=True,
    ).astype(jnp.float32)
    middle = inputs + merged
    second_normed, second_inverse, second_out = local_norm(middle, norm_gains[2], norm_biases[2])
    second_rows = lax.all_gather(second_out.astype(jnp.bfloat16), "tensor", axis=0, tiled=True)
    expanded = jnp.dot(second_rows, expand_weight, preferred_element_type=jnp.float32)
    activated, gelu_back = jax.vjp(partial(jax.nn.gelu, approximate=False), expanded)
    hidden_normed, hidden_inverse, hidden_out = split_norm(
        activated, hidden_width, wide_gain, wide_bias
    )
    hidden_low = hidden_out.astype(jnp.bfloat16)
    piece = lax.slice_in_dim(hidden_low, 0, lax.axis_size("tensor") * row_count, axis=0)
    layer_output = (
        middle
        + lax.psum_scatter(
            jnp.einsum(
                "gf,df->gd", piece, contract_weight, preferred_element_type=jnp.float32
            ).astype(jnp.bfloat16),
            "tensor",
            scatter_dimension=0,
            tiled=True,
        ).astype(jnp.float32)
    ).astype(jnp.bfloat16)
    cotangent_rows = lax.all_gather(output_cotangent, "tensor", axis=0, tiled=True)
    contract_grad = jnp.einsum(
        "gd,gf->df", cotangent_rows, hidden_low, preferred_element_type=jnp.float32
    )
    hidden_grad = jnp.dot(cotangent_rows, contract_weight, preferred_element_type=jnp.float32)
    wide_gain_grad = jnp.sum(hidden_grad * hidden_normed, axis=0)
    wide_bias_grad = jnp.sum(hidden_grad, axis=0)
    activated_grad = split_norm_back(
        hidden_grad, hidden_normed, hidden_inverse, wide_gain, hidden_width
    )
    expanded_grad = gelu_back(activated_grad)[0].astype(jnp.bfloat16)
    expand_grad = jnp.einsum(
        "gd,gf->df", second_rows, expanded_grad, preferred_element_type=jnp.float32
    )
    piece = expanded_grad
    second_grad = lax.psum_scatter(
        jnp.einsum("gf,df->gd", piece, expand_weight, preferred_element_type=jnp.float32).astype(
            jnp.bfloat16
        ),
        "tensor",
        scatter_dimension=0,
        tiled=True,
    ).astype(jnp.float32)
    middle_grad = output_cotangent.astype(jnp.float32) + local_norm_back(
        second_grad, second_normed, second_inverse, norm_gains[2]
    )
    middle_rows = lax.all_gather(middle_grad.astype(jnp.bfloat16), "tensor", axis=0, tiled=True)
    merge_grad = jnp.einsum("go,gi->oi", middle_rows, inner_low, preferred_element_type=jnp.float32)
    inner_grad = jnp.dot(middle_rows, merge_weight, preferred_element_type=jnp.float32)
    inner_gain_grad = jnp.sum(inner_grad * inner_normed, axis=0)
    inner_bias_grad = jnp.sum(inner_grad, axis=0)
    attended_grad = split_norm_back(
        inner_grad, inner_normed, inner_inverse, inner_gain, model_width
    ).astype(jnp.bfloat16)
    packed_grad = attend_backward(packed, segment_index, log_sums, attended_grad, head_count)
    triple_grad = jnp.einsum(
        "gd,gcf->dcf", first_rows, packed_grad, preferred_element_type=jnp.float32
    )
    piece = packed_grad
    first_grad = lax.psum_scatter(
        jnp.einsum("gcf,dcf->gd", piece, triple_weight, preferred_element_type=jnp.float32).astype(
            jnp.bfloat16
        ),
        "tensor",
        scatter_dimension=0,
        tiled=True,
    ).astype(jnp.float32)
    input_gradient = (
        middle_grad + local_norm_back(first_grad, first_normed, first_inverse, norm_gains[0])
    ).astype(jnp.bfloat16)
    triple_total, merge_total, expand_total, contract_total = reduce_grads(
        (triple_grad, merge_grad, expand_grad, contract_grad)
    )
    gain_terms = jnp.stack(
        [
            jnp.sum(first_grad * first_normed, axis=0),
            place_into(inner_gain_grad, model_width, shard_index),
            jnp.sum(second_grad * second_normed, axis=0),
        ]
    )
    bias_terms = jnp.stack(
        [
            jnp.sum(first_grad, axis=0),
            place_into(inner_bias_grad, model_width, shard_index),
            jnp.sum(second_grad, axis=0),
        ]
    )
    gains_total, biases_total, wide_gain_total, wide_bias_total = lax.psum(
        (
            gain_terms,
            bias_terms,
            place_into(wide_gain_grad, hidden_width, shard_index),
            place_into(wide_bias_grad, hidden_width, shard_index),
        ),
        ("dp", "tensor"),
    )
    return (
        layer_output,
        input_gradient,
        triple_total,
        merge_total,
        expand_total,
        contract_total,
        gains_total,
        biases_total,
        wide_gain_total,
        wide_bias_total,
    )


def solution(mesh):
    return jax.shard_map(
        body,
        mesh=mesh,
        in_specs=(
            P(("dp", "tensor"), None),
            P("dp"),
            P(("dp", "tensor"), None),
            P(None, None, "tensor"),
            P(None, "tensor"),
            P(None, "tensor"),
            P(None, "tensor"),
            P(),
            P(),
            P(),
            P(),
        ),
        out_specs=(
            P(("dp", "tensor"), None),
            P(("dp", "tensor"), None),
            P("dp", None, "tensor"),
            P("dp", "tensor"),
            P("dp", "tensor"),
            P("dp", "tensor"),
            P(),
            P(),
            P(),
            P(),
        ),
        check_vma=False,
    )
```

profile of v0, /device:TPU:0, one launch (start us, length us, event | category | flops | bytes accessed | tf_op | source)
XLA Modules:
  0.0 700.0 jit_solution(14478442457511357781)
XLA Ops:
  17.7 26.5 %all-gather.5.cloned.1.call-done = bf16[1024,768]{1,0:T(8,128)(2,1)} async-done(((bf16[512,768]{1,0:T(8,128)(2,1)}), bf16[1024,768]{1,0:T(8,128)(2,1)}) %all-gather.5.cloned.1.call-update) | async-done | bytes 1572880 | tf_op jit(solution)/shard_map/all_gather | solution.py:180
  66.1 5.6 psum.84
  75.5 5.5 psum.85
  87.6 26.2 %reduce-scatter.11.cloned.1.call-done = bf16[512,768]{1,0:T(8,128)(2,1)} async-done(((bf16[1024,768]{1,0:T(8,128)(2,1)}), bf16[512,768]{1,0:T(8,128)(2,1)}) %reduce-scatter.11.cloned.1.call-update) | async-done | bytes 786448 | tf_op jit(solution)/shard_map/reduce_scatter | solution.py:190
  122.1 24.0 %all-gather.7.cloned.1.call-done = bf16[1024,768]{1,0:T(8,128)(2,1)} async-done(((bf16[512,768]{1,0:T(8,128)(2,1)}), bf16[1024,768]{1,0:T(8,128)(2,1)}) %all-gather.7.cloned.1.call-update) | async-done | bytes 1572880 | tf_op jit(solution)/shard_map/all_gather | solution.py:200
  146.1 19.4 %fusion.67 = (f32[1024]{0:T(1024)}, f32[1024,1536]{1,0:T(8,128)}, f32[1024,1536]{1,0:T(8,128)}, f32[1024,1536]{1,0:T(8,128)}) fusion(bf16[1024,768]{1,0:T(8,128)(2,1)} %all-gather.7.cloned.1.call-done, bf16[768,1536]{1,0:T(8,128)(2,1)S(1)} %copy-done), kind=kOutput, calls=%fused_computation.152 | convolution fusion | flops 2518154240 | bytes 22810624 | tf_op jit(solution)/shard_map/dot_general | solution.py:201
  165.6 5.7 psum.86
  172.5 4.1 multiply_reduce_fusion.4
  176.6 5.6 psum.87
  183.6 10.3 %multiply_reduce_fusion.1 = (f32[1536]{0:T(1024)}, f32[1024]{0:T(1024)}, f32[1024]{0:T(1024)}, f32[1536]{0:T(1024)}, f32[1024,1536]{1,0:T(8,128)}) fusion(f32[1024,1536]{1,0:T(8,128)} %get-tuple-element.123, f32[1024]{0:T(1024)} %add_rsqrt_fusion, f32[1024]{0:T(1024)} %copy-done.45, f32[1536]{0:T(1024)} %dynamic_slice.14, ...), kind=kOutput, calls=%fused_computation.11 | convolution fusion | flops 2430069760 | bytes 16549888 | tf_op jit(solution)/shard_map/dot_general | solution.py:223
  193.9 5.8 all-reduce.4
  200.4 12.3 %add_convert_fusion = (bf16[1024,1536]{1,0:T(8,128)(2,1)S(1)}, bf16[1024,1536]{1,0:T(8,128)(2,1)}) fusion(f32[1024,1536]{1,0:T(8,128)} %get-tuple-element.124, f32[1024,1536]{1,0:T(8,128)} %get-tuple-element.147, f32[1024,1536]{1,0:T(8,128)} %get-tuple-element.148, f32[1024,1536]{1,0:T(8,128)} %get-tuple-element.123, f32[1024]{0:T(1024)} %get-tuple-element.120, ...), kind=kLoop, calls=%fused_computation.16 | loop fusion | flops 39321600 | bytes 31485952 | tf_op jit(solution)/shard_map/convert_element_type | solution.py:229
  218.3 26.2 %reduce-scatter.15.cloned.1.call-done = bf16[512,768]{1,0:T(8,128)(2,1)} async-done(((bf16[1024,768]{1,0:T(8,128)(2,1)}), bf16[512,768]{1,0:T(8,128)(2,1)}) %reduce-scatter.15.cloned.1.call-update) | async-done | bytes 786448 | tf_op jit(solution)/shard_map/reduce_scatter | solution.py:234
  253.7 25.2 %all-gather.11.cloned.1.call-done = bf16[1024,768]{1,0:T(8,128)(2,1)} async-done(((bf16[512,768]{1,0:T(8,128)(2,1)}), bf16[1024,768]{1,0:T(8,128)(2,1)}) %all-gather.11.cloned.1.call-update) | async-done | bytes 1572880 | tf_op jit(solution)/shard_map/all_gather | solution.py:245
  278.9 4.4 multiply_reduce_fusion.6
  283.4 5.5 all-reduce.3
  291.1 4.0 fusion.52
  295.1 6.8 multiply_reduce_fusion.2
  302.0 6.4 multiply_convert_fusion.1
  314.9 7.0 multiply_reduce_fusion
  325.3 9.5 %multiply_convert_fusion = bf16[6,512,1024]{2,1,0:T(8,128)(2,1)S(1)} fusion(f32[6,512,1024]{2,1,0:T(8,128)} %get-tuple-element.153, f32[6,512,1024]{2,1,0:T(8,128)} %copy-done.2, f32[6,512]{1,0:T(8,128)} %get-tuple-element.152, f32[6,512]{1,0:T(8,128)S(1)} %log_add_fusion), kind=kLoop, calls=%fused_computation | loop fusion | flops 12582912 | bytes 31481856 | tf_op jit(solution)/shard_map/convert_element_type | solution.py:124
  339.9 5.4 bitcast_convert_fusion
  345.4 6.4 convolution_convert_fusion.3
  355.7 6.1 fusion.76
  363.2 6.8 convolution_bitcast_fusion
  370.0 6.1 copy.48
  377.5 5.4 fusion.46
  386.3 41.3 %all-reduce.2 = (f32[3,768]{1,0:T(4,128)}, f32[3,768]{1,0:T(4,128)}, f32[3072]{0:T(1024)}, f32[3072]{0:T(1024)}) all-reduce(f32[3,768]{1,0:T(4,128)S(1)} %pad_maximum_fusion.5, f32[3,768]{1,0:T(4,128)S(1)} %pad_maximum_fusion.6, f32[3072]{0:T(1024)S(1)} %dynamic_update_slice.16, ...), channel_id=1, replica_groups=mesh['dp'=16,'tensor'=2] {'dp','tensor'}, use_global_device_ids=true, to_apply=%region_41.42 | all-reduce | flops 10752 | bytes 86016 | tf_op jit(solution)/shard_map/psum | solution.py:286
  431.7 31.3 %reduce-scatter.21.cloned.1.call-done = f32[48,384]{1,0:T(8,128)} async-done(((f32[768,384]{1,0:T(8,128)}), f32[48,384]{1,0:T(8,128)}) %reduce-scatter.21.cloned.1.call-update) | async-done | bytes 73744 | tf_op jit(solution)/shard_map/reduce_scatter | solution.py:142
  463.0 78.8 %reduce-scatter.23.cloned.1.call-done = f32[48,1536]{1,0:T(8,128)} async-done(((f32[768,1536]{1,0:T(8,128)}), f32[48,1536]{1,0:T(8,128)}) %reduce-scatter.23.cloned.1.call-update) | async-done | bytes 294928 | tf_op jit(solution)/shard_map/reduce_scatter | solution.py:143
  541.8 79.5 %reduce-scatter.25.cloned.1.call-done = f32[48,1536]{1,0:T(8,128)} async-done(((f32[768,1536]{1,0:T(8,128)}), f32[48,1536]{1,0:T(8,128)}) %reduce-scatter.25.cloned.1.call-update) | async-done | bytes 294928
  621.3 71.4 %reduce-scatter.19.cloned.1.call-done = f32[48,3,384]{2,0,1:T(8,128)} async-done(((f32[768,3,384]{2,0,1:T(8,128)}), f32[48,3,384]{2,0,1:T(8,128)}) %reduce-scatter.19.cloned.1.call-update) | async-done | bytes 221200 | tf_op jit(solution)/shard_map/reduce_scatter | solution.py:141
  (237 shorter events, 99.5 us)
Async XLA Ops:
  7.2 138.9 %copy-start = (bf16[768,1536]{1,0:T(8,128)(2,1)S(1)}, bf16[768,1536]{1,0:T(8,128)(2,1)}, u32[]{:S(2)}) copy-start(bf16[768,1536]{1,0:T(8,128)(2,1)} %param.28) | copy-start | bytes 7077892
  7.2 37.0 %all-gather.5.cloned.1.call-start = ((), (), s32[]{:S(2)}) async-start(), calls=%async_computation.8 | async-start | bytes 2359296 | tf_op jit(solution)/shard_map/all_gather | solution.py:180
  8.7 39.4 %copy-start.40 = (f32[512]{0:T(512)}, f32[512]{0:T(512)S(1)}, u32[]{:S(2)}) copy-start(f32[512]{0:T(512)S(1)} %broadcast_multiply_fusion.9) | copy-start | bytes 6148
  10.2 37.9 %copy-start.46 = (f32[512]{0:T(512)}, f32[512]{0:T(512)S(1)}, u32[]{:S(2)}) copy-start(f32[512]{0:T(512)S(1)} %add_rsqrt_fusion.3) | copy-start | bytes 6148
  11.7 36.5 %copy-start.35 = (f32[768]{0:T(1024)}, f32[768]{0:T(1024)S(1)}, u32[]{:S(2)}) copy-start(f32[768]{0:T(1024)S(1)} %get-tuple-element.156) | copy-start | bytes 9220
  14.1 99.6 %reduce-scatter.11.cloned.1.call-start = ((), (), s32[]{:S(2)}) async-start(), calls=%async_computation.9 | async-start | bytes 2359296 | tf_op jit(solution)/shard_map/reduce_scatter | solution.py:190
  48.5 11.1 %copy-start.15 = (bf16[1024,1,384]{0,2,1:T(8,128)(2,1)}, bf16[1024,1,384]{0,2,1:T(8,128)(2,1)S(1)}, u32[]{:S(2)}) copy-start(bf16[1024,1,384]{0,2,1:T(8,128)(2,1)S(1)} %get-tuple-element.132) | copy-start | bytes 2359300
  54.4 11.0 %copy-start.17 = (f32[512,6,64]{0,2,1:T(8,128)}, f32[512,6,64]{0,2,1:T(8,128)S(1)}, u32[]{:S(2)}) copy-start(f32[512,6,64]{0,2,1:T(8,128)S(1)} %fusion.51) | copy-start | bytes 2359300
  81.6 32.2 %copy-start.4 = (bf16[512,768]{1,0:T(8,128)(2,1)S(1)}, bf16[512,768]{1,0:T(8,128)(2,1)}, u32[]{:S(2)}) copy-start(bf16[512,768]{1,0:T(8,128)(2,1)} %param.23) | copy-start | bytes 2359300
  87.5 58.6 %all-gather.7.cloned.1.call-start = ((), (), s32[]{:S(2)}) async-start(), calls=%async_computation.10 | async-start | bytes 2359296 | tf_op jit(solution)/shard_map/all_gather | solution.py:200
  118.7 64.8 %all-gather.9.cloned.1.call-start = ((), (), s32[]{:S(2)}) async-start(), calls=%async_computation.12 | async-start | bytes 2359296 | tf_op jit(solution)/shard_map/all_gather | solution.py:219
  119.3 125.2 %reduce-scatter.15.cloned.1.call-start = ((), (), s32[]{:S(2)}) async-start(), calls=%async_computation.13 | async-start | bytes 2359296 | tf_op jit(solution)/shard_map/reduce_scatter | solution.py:234
  218.2 30.3 %copy-start.6 = (bf16[512,768]{1,0:T(8,128)(2,1)S(1)}, bf16[512,768]{1,0:T(8,128)(2,1)}, u32[]{:S(2)}) copy-start(bf16[512,768]{1,0:T(8,128)(2,1)} %reduce-scatter.11.cloned.1.call-done) | copy-start | bytes 2359300
  218.3 60.7 %copy-start.7 = (f32[1024,6,64]{0,2,1:T(8,128)S(1)}, f32[1024,6,64]{0,2,1:T(8,128)}, u32[]{:S(2)}) copy-start(f32[1024,6,64]{0,2,1:T(8,128)} %get-tuple-element.136) | copy-start | bytes 4718596
  218.3 60.6 %all-gather.11.cloned.1.call-start = ((), (), s32[]{:S(2)}) async-start(), calls=%async_computation.14 | async-start | bytes 2359296 | tf_op jit(solution)/shard_map/all_gather | solution.py:245
  251.6 132.7 %reduce-scatter.17.cloned.1.call-start = ((), (), s32[]{:S(2)}) async-start(), calls=%async_computation.15 | async-start | bytes 2359296 | tf_op jit(solution)/shard_map/reduce_scatter | solution.py:258
  291.1 10.8 %slice-start.3 = ((s8[6291456]{0:T(1024)(128)(4,1)}), s8[4194304]{0:T(1024)(128)(4,1)S(1)}, s32[]{:S(2)}) async-start(s8[6291456]{0:T(1024)(128)(4,1)} %bitcast.96), calls=%async_computation.23 | async-start | bytes 8388608
  301.9 9.9 %copy-start.12 = (bf16[512,1,384]{0,2,1:T(8,128)(2,1)S(1)}, bf16[512,1,384]{0,2,1:T(8,128)(2,1)}, u32[]{:S(2)}) copy-start(bf16[512,1,384]{0,2,1:T(8,128)(2,1)} %copy-done.11) | copy-start | bytes 1179652
  301.9 12.9 %slice-start = ((s8[12582912]{0:T(1024)(128)(4,1)}), s8[4194304]{0:T(1024)(128)(4,1)S(1)}, s32[]{:S(2)}) async-start(s8[12582912]{0:T(1024)(128)(4,1)} %bitcast.94), calls=%async_computation.20 | async-start | bytes 8388608
  301.9 12.9 %slice-start.1 = ((s8[12582912]{0:T(1024)(128)(4,1)}), s8[4194304]{0:T(1024)(128)(4,1)S(1)}, s32[]{:S(2)}) async-start(s8[12582912]{0:T(1024)(128)(4,1)} %bitcast.94), calls=%async_computation.21 | async-start | bytes 8388608
  325.3 9.5 %copy-start.10 = (bf16[1024,1,384]{0,2,1:T(8,128)(2,1)S(1)}, bf16[1024,1,384]{0,2,1:T(8,128)(2,1)}, u32[]{:S(2)}) copy-start(bf16[1024,1,384]{0,2,1:T(8,128)(2,1)} %copy-done.9) | copy-start | bytes 2359300
  345.3 82.3 %reduce-scatter.13.cloned.1.call-start = ((), (), s32[]{:S(2)}) async-start(), calls=%async_computation.11 | async-start | bytes 2359296 | tf_op jit(solution)/shard_map/reduce_scatter | solution.py:210
  351.8 111.2 %reduce-scatter.21.cloned.1.call-start = ((), (), s32[]{:S(2)}) async-start(), calls=%async_computation.17 | async-start | bytes 1253376 | tf_op jit(solution)/shard_map/reduce_scatter | solution.py:142
  355.6 186.2 %reduce-scatter.23.cloned.1.call-start = ((), (), s32[]{:S(2)}) async-start(), calls=%async_computation.18 | async-start | bytes 5013504 | tf_op jit(solution)/shard_map/reduce_scatter | solution.py:143
  361.8 259.5 %reduce-scatter.25.cloned.1.call-start = ((), (), s32[]{:S(2)}) async-start(), calls=%async_computation.19 | async-start | bytes 5013504
  376.2 316.6 %reduce-scatter.19.cloned.1.call-start = ((), (), s32[]{:S(2)}) async-start(), calls=%async_computation.16 | async-start | bytes 3760128 | tf_op jit(solution)/shard_map/reduce_scatter | solution.py:141
  383.0 44.6 %copy-start.32 = (f32[768]{0:T(1024)S(1)}, f32[768]{0:T(1024)}, u32[]{:S(2)}) copy-start(f32[768]{0:T(1024)} %get-tuple-element.155) | copy-start | bytes 9220
  383.0 44.6 %copy-start.34 = (f32[512]{0:T(512)S(1)}, f32[512]{0:T(512)}, u32[]{:S(2)}) copy-start(f32[512]{0:T(512)} %copy-done.33) | copy-start | bytes 6148
  383.0 44.6 %copy-start.43 = (f32[512]{0:T(512)S(1)}, f32[512]{0:T(512)}, u32[]{:S(2)}) copy-start(f32[512]{0:T(512)} %copy-done.42) | copy-start | bytes 6148
  383.0 44.6 %copy-start.49 = (f32[512]{0:T(512)S(1)}, f32[512]{0:T(512)}, u32[]{:S(2)}) copy-start(f32[512]{0:T(512)} %copy-done.48) | copy-start | bytes 6148
  383.1 44.6 %copy-start.51 = (f32[512]{0:T(512)S(1)}, f32[512]{0:T(512)}, u32[]{:S(2)}) copy-start(f32[512]{0:T(512)} %copy-done.50) | copy-start | bytes 6148
  427.6 265.1 %copy-start.1 = (bf16[768,1536]{1,0:T(8,128)(2,1)S(1)}, bf16[768,1536]{1,0:T(8,128)(2,1)}, u32[]{:S(2)}) copy-start(bf16[768,1536]{1,0:T(8,128)(2,1)} %param.28) | copy-start | bytes 7077892
  (46 other events, 122.7 us)
Sparse Core Ops, SparseCore 0:
  14.2 29.8 all-gather.4
  87.6 26.0 reduce-scatter.10
  118.9 27.2 all-gather.6
  147.6 27.2 all-gather.8
  218.4 26.0 reduce-scatter.14
  251.7 27.2 all-gather.10
  345.4 26.0 reduce-scatter.16
  373.9 26.5 reduce-scatter.12
  404.7 58.1 reduce-scatter.20
  467.2 74.4 reduce-scatter.22
  546.7 74.5 reduce-scatter.24
  625.6 67.1 reduce-scatter.18
where the time goes:
time: 709 us; the launch traced here: 700 us
  waiting for transfers between devices  390 us (55%)
  matrix products  118 us (17%)
  blocking collectives  75.1 us (11%)
  other arithmetic  73 us (10%)
  local copies, waits for them, and re-layouts  28 us (4%)
  between operations  15.6 us (2%)
    unnamed x13, waiting for transfers between devices  80.2 us
    reduce_scatter x1, waiting for transfers between devices, reduce_grads(): lax.psum_scatter(grads[2], 'dp', scatter_dimension=0, tiled=True)  78.8 us
    reduce_scatter x1, waiting for transfers between devices, reduce_grads(): lax.psum_scatter(grads[0], 'dp', scatter_dimension=0, tiled=True)  71.4 us
    psum x1, blocking collectives, body(): lax.psum((gain_terms, bias_terms, place_into(wide_gain_grad, hidden_width...  41.3 us
    reduce_scatter x1, waiting for transfers between devices, reduce_grads(): lax.psum_scatter(grads[1], 'dp', scatter_dimension=0, tiled=True)  31.3 us
    all_gather x1, waiting for transfers between devices, body(): lax.all_gather(first_out.astype(jnp.bfloat16), 'tensor', axis=0, tiled=True)  26.5 us
    reduce_scatter x1, waiting for transfers between devices, body(): lax.psum_scatter(jnp.einsum('gf,df->gd', piece, expand_weight, preferred_...  26.2 us
    reduce_scatter x1, waiting for transfers between devices, body(): lax.psum_scatter(jnp.einsum('gi,oi->go', piece, merge_weight, preferred_e...  26.2 us
  transfers between devices with their start and end apart: 12, of which 9 were waited for; matrix products, arithmetic and copies ran while one was open for 11% of the time, Pallas kernels for 0%

commit v1 on v0

v1 whole, which is shorter than its diff:
```python
from functools import partial

import jax
import jax.numpy as jnp
from jax import lax
from jax.sharding import PartitionSpec as P

HEAD = 64

epsilon = 1e-05


def local_norm(values, norm_gain, norm_bias):
    centered = values - jnp.mean(values, axis=-1, keepdims=True)
    inverse = lax.rsqrt(jnp.mean(centered * centered, axis=-1, keepdims=True) + epsilon)
    normed = centered * inverse
    return (normed, inverse, normed * norm_gain + norm_bias)


def local_norm_back(upstream, normed, inverse, norm_gain):
    scaled = upstream * norm_gain
    return inverse * (
        scaled
        - jnp.mean(scaled, axis=-1, keepdims=True)
        - normed * jnp.mean(scaled * normed, axis=-1, keepdims=True)
    )


def masked_scores(query_rows, key_rows, segment, first_row, last_row):
    positions = lax.iota(jnp.int32, last_row)
    scores = (
        jnp.einsum("qhd,khd->hqk", query_rows, key_rows, preferred_element_type=jnp.float32) * 0.125
    )
    allowed = (segment[first_row:last_row, None] == segment[None, :last_row]) & (
        positions[None, :] <= positions[first_row:last_row, None]
    )
    return jnp.where(allowed[None], scores, -1e30)


def split_packed(packed, head_count):
    token_count = packed.shape[0]
    queries = packed[:, 0].reshape(token_count, head_count, HEAD)
    keys_all = packed[:, 1].reshape(token_count, head_count, HEAD)
    values_all = packed[:, 2].reshape(token_count, head_count, HEAD)
    return (token_count, queries, keys_all, values_all)


def attend_forward(packed, segment, head_count):
    token_count, queries, keys_all, values_all = split_packed(packed, head_count)
    block_rows = min(512, token_count)
    outputs = []
    log_sums = []
    for block_number in range(token_count // block_rows):
        first_row = block_number * block_rows
        last_row = first_row + block_rows
        scores = masked_scores(
            queries[first_row:last_row], keys_all[:last_row], segment, first_row, last_row
        )
        maxima = jnp.max(scores, axis=-1, keepdims=True)
        weights = jnp.exp(scores - maxima)
        totals = jnp.sum(weights, axis=-1, keepdims=True)
        shares_low = (weights / totals).astype(jnp.bfloat16)
        outputs.append(
            jnp.einsum(
                "hqk,khd->qhd",
                shares_low,
                values_all[:last_row],
                preferred_element_type=jnp.float32,
            )
        )
        log_sums.append((maxima + jnp.log(totals))[..., 0])
    attended = jnp.concatenate(outputs, axis=0).reshape(token_count, head_count * HEAD)
    return (attended, jnp.concatenate(log_sums, axis=1))


def attend_backward(packed, segment, log_sums, attended_grad, head_count):
    token_count, queries, keys_all, values_all = split_packed(packed, head_count)
    block_rows = min(512, token_count)
    upstream = attended_grad.reshape(token_count, head_count, HEAD)
    key_grads = jnp.zeros((token_count, head_count, HEAD), jnp.float32)
    value_grads = jnp.zeros((token_count, head_count, HEAD), jnp.float32)
    query_grads = []
    for block_number in range(token_count // block_rows):
        first_row = block_number * block_rows
        last_row = first_row + block_rows
        query_rows = queries[first_row:last_row]
        scores = masked_scores(query_rows, keys_all[:last_row], segment, first_row, last_row)
        shares = jnp.exp(scores - log_sums[:, first_row:last_row, None])
        shares_low = shares.astype(jnp.bfloat16)
        upstream_rows = upstream[first_row:last_row]
        value_grads = value_grads.at[:last_row].add(
            jnp.einsum(
                "hqk,qhd->khd", shares_low, upstream_rows, preferred_element_type=jnp.float32
            )
        )
        share_grads = jnp.einsum(
            "qhd,khd->hqk", upstream_rows, values_all[:last_row], preferred_element_type=jnp.float32
        )
        centre = jnp.sum(shares * share_grads, axis=-1, keepdims=True)
        score_grads = (shares * (share_grads - centre)).astype(jnp.bfloat16)
        query_grads.append(
            jnp.einsum(
                "hqk,khd->qhd", score_grads, keys_all[:last_row], preferred_element_type=jnp.float32
            )
            * 0.125
        )
        key_grads = key_grads.at[:last_row].add(
            jnp.einsum("hqk,qhd->khd", score_grads, query_rows, preferred_element_type=jnp.float32)
            * 0.125
        )
    stacked = jnp.stack([jnp.concatenate(query_grads, axis=0), key_grads, value_grads], axis=1)
    return stacked.reshape(token_count, 3, head_count * HEAD).astype(jnp.bfloat16)


def cross(values, bit):
    count = lax.axis_size("dp")
    return lax.ppermute(values, "dp", [(i, i ^ bit) for i in range(count)])


def cross_x(values):
    return lax.ppermute(values, "tensor", [(0, 1), (1, 0)])


def regroup(values):
    pairs = []
    for d in range(lax.axis_size("dp")):
        for t in range(2):
            here = d * 2 + t
            pairs.append((here, here if (d & 1) == t else (d ^ 1) * 2 + (t ^ 1)))
    return lax.ppermute(values, ("dp", "tensor"), pairs)


def ordered(flag, first, second, axis):
    return jnp.where(
        flag == 0,
        jnp.concatenate([first, second], axis=axis),
        jnp.concatenate([second, first], axis=axis),
    )


def add_low(a, b):
    return (a.astype(jnp.float32) + b.astype(jnp.float32)).astype(jnp.bfloat16)


def halve(values, bit_value, bit):
    count = values.shape[0]
    paired = values.reshape((count // 2, 2) + values.shape[1:])
    send = lax.dynamic_index_in_dim(paired, 1 - bit_value, axis=1, keepdims=False)
    keep = lax.dynamic_index_in_dim(paired, bit_value, axis=1, keepdims=False)
    return keep, cross(send, bit)


def finish_reduce(values, d, first_bit):
    count = lax.axis_size("dp")
    bit = first_bit
    while bit < count:
        keep, got = halve(values, (d // bit) % 2, bit)
        bit *= 2
        if bit < count:
            values = add_low(keep, got)
        else:
            values = keep.astype(jnp.float32) + got.astype(jnp.float32)
    return values[0]


def reduce_wide(gradient, d, c):
    count = lax.axis_size("dp")
    rows, columns = gradient.shape
    low = gradient.astype(jnp.bfloat16).reshape(count, rows // count, columns)
    keep, got = halve(low, c, 1)
    low = add_low(keep, got)
    half = columns // 2
    low = add_low(low[..., :half], cross_x(low[..., half:]))
    return finish_reduce(low, d, 2)


def sum_everywhere(values):
    values = values + cross_x(values)
    bit = 1
    while bit < lax.axis_size("dp"):
        values = values + cross(values, bit)
        bit *= 2
    return values


def fetch_foreign(weight, c, y):
    rows = weight.shape[0]
    quarter = rows // 4
    mine = lax.dynamic_slice_in_dim(weight, (c * 2 + y) * quarter, quarter, axis=0)
    got = cross_x(mine)
    relayed = cross(got, 2)
    half = ordered(y, got, relayed, 0)
    return ordered(c, half, cross(half, 1), 0)


def body(
    block_input,
    segment_index,
    output_cotangent,
    triple_weight,
    merge_weight,
    expand_weight,
    contract_weight,
    norm_gains,
    norm_biases,
    hidden_gain,
    hidden_bias,
):
    row_count, model_width = block_input.shape
    local_width = triple_weight.shape[2]
    sub_width = local_width // 2
    hidden_local = expand_weight.shape[1]
    head_count = sub_width // HEAD
    d = lax.axis_index("dp")
    t = lax.axis_index("tensor")
    c = d % 2
    y = (d // 2) % 2
    part = t * 2 + c

    rows_in = regroup(block_input)
    triple_local = lax.dynamic_slice_in_dim(triple_weight, c * sub_width, sub_width, axis=2)
    half_rows = model_width // 2
    got = cross_x(lax.dynamic_slice_in_dim(triple_local, y * half_rows, half_rows, axis=0))
    triple_foreign = ordered(y, got, cross(got, 2), 0)
    merge_foreign = fetch_foreign(merge_weight, c, y)
    expand_foreign = fetch_foreign(expand_weight, c, y)
    contract_foreign = fetch_foreign(contract_weight, c, y)
    cotangent = regroup(output_cotangent)
    segment = jnp.where(c == t, segment_index, cross(segment_index, 1))

    inputs = rows_in.astype(jnp.float32)
    first_normed, first_inverse, first_out = local_norm(inputs, norm_gains[0], norm_biases[0])
    first_low = first_out.astype(jnp.bfloat16)
    first_rows = ordered(c, first_low, cross(first_low, 1), 0)

    attended_parts = []
    kept = []
    for weight in (triple_local, triple_foreign):
        packed = jnp.einsum(
            "gd,dcf->gcf", first_rows, weight, preferred_element_type=jnp.float32
        ).astype(jnp.bfloat16)
        attended, log_sums = attend_forward(packed, segment, head_count)
        attended_parts.append(attended.astype(jnp.bfloat16))
        kept.append((packed, log_sums))
    attended = jnp.concatenate(attended_parts, axis=1)
    attended_send = lax.dynamic_slice_in_dim(attended, (1 - c) * row_count, row_count, axis=0)
    attended_keep = lax.dynamic_slice_in_dim(attended, c * row_count, row_count, axis=0)
    attended = jnp.concatenate([attended_keep, cross(attended_send, 1)], axis=1)
    order = (part, part ^ 2, part ^ 1, part ^ 3)

    def in_order(vector):
        return jnp.concatenate(
            [lax.dynamic_slice_in_dim(vector, p * sub_width, sub_width) for p in order]
        )

    inner_gain = in_order(norm_gains[1])
    inner_bias = in_order(norm_biases[1])
    local_c, local_o = (
        lax.dynamic_slice_in_dim(merge_weight, i * sub_width, sub_width, axis=1) for i in (c, 1 - c)
    )
    foreign_c, foreign_o = (
        lax.dynamic_slice_in_dim(merge_foreign, i * sub_width, sub_width, axis=1)
        for i in (c, 1 - c)
    )
    merge_all = jnp.concatenate([local_c, foreign_c, local_o, foreign_o], axis=1)
    inner_normed, inner_inverse, inner_out = local_norm(
        attended.astype(jnp.float32), inner_gain, inner_bias
    )
    inner_low = inner_out.astype(jnp.bfloat16)
    middle = inputs + jnp.einsum(
        "gi,oi->go", inner_low, merge_all, preferred_element_type=jnp.float32
    )
    second_normed, second_inverse, second_out = local_norm(middle, norm_gains[2], norm_biases[2])
    second_low = second_out.astype(jnp.bfloat16)
    expand_all = jnp.concatenate([expand_weight, expand_foreign], axis=1)
    contract_all = jnp.concatenate([contract_weight, contract_foreign], axis=1)

    def wide_order(vector):
        halves = vector.reshape(2, hidden_local)
        return jnp.where(t == 0, halves, halves[::-1]).reshape(-1)

    wide_gain = wide_order(hidden_gain)
    wide_bias = wide_order(hidden_bias)
    expanded = jnp.dot(second_low, expand_all, preferred_element_type=jnp.float32)
    activated, gelu_back = jax.vjp(partial(jax.nn.gelu, approximate=False), expanded)
    hidden_normed, hidden_inverse, hidden_out = local_norm(activated, wide_gain, wide_bias)
    hidden_low = hidden_out.astype(jnp.bfloat16)
    layer_output = regroup(
        (
            middle
            + jnp.einsum("gf,df->gd", hidden_low, contract_all, preferred_element_type=jnp.float32)
        ).astype(jnp.bfloat16)
    )
    contract_grad = jnp.einsum(
        "gd,gf->df", cotangent, hidden_low, preferred_element_type=jnp.float32
    )
    contract_total = reduce_wide(contract_grad, d, c)
    hidden_grad = jnp.dot(cotangent, contract_all, preferred_element_type=jnp.float32)
    wide_gain_grad = jnp.sum(hidden_grad * hidden_normed, axis=0)
    wide_bias_grad = jnp.sum(hidden_grad, axis=0)
    activated_grad = local_norm_back(hidden_grad, hidden_normed, hidden_inverse, wide_gain)
    expanded_grad = gelu_back(activated_grad)[0].astype(jnp.bfloat16)
    expand_grad = jnp.einsum(
        "gd,gf->df", second_low, expanded_grad, preferred_element_type=jnp.float32
    )
    expand_total = reduce_wide(expand_grad, d, c)
    second_grad = jnp.einsum(
        "gf,df->gd", expanded_grad, expand_all, preferred_element_type=jnp.float32
    )
    middle_grad = cotangent.astype(jnp.float32) + local_norm_back(
        second_grad, second_normed, second_inverse, norm_gains[2]
    )
    middle_low = middle_grad.astype(jnp.bfloat16)
    merge_grad = jnp.einsum("go,gi->oi", middle_low, inner_low, preferred_element_type=jnp.float32)
    merge_parts = jnp.split(merge_grad, 4, axis=1)
    merge_total = reduce_wide(
        jnp.concatenate(
            [
                ordered(c, merge_parts[0], merge_parts[2], 1),
                ordered(c, merge_parts[1], merge_parts[3], 1),
            ],
            axis=1,
        ),
        d,
        c,
    )
    inner_grad = jnp.dot(middle_low, merge_all, preferred_element_type=jnp.float32)
    inner_gain_grad = jnp.sum(inner_grad * inner_normed, axis=0)
    inner_bias_grad = jnp.sum(inner_grad, axis=0)
    attended_grad = local_norm_back(
        inner_grad, inner_normed, inner_inverse, inner_gain
    ).astype(jnp.bfloat16)

    def out_of_order(vector):
        parts = vector.reshape(4, sub_width)
        rows = []
        for p in range(4):
            i = part ^ p
            place = (i // 2) + (i % 2) * 2
            rows.append(lax.dynamic_index_in_dim(parts, place, 0, keepdims=False))
        return jnp.concatenate(rows)

    early = sum_everywhere(
        jnp.concatenate(
            [
                out_of_order(inner_gain_grad),
                out_of_order(inner_bias_grad),
                jnp.sum(second_grad * second_normed, axis=0),
                jnp.sum(second_grad, axis=0),
                wide_order(wide_gain_grad),
                wide_order(wide_bias_grad),
            ]
        )
    )

    attended_grad = ordered(
        c, attended_grad[:, :local_width], cross(attended_grad[:, local_width:], 1), 0
    )
    partial_grad = 0.0
    triple_grads = []
    for i, weight in enumerate((triple_local, triple_foreign)):
        packed, log_sums = kept[i]
        packed_grad = attend_backward(
            packed,
            segment,
            log_sums,
            attended_grad[:, i * sub_width : (i + 1) * sub_width],
            head_count,
        )
        triple_grads.append(
            jnp.einsum("gd,gcf->dcf", first_rows, packed_grad, preferred_element_type=jnp.float32)
        )
        partial_grad = partial_grad + jnp.einsum(
            "gcf,dcf->gd", packed_grad, weight, preferred_element_type=jnp.float32
        )
    triple_low = add_low(triple_grads[0], cross_x(triple_grads[1].astype(jnp.bfloat16)))
    count = lax.axis_size("dp")
    keep, got = halve(triple_low.reshape((count, -1) + triple_low.shape[1:]), c, 1)
    triple_total = finish_reduce(ordered(c, keep, got, 3), d, 2)

    partial_low = partial_grad.astype(jnp.bfloat16)
    first_grad = lax.dynamic_slice_in_dim(partial_grad, c * row_count, row_count, axis=0) + cross(
        lax.dynamic_slice_in_dim(partial_low, (1 - c) * row_count, row_count, axis=0), 1
    ).astype(jnp.float32)
    input_gradient = regroup(
        (
            middle_grad + local_norm_back(first_grad, first_normed, first_inverse, norm_gains[0])
        ).astype(jnp.bfloat16)
    )
    late = sum_everywhere(
        jnp.concatenate([jnp.sum(first_grad * first_normed, axis=0), jnp.sum(first_grad, axis=0)])
    )
    late = late.reshape(2, model_width)
    norms = early[: 4 * model_width].reshape(2, 2, model_width)
    wides = early[4 * model_width :].reshape(2, 2 * hidden_local)
    return (
        layer_output,
        input_gradient,
        triple_total,
        merge_total,
        expand_total,
        contract_total,
        jnp.stack([late[0], norms[0, 0], norms[1, 0]]),
        jnp.stack([late[1], norms[0, 1], norms[1, 1]]),
        wides[0],
        wides[1],
    )


def solution(mesh):
    return jax.shard_map(
        body,
        mesh=mesh,
        in_specs=(
            P(("dp", "tensor"), None),
            P("dp"),
            P(("dp", "tensor"), None),
            P(None, None, "tensor"),
            P(None, "tensor"),
            P(None, "tensor"),
            P(None, "tensor"),
            P(),
            P(),
            P(),
            P(),
        ),
        out_specs=(
            P(("dp", "tensor"), None),
            P(("dp", "tensor"), None),
            P("dp", None, "tensor"),
            P("dp", "tensor"),
            P("dp", "tensor"),
            P("dp", "tensor"),
            P(),
            P(),
            P(),
            P(),
        ),
        check_vma=False,
    )
```

time: 709 us -> 425 us (0.60)
  waiting for transfers between devices: 390 us -> 124 us
  blocking collectives: 75.1 us -> 0 us
  starting transfers between devices: 0.75 us -> 70.6 us
  local copies, waits for them, and re-layouts: 28 us -> 50.1 us
  matrix products: 118 us -> 104 us
  between operations: 15.6 us -> 3.05 us
    reduce_scatter x7 -> x0, waiting for transfers between devices: 234 us -> none  [the longest x1 78.8 us: reduce_grads(): lax.psum_scatter(grads[2], 'dp', scatter_dimension=0, tiled=True)]
    ppermute x0 -> x50, waiting for transfers between devices: none -> 124 us  [the longest x36 63.7 us: cross(): return lax.ppermute(values, 'dp', [(i, i ^ bit) for i in range(count)])]
    unnamed x13 -> x0, waiting for transfers between devices: 80.2 us -> none
    all_gather x4 -> x0, waiting for transfers between devices: 75.7 us -> none  [the longest x1 26.5 us: body(): lax.all_gather(first_out.astype(jnp.bfloat16), 'tensor', axis=0, tiled=True)]
    psum x7 -> x0, blocking collectives: 75.1 us -> none  [the longest x1 41.3 us: body(): lax.psum((gain_terms, bias_terms, place_into(wide_gain_grad, hidden_width...]
    ppermute x0 -> x50, starting transfers between devices: none -> 70.6 us  [the longest x36 43.1 us: cross(): return lax.ppermute(values, 'dp', [(i, i ^ bit) for i in range(count)])]
    dot_general x12 -> x11, matrix products: 79.1 us -> 57.3 us  [the longest x1 19.6 us: body(): jnp.dot(second_low, expand_all, preferred_element_type=jnp.float32)]
    select_n x0 -> x14, other arithmetic: none -> 15.6 us  [the longest x9 15.5 us: ordered(): jnp.where(flag == 0, jnp.concatenate([first, second], axis=axis), jnp.con...]
  transfers between devices with their start and end apart: 12 -> 50, of which waited for: 9 -> 20; matrix products, arithmetic and copies ran while one was open for 11% -> 35% of each run, Pallas kernels for 0% -> 0%
where the time goes in v1:
time: 425 us; the launch traced here: 420 us
  waiting for transfers between devices  124 us (29%)
  matrix products  104 us (24%)
  starting transfers between devices  70.6 us (17%)
  other arithmetic  67.8 us (16%)
  local copies, waits for them, and re-layouts  50.1 us (12%)
    ppermute x36, waiting for transfers between devices, cross(): return lax.ppermute(values, 'dp', [(i, i ^ bit) for i in range(count)])  63.7 us
    ppermute x10, waiting for transfers between devices, cross_x(): return lax.ppermute(values, 'tensor', [(0, 1), (1, 0)])  60.5 us
    ppermute x36, starting transfers between devices, cross(): return lax.ppermute(values, 'dp', [(i, i ^ bit) for i in range(count)])  43.1 us
    dot_general x1, matrix products, body(): jnp.dot(second_low, expand_all, preferred_element_type=jnp.float32)  19.6 us
    ppermute x4, starting transfers between devices, regroup(): return lax.ppermute(values, ('dp', 'tensor'), pairs)  18.1 us
    select_n x9, other arithmetic, ordered(): jnp.where(flag == 0, jnp.concatenate([first, second], axis=axis), jnp.con...  15.5 us
    dot_general x4, matrix products, attend_backward(): jnp.einsum('qhd,khd->hqk', upstream_rows, values_all[:last_row], preferre...  13.6 us
    unnamed x199, local copies, waits for them, and re-layouts  12.9 us
  transfers between devices with their start and end apart: 50, of which 20 were waited for; matrix products, arithmetic and copies ran while one was open for 35% of the time, Pallas kernels for 0%

profile of v1, /device:TPU:0, one launch (start us, length us, event | category | flops | bytes accessed | tf_op | source)
XLA Modules:
  0.0 419.8 jit_solution(4300160072350715837)
XLA Ops:
  26.3 3.4 collective-permute-done.7
  33.7 7.9 %collective-permute-start.16 = (bf16[512,768]{1,0:T(8,128)(2,1)}, bf16[512,768]{1,0:T(8,128)(2,1)}, u32[]{:S(2)}, u32[]{:S(2)}) collective-permute-start(bf16[512,768]{1,0:T(8,128)(2,1)} %param.37), channel_id=1, source_target_pairs={{0,0},{1,2},{2,1},{3,3},{4,4},{5,6},{6,5},{7,7},{8,8},{9,10},{10,9... | collective-permute-start | bytes 2359304 | tf_op jit(solution)/shard_map/ppermute | solution.py:130
  47.8 6.5 %collective-permute-start.1 = (bf16[512,768]{1,0:T(8,128)(2,1)S(1)}, bf16[512,768]{1,0:T(8,128)(2,1)S(1)}, u32[]{:S(2)}, u32[]{:S(2)}) collective-permute-start(bf16[512,768]{1,0:T(8,128)(2,1)S(1)} %fusion.44), channel_id=1, source_target_pairs={{0,2},{2,0},{4,6},{6,4},{8,10},{10,8},{12,14},{14,12},{16,18},{18,... | collective-permute-start | bytes 2359304 | tf_op jit(solution)/shard_map/ppermute | solution.py:117
  57.0 17.6 %collective-permute-done.10 = bf16[192,1536]{1,0:T(8,128)(2,1)S(1)} collective-permute-done((bf16[192,1536]{1,0:T(8,128)(2,1)}, bf16[192,1536]{1,0:T(8,128)(2,1)S(1)}, u32[]{:S(2)}, u32[]{:S(2)}) %collective-permute-start.10) | collective-permute-done | bytes 589856 | tf_op jit(solution)/shard_map/ppermute | solution.py:117
  109.4 6.6 %fusion.169 = (f32[3072]{0:T(1024)S(1)}, f32[3072,512]{1,0:T(8,128)}) fusion(bf16[512,768]{1,0:T(8,128)(2,1)} %collective-permute-done.16, bf16[768,1536]{1,0:T(8,128)(2,1)S(1)} %maximum_select_fusion.1, bf16[768,1536]{1,0:T(8,128)(2,1)S(1)} %copy-done.62), kind=kOutput, calls=%fused_computation.346 | convolution fusion | flops 2426926080 | bytes 11808768 | tf_op jit(solution)/shard_map/dot_general | solution.py:298
  115.9 6.5 %copy.105 = f32[3072,512]{0,1:T(8,128)} copy(f32[3072,512]{1,0:T(8,128)} %get-tuple-element.244) | data formatting | bytes 12582912 | tf_op jit(solution)/shard_map/dot_general | solution.py:298
  125.6 19.6 %fusion.152 = (f32[512]{0:T(512)S(1)}, f32[512,3072]{1,0:T(8,128)S(1)}, f32[512,3072]{1,0:T(8,128)}, f32[512,3072]{1,0:T(8,128)}) fusion(bf16[768,1536]{1,0:T(8,128)(2,1)S(1)} %maximum_select_fusion, bf16[768,1536]{1,0:T(8,128)(2,1)S(1)} %copy-done.61, f32[512,768]{1,0:T(8,128)S(1)} %get-tuple-element.231, f32[768]{0:T(1024)S(1)} %copy-done.82, ...), kind=kOutput, calls=%fused_computation.330 | convolution fusion | flops 2529558016 | bytes 25178112 | tf_op jit(solution)/shard_map/dot_general | solution.py:284
  146.0 2.9 fusion.1
  148.9 10.0 %add_convert_fusion = (bf16[512,3072]{1,0:T(8,128)(2,1)S(1)}, bf16[512,3072]{1,0:T(8,128)(2,1)}) fusion(f32[512,3072]{1,0:T(8,128)} %get-tuple-element.160, f32[512,3072]{1,0:T(8,128)} %get-tuple-element.232, f32[3072,512]{0,1:T(8,128)S(1)} %bitcast.270, f32[512,3072]{1,0:T(8,128)S(1)} %get-tuple-element.159, f32[512]{0:T(512)S(1)} %broadcast_multiply_fusion, ...), kind=kLoop, calls=%fused_computation.11 | loop fusion | flops 37748736 | bytes 31490048 | tf_op jit(solution)/shard_map/convert_element_type | solution.py:302
  158.9 6.4 %multiply_reduce_fusion.6 = (f32[768]{0:T(1024)S(1)}, f32[512]{0:T(512)S(1)}, f32[512]{0:T(512)S(1)}, f32[768]{0:T(1024)S(1)}, f32[512,768]{1,0:T(8,128)}) fusion(f32[512,768]{1,0:T(8,128)S(1)} %get-tuple-element.231, f32[512]{0:T(512)S(1)} %add_rsqrt_fusion.1, f32[512]{0:T(512)S(1)} %broadcast_multiply_fusion.9, f32[768]{0:T(1024)S(1)} %copy-done.73, ...), kind=kOutput, calls=%fused_computation.123 | convolution fusion | flops 2428892672 | bytes 11027456 | tf_op jit(solution)/shard_map/gf,df->gd/dot_general | solution.py:307
  165.3 4.9 %convolution_convert_fusion.1 = bf16[768,3072]{1,0:T(8,128)(2,1)} fusion(bf16[512,3072]{1,0:T(8,128)(2,1)S(1)} %get-tuple-element.161, f32[512,768]{1,0:T(8,128)S(1)} %get-tuple-element.231, f32[768]{0:T(1024)S(1)} %copy-done.82, f32[768]{0:T(1024)S(1)} %copy-done.73, f32[512]{0:T(512)S(1)} %add_rsqrt_fusion.1, f32[512]{0:T(512)S(1)} %broadcast_multiply_fusion.9), kind=kOutput, calls=%fused_computation.40 | convolution fusion | flops 2420244480 | bytes 9447424 | tf_op jit(solution)/shard_map/gd,gf->df/dot_general | solution.py:303
  170.5 6.8 %add_convert_fusion.5 = bf16[512,768]{1,0:T(8,128)(2,1)} fusion(f32[512,768]{1,0:T(8,128)S(1)} %get-tuple-element.231, bf16[512,3072]{1,0:T(8,128)(2,1)} %get-tuple-element.162, bf16[768,1536]{1,0:T(8,128)(2,1)} %copy-done.26, bf16[768,1536]{1,0:T(8,128)(2,1)} %param.41), kind=kOutput, calls=%fused_computation.129 | convolution fusion | flops 2426142720 | bytes 10223616 | tf_op jit(solution)/shard_map/gf,df->gd/dot_general | solution.py:291
  195.4 7.5 %collective-permute-start.15 = (bf16[512,768]{1,0:T(8,128)(2,1)}, bf16[512,768]{1,0:T(8,128)(2,1)}, u32[]{:S(2)}, u32[]{:S(2)}) collective-permute-start(bf16[512,768]{1,0:T(8,128)(2,1)} %add_convert_fusion.5), channel_id=1, source_target_pairs={{0,0},{1,2},{2,1},{3,3},{4,4},{5,6},{6,5},{7,7},{8,8},{9,10},{10,9... | collective-permute-start | bytes 2359304 | tf_op jit(solution)/shard_map/ppermute | solution.py:130
  204.7 4.2 %convolution_convert_fusion = bf16[3072,768]{0,1:T(8,128)(2,1)S(1)} fusion(bf16[512,3072]{1,0:T(8,128)(2,1)S(1)} %copy-done.25, bf16[512,768]{1,0:T(8,128)(2,1)} %collective-permute-done.16), kind=kOutput, calls=%fused_computation.39 | convolution fusion | flops 2418278400 | bytes 8650752 | tf_op jit(solution)/shard_map/gd,gf->df/dot_general | solution.py:294
  221.7 3.2 fusion.95
  225.0 4.8 %multiply_reduce_fusion.4 = (f32[3,512]{1,0:T(4,128)}, f32[3,512,512]{1,2,0:T(8,128)}) fusion(f32[3,512,512]{1,2,0:T(8,128)} %copy-done.4, f32[3,512]{1,0:T(4,128)S(1)} %log_add_fusion.1, bf16[512,3,64]{0,2,1:T(8,128)(2,1)S(1)} %bitcast.304, bf16[512,3,64]{0,2,1:T(8,128)(2,1)S(1)} %bitcast.350), kind=kOutput, calls=%fused_computation.54 | convolution fusion | flops 103021056 | bytes 6696960 | tf_op jit(solution)/shard_map/qhd,khd->hqk/dot_general | solution.py:96
  229.9 3.3 fusion.92
  242.3 4.1 multiply_reduce_fusion.1
  246.4 4.0 fusion.89
  270.8 8.4 %collective-permute-done.26 = bf16[8,48,384]{2,1,0:T(8,128)(2,1)S(1)} collective-permute-done((bf16[8,48,384]{2,1,0:T(8,128)(2,1)S(1)}, bf16[8,48,384]{2,1,0:T(8,128)(2,1)S(1)}, u32[]{:S(2)}, u32[]{:S(2)}) %collective-permute-start.26) | collective-permute-done | bytes 294944 | tf_op jit(solution)/shard_map/ppermute | solution.py:121
  280.9 4.0 collective-permute-done.27
  292.2 2.9 collective-permute-start.29
  295.1 13.2 %collective-permute-done.40 = f32[1536]{0:T(1024)S(1)} collective-permute-done((f32[1536]{0:T(1024)S(1)}, f32[1536]{0:T(1024)S(1)}, u32[]{:S(2)}, u32[]{:S(2)}) %collective-permute-start.40) | collective-permute-done | bytes 6176 | tf_op jit(solution)/shard_map/ppermute | solution.py:121
  313.8 3.4 collective-permute-done.43
  317.2 2.9 collective-permute-start.44
  324.6 7.4 %collective-permute-done.22 = bf16[4,48,3,384]{3,1,2,0:T(8,128)(2,1)S(1)} collective-permute-done((bf16[4,48,3,384]{3,1,2,0:T(8,128)(2,1)S(1)}, bf16[4,48,3,384]{3,1,2,0:T(8,128)(2,1)S(1)}, u32[]{:S(2)}, u32[]{:S(2)}) %collective-permute-start.22) | collective-permute-done | bytes 442400 | tf_op jit(solution)/shard_map/ppermute | solution.py:117
  332.6 3.3 fusion.13
  342.0 4.8 %collective-permute-done.24 = bf16[1,48,3,384]{3,1,2,0:T(8,128)(2,1)S(1)} collective-permute-done((bf16[1,48,3,384]{3,1,2,0:T(8,128)(2,1)S(1)}, bf16[1,48,3,384]{3,1,2,0:T(8,128)(2,1)S(1)}, u32[]{:S(2)}, u32[]{:S(2)}) %collective-permute-start.24) | collective-permute-done | bytes 110624 | tf_op jit(solution)/shard_map/ppermute | solution.py:117
  347.4 17.5 %collective-permute-done.31 = bf16[8,48,1536]{2,1,0:T(8,128)(2,1)S(1)} collective-permute-done((bf16[8,48,1536]{2,1,0:T(8,128)(2,1)S(1)}, bf16[8,48,1536]{2,1,0:T(8,128)(2,1)S(1)}, u32[]{:S(2)}, u32[]{:S(2)}) %collective-permute-start.31) | collective-permute-done | bytes 1179680 | tf_op jit(solution)/shard_map/ppermute | solution.py:121
  366.9 20.2 %collective-permute-done.36 = bf16[8,48,1536]{2,1,0:T(8,128)(2,1)S(1)} collective-permute-done((bf16[8,48,1536]{2,1,0:T(8,128)(2,1)S(1)}, bf16[8,48,1536]{2,1,0:T(8,128)(2,1)S(1)}, u32[]{:S(2)}, u32[]{:S(2)}) %collective-permute-start.36) | collective-permute-done | bytes 1179680 | tf_op jit(solution)/shard_map/ppermute | solution.py:121
  391.0 8.8 %collective-permute-done.37 = bf16[4,48,1536]{2,1,0:T(8,128)(2,1)S(1)} collective-permute-done((bf16[4,48,1536]{2,1,0:T(8,128)(2,1)S(1)}, bf16[4,48,1536]{2,1,0:T(8,128)(2,1)S(1)}, u32[]{:S(2)}, u32[]{:S(2)}) %collective-permute-start.37) | collective-permute-done | bytes 589856 | tf_op jit(solution)/shard_map/ppermute | solution.py:117
  402.7 5.1 %collective-permute-done.38 = bf16[2,48,1536]{2,1,0:T(8,128)(2,1)S(1)} collective-permute-done((bf16[2,48,1536]{2,1,0:T(8,128)(2,1)S(1)}, bf16[2,48,1536]{2,1,0:T(8,128)(2,1)S(1)}, u32[]{:S(2)}, u32[]{:S(2)}) %collective-permute-start.38) | collective-permute-done | bytes 294944 | tf_op jit(solution)/shard_map/ppermute | solution.py:117
  (488 shorter events, 184.6 us)
Async XLA Ops:
  0.7 21.8 %collective-permute-start.2 = (s32[1024]{0:T(1024)}, s32[1024]{0:T(1024)}, u32[]{:S(2)}, u32[]{:S(2)}) collective-permute-start(s32[1024]{0:T(1024)} %param.36), channel_id=1, source_target_pairs={{0,2},{2,0},{4,6},{6,4},{8,10},{10,8},{12,14},{14,12},{16,18},{18,... | collective-permute-start | bytes 12296 | tf_op jit(solution)/shard_map/ppermute | solution.py:117
  2.8 21.4 %collective-permute-start.6 = (bf16[192,384]{1,0:T(8,128)(2,1)}, bf16[192,384]{1,0:T(8,128)(2,1)}, u32[]{:S(2)}, u32[]{:S(2)}) collective-permute-start(bf16[192,384]{1,0:T(8,128)(2,1)} %constant_dynamic-slice_fusion.19), channel_id=1, source_target_pairs={{0,1},{1,0},{2,3},{3,2},{4,5},{5,4},{6,7},{7,6},{8,9},{9,8},{10,11... | collective-permute-start | bytes 442376 | tf_op jit(solution)/shard_map/ppermute | solution.py:121
  6.8 26.9 %collective-permute-start.3 = (bf16[384,3,192]{0,2,1:T(8,128)(2,1)}, bf16[384,3,192]{0,2,1:T(8,128)(2,1)}, u32[]{:S(2)}, u32[]{:S(2)}) collective-permute-start(bf16[384,3,192]{0,2,1:T(8,128)(2,1)} %copy.136), channel_id=1, source_target_pairs={{0,1},{1,0},{2,3},{3,2},{4,5},{5,4},{6,7},{7,6},{8,9},{9,8},{10,11... | collective-permute-start | bytes 1327112 | tf_op jit(solution)/shard_map/ppermute | solution.py:121
  8.8 34.6 %collective-permute-start.12 = (bf16[192,1536]{1,0:T(8,128)(2,1)}, bf16[192,1536]{1,0:T(8,128)(2,1)}, u32[]{:S(2)}, u32[]{:S(2)}) collective-permute-start(bf16[192,1536]{1,0:T(8,128)(2,1)} %constant_dynamic-slice_fusion.14), channel_id=1, source_target_pairs={{0,1},{1,0},{2,3},{3,2},{4,5},{5,4},{6,7},{7,6},{8,9},{9,8},{10,11... | collective-permute-start | bytes 1769480 | tf_op jit(solution)/shard_map/ppermute | solution.py:121
  12.6 32.2 %collective-permute-start.9 = (bf16[192,1536]{1,0:T(8,128)(2,1)}, bf16[192,1536]{1,0:T(8,128)(2,1)}, u32[]{:S(2)}, u32[]{:S(2)}) collective-permute-start(bf16[192,1536]{1,0:T(8,128)(2,1)} %constant_dynamic-slice_fusion.15), channel_id=1, source_target_pairs={{0,1},{1,0},{2,3},{3,2},{4,5},{5,4},{6,7},{7,6},{8,9},{9,8},{10,11... | collective-permute-start | bytes 1769480 | tf_op jit(solution)/shard_map/ppermute | solution.py:121
  22.4 24.4 %collective-permute-start = (bf16[512,768]{1,0:T(8,128)(2,1)}, bf16[512,768]{1,0:T(8,128)(2,1)S(1)}, u32[]{:S(2)}, u32[]{:S(2)}) collective-permute-start(bf16[512,768]{1,0:T(8,128)(2,1)} %param.35), channel_id=1, source_target_pairs={{0,0},{1,2},{2,1},{3,3},{4,4},{5,6},{6,5},{7,7},{8,8},{9,10},{10,9... | collective-permute-start | bytes 2359304 | tf_op jit(solution)/shard_map/ppermute | solution.py:130
  30.7 10.9 %collective-permute-start.8 = (bf16[384,384]{1,0:T(8,128)(2,1)S(1)}, bf16[384,384]{1,0:T(8,128)(2,1)S(1)}, u32[]{:S(2)}, u32[]{:S(2)}) collective-permute-start(bf16[384,384]{1,0:T(8,128)(2,1)S(1)} %maximum_select_fusion.11), channel_id=1, source_target_pairs={{0,2},{2,0},{4,6},{6,4},{8,10},{10,8},{12,14},{14,12},{16,18},{18,... | collective-permute-start | bytes 884744 | tf_op jit(solution)/shard_map/ppermute | solution.py:117
  33.7 75.4 %collective-permute-start.16 = (bf16[512,768]{1,0:T(8,128)(2,1)}, bf16[512,768]{1,0:T(8,128)(2,1)}, u32[]{:S(2)}, u32[]{:S(2)}) collective-permute-start(bf16[512,768]{1,0:T(8,128)(2,1)} %param.37), channel_id=1, source_target_pairs={{0,0},{1,2},{2,1},{3,3},{4,4},{5,6},{6,5},{7,7},{8,8},{9,10},{10,9... | collective-permute-start | bytes 2359304 | tf_op jit(solution)/shard_map/ppermute | solution.py:130
  41.6 13.9 %collective-permute-start.4 = (bf16[384,3,192]{0,2,1:T(8,128)(2,1)}, bf16[384,3,192]{0,2,1:T(8,128)(2,1)S(1)}, u32[]{:S(2)}, u32[]{:S(2)}) collective-permute-start(bf16[384,3,192]{0,2,1:T(8,128)(2,1)} %collective-permute-done.3), channel_id=1, source_target_pairs={{0,4},{2,6},{4,0},{6,2},{8,12},{10,14},{12,8},{14,10},{16,20},{18,... | collective-permute-start | bytes 1327112 | tf_op jit(solution)/shard_map/ppermute | solution.py:117
  43.4 33.8 %collective-permute-start.13 = (bf16[192,1536]{1,0:T(8,128)(2,1)}, bf16[192,1536]{1,0:T(8,128)(2,1)S(1)}, u32[]{:S(2)}, u32[]{:S(2)}) collective-permute-start(bf16[192,1536]{1,0:T(8,128)(2,1)} %collective-permute-done.12), channel_id=1, source_target_pairs={{0,4},{2,6},{4,0},{6,2},{8,12},{10,14},{12,8},{14,10},{16,20},{18,... | collective-permute-start | bytes 1769480 | tf_op jit(solution)/shard_map/ppermute | solution.py:117
  44.8 29.7 %collective-permute-start.10 = (bf16[192,1536]{1,0:T(8,128)(2,1)}, bf16[192,1536]{1,0:T(8,128)(2,1)S(1)}, u32[]{:S(2)}, u32[]{:S(2)}) collective-permute-start(bf16[192,1536]{1,0:T(8,128)(2,1)} %collective-permute-done.9), channel_id=1, source_target_pairs={{0,4},{2,6},{4,0},{6,2},{8,12},{10,14},{12,8},{14,10},{16,20},{18,... | collective-permute-start | bytes 1769480 | tf_op jit(solution)/shard_map/ppermute | solution.py:117
  47.8 32.6 %collective-permute-start.1 = (bf16[512,768]{1,0:T(8,128)(2,1)S(1)}, bf16[512,768]{1,0:T(8,128)(2,1)S(1)}, u32[]{:S(2)}, u32[]{:S(2)}) collective-permute-start(bf16[512,768]{1,0:T(8,128)(2,1)S(1)} %fusion.44), channel_id=1, source_target_pairs={{0,2},{2,0},{4,6},{6,4},{8,10},{10,8},{12,14},{14,12},{16,18},{18,... | collective-permute-start | bytes 2359304 | tf_op jit(solution)/shard_map/ppermute | solution.py:117
  77.2 45.3 %collective-permute-start.11 = (bf16[384,1536]{1,0:T(8,128)(2,1)}, bf16[384,1536]{1,0:T(8,128)(2,1)}, u32[]{:S(2)}, u32[]{:S(2)}) collective-permute-start(bf16[384,1536]{1,0:T(8,128)(2,1)} %maximum_select_fusion.3), channel_id=1, source_target_pairs={{0,2},{2,0},{4,6},{6,4},{8,10},{10,8},{12,14},{14,12},{16,18},{18,... | collective-permute-start | bytes 3538952 | tf_op jit(solution)/shard_map/ppermute | solution.py:117
  79.8 26.4 %collective-permute-start.14 = (bf16[384,1536]{1,0:T(8,128)(2,1)}, bf16[384,1536]{1,0:T(8,128)(2,1)}, u32[]{:S(2)}, u32[]{:S(2)}) collective-permute-start(bf16[384,1536]{1,0:T(8,128)(2,1)} %maximum_select_fusion.4), channel_id=1, source_target_pairs={{0,2},{2,0},{4,6},{6,4},{8,10},{10,8},{12,14},{14,12},{16,18},{18,... | collective-permute-start | bytes 3538952 | tf_op jit(solution)/shard_map/ppermute | solution.py:117
  191.2 28.0 %collective-permute-start.17 = (bf16[512,384]{1,0:T(8,128)(2,1)}, bf16[512,384]{1,0:T(8,128)(2,1)}, u32[]{:S(2)}, u32[]{:S(2)}) collective-permute-start(bf16[512,384]{1,0:T(8,128)(2,1)} %get-tuple-element.188), channel_id=1, source_target_pairs={{0,2},{2,0},{4,6},{6,4},{8,10},{10,8},{12,14},{14,12},{16,18},{18,... | collective-permute-start | bytes 1179656 | tf_op jit(solution)/shard_map/ppermute | solution.py:117
  195.3 73.2 %collective-permute-start.25 = (bf16[8,48,768]{2,1,0:T(8,128)(2,1)}, bf16[8,48,768]{2,1,0:T(8,128)(2,1)}, u32[]{:S(2)}, u32[]{:S(2)}) collective-permute-start(bf16[8,48,768]{2,1,0:T(8,128)(2,1)} %fusion.124), channel_id=1, source_target_pairs={{0,2},{2,0},{4,6},{6,4},{8,10},{10,8},{12,14},{14,12},{16,18},{18,... | collective-permute-start | bytes 1769480 | tf_op jit(solution)/shard_map/ppermute | solution.py:117
  195.4 92.6 %collective-permute-start.15 = (bf16[512,768]{1,0:T(8,128)(2,1)}, bf16[512,768]{1,0:T(8,128)(2,1)}, u32[]{:S(2)}, u32[]{:S(2)}) collective-permute-start(bf16[512,768]{1,0:T(8,128)(2,1)} %add_convert_fusion.5), channel_id=1, source_target_pairs={{0,0},{1,2},{2,1},{3,3},{4,4},{5,6},{6,5},{7,7},{8,8},{9,10},{10,9... | collective-permute-start | bytes 2359304 | tf_op jit(solution)/shard_map/ppermute | solution.py:130
  217.3 115.2 %collective-permute-start.30 = (bf16[8,48,3072]{2,1,0:T(8,128)(2,1)}, bf16[8,48,3072]{2,1,0:T(8,128)(2,1)}, u32[]{:S(2)}, u32[]{:S(2)}) collective-permute-start(bf16[8,48,3072]{2,1,0:T(8,128)(2,1)} %dynamic-slice_bitcast_fusion.1), channel_id=1, source_target_pairs={{0,2},{2,0},{4,6},{6,4},{8,10},{10,8},{12,14},{14,12},{16,18},{18,... | collective-permute-start | bytes 7077896 | tf_op jit(solution)/shard_map/ppermute | solution.py:117
  217.9 118.8 %collective-permute-start.35 = (bf16[8,48,3072]{2,1,0:T(8,128)(2,1)}, bf16[8,48,3072]{2,1,0:T(8,128)(2,1)}, u32[]{:S(2)}, u32[]{:S(2)}) collective-permute-start(bf16[8,48,3072]{2,1,0:T(8,128)(2,1)} %dynamic-slice_bitcast_fusion), channel_id=1, source_target_pairs={{0,2},{2,0},{4,6},{6,4},{8,10},{10,8},{12,14},{14,12},{16,18},{18,... | collective-permute-start | bytes 7077896 | tf_op jit(solution)/shard_map/ppermute | solution.py:117
  269.8 9.5 %collective-permute-start.26 = (bf16[8,48,384]{2,1,0:T(8,128)(2,1)S(1)}, bf16[8,48,384]{2,1,0:T(8,128)(2,1)S(1)}, u32[]{:S(2)}, u32[]{:S(2)}) collective-permute-start(bf16[8,48,384]{2,1,0:T(8,128)(2,1)S(1)} %slice.466), channel_id=1, source_target_pairs={{0,1},{1,0},{2,3},{3,2},{4,5},{5,4},{6,7},{7,6},{8,9},{9,8},{10,11... | collective-permute-start | bytes 884744 | tf_op jit(solution)/shard_map/ppermute | solution.py:121
  270.0 19.5 %collective-permute-start.18 = (bf16[512,768]{1,0:T(8,128)(2,1)S(1)}, bf16[512,768]{1,0:T(8,128)(2,1)S(1)}, u32[]{:S(2)}, u32[]{:S(2)}) collective-permute-start(bf16[512,768]{1,0:T(8,128)(2,1)S(1)} %dynamic-slice_convert_fusion), channel_id=1, source_target_pairs={{0,2},{2,0},{4,6},{6,4},{8,10},{10,8},{12,14},{14,12},{16,18},{18,... | collective-permute-start | bytes 2359304 | tf_op jit(solution)/shard_map/ppermute | solution.py:117
  288.0 22.1 %collective-permute-start.20 = (bf16[768,3,192]{0,2,1:T(8,128)(2,1)S(1)}, bf16[768,3,192]{0,2,1:T(8,128)(2,1)S(1)}, u32[]{:S(2)}, u32[]{:S(2)}) collective-permute-start(bf16[768,3,192]{0,2,1:T(8,128)(2,1)S(1)} %convert_element_type.335), channel_id=1, source_target_pairs={{0,1},{1,0},{2,3},{3,2},{4,5},{5,4},{6,7},{7,6},{8,9},{9,8},{10,11... | collective-permute-start | bytes 2654216 | tf_op jit(solution)/shard_map/ppermute | solution.py:121
  291.6 16.8 %collective-permute-start.40 = (f32[1536]{0:T(1024)S(1)}, f32[1536]{0:T(1024)S(1)}, u32[]{:S(2)}, u32[]{:S(2)}) collective-permute-start(f32[1536]{0:T(1024)S(1)} %pad_maximum_fusion.18), channel_id=1, source_target_pairs={{0,1},{1,0},{2,3},{3,2},{4,5},{5,4},{6,7},{7,6},{8,9},{9,8},{10,11... | collective-permute-start | bytes 18440 | tf_op jit(solution)/shard_map/ppermute | solution.py:121
  292.2 16.1 %collective-permute-start.29 = (bf16[1,48,384]{2,1,0:T(8,128)(2,1)S(1)}, bf16[1,48,384]{2,1,0:T(8,128)(2,1)S(1)}, u32[]{:S(2)}, u32[]{:S(2)}) collective-permute-start(bf16[1,48,384]{2,1,0:T(8,128)(2,1)S(1)} %constant_dynamic-slice_fusion.10), channel_id=1, source_target_pairs={{0,16},{2,18},{4,20},{6,22},{8,24},{10,26},{12,28},{14,30},{16,0},... | collective-permute-start | bytes 110600 | tf_op jit(solution)/shard_map/ppermute | solution.py:117
  320.9 11.2 %collective-permute-start.22 = (bf16[4,48,3,384]{3,1,2,0:T(8,128)(2,1)S(1)}, bf16[4,48,3,384]{3,1,2,0:T(8,128)(2,1)S(1)}, u32[]{:S(2)}, u32[]{:S(2)}) collective-permute-start(bf16[4,48,3,384]{3,1,2,0:T(8,128)(2,1)S(1)} %dynamic-slice_bitcast_fusion.4), channel_id=1, source_target_pairs={{0,4},{2,6},{4,0},{6,2},{8,12},{10,14},{12,8},{14,10},{16,20},{18,... | collective-permute-start | bytes 1327112 | tf_op jit(solution)/shard_map/ppermute | solution.py:117
  323.1 18.9 %collective-permute-start.19 = (bf16[512,768]{1,0:T(8,128)(2,1)S(1)}, bf16[512,768]{1,0:T(8,128)(2,1)S(1)}, u32[]{:S(2)}, u32[]{:S(2)}) collective-permute-start(bf16[512,768]{1,0:T(8,128)(2,1)S(1)} %fusion.49), channel_id=1, source_target_pairs={{0,0},{1,2},{2,1},{3,3},{4,4},{5,6},{6,5},{7,7},{8,8},{9,10},{10,9... | collective-permute-start | bytes 2359304 | tf_op jit(solution)/shard_map/ppermute | solution.py:130
  336.0 29.0 %collective-permute-start.31 = (bf16[8,48,1536]{2,1,0:T(8,128)(2,1)S(1)}, bf16[8,48,1536]{2,1,0:T(8,128)(2,1)S(1)}, u32[]{:S(2)}, u32[]{:S(2)}) collective-permute-start(bf16[8,48,1536]{2,1,0:T(8,128)(2,1)S(1)} %slice.468), channel_id=1, source_target_pairs={{0,1},{1,0},{2,3},{3,2},{4,5},{5,4},{6,7},{7,6},{8,9},{9,8},{10,11... | collective-permute-start | bytes 3538952 | tf_op jit(solution)/shard_map/ppermute | solution.py:121
  339.5 47.6 %collective-permute-start.36 = (bf16[8,48,1536]{2,1,0:T(8,128)(2,1)S(1)}, bf16[8,48,1536]{2,1,0:T(8,128)(2,1)S(1)}, u32[]{:S(2)}, u32[]{:S(2)}) collective-permute-start(bf16[8,48,1536]{2,1,0:T(8,128)(2,1)S(1)} %slice.470), channel_id=1, source_target_pairs={{0,1},{1,0},{2,3},{3,2},{4,5},{5,4},{6,7},{7,6},{8,9},{9,8},{10,11... | collective-permute-start | bytes 3538952 | tf_op jit(solution)/shard_map/ppermute | solution.py:121
  365.4 23.8 %collective-permute-start.32 = (bf16[4,48,1536]{2,1,0:T(8,128)(2,1)S(1)}, bf16[4,48,1536]{2,1,0:T(8,128)(2,1)S(1)}, u32[]{:S(2)}, u32[]{:S(2)}) collective-permute-start(bf16[4,48,1536]{2,1,0:T(8,128)(2,1)S(1)} %dynamic-slice_bitcast_fusion.3), channel_id=1, source_target_pairs={{0,4},{2,6},{4,0},{6,2},{8,12},{10,14},{12,8},{14,10},{16,20},{18,... | collective-permute-start | bytes 1769480 | tf_op jit(solution)/shard_map/ppermute | solution.py:117
  387.5 12.3 %collective-permute-start.37 = (bf16[4,48,1536]{2,1,0:T(8,128)(2,1)S(1)}, bf16[4,48,1536]{2,1,0:T(8,128)(2,1)S(1)}, u32[]{:S(2)}, u32[]{:S(2)}) collective-permute-start(bf16[4,48,1536]{2,1,0:T(8,128)(2,1)S(1)} %dynamic-slice_bitcast_fusion.2), channel_id=1, source_target_pairs={{0,4},{2,6},{4,0},{6,2},{8,12},{10,14},{12,8},{14,10},{16,20},{18,... | collective-permute-start | bytes 1769480 | tf_op jit(solution)/shard_map/ppermute | solution.py:117
  389.3 12.4 %collective-permute-start.33 = (bf16[2,48,1536]{2,1,0:T(8,128)(2,1)S(1)}, bf16[2,48,1536]{2,1,0:T(8,128)(2,1)S(1)}, u32[]{:S(2)}, u32[]{:S(2)}) collective-permute-start(bf16[2,48,1536]{2,1,0:T(8,128)(2,1)S(1)} %dynamic-slice_bitcast_fusion.6), channel_id=1, source_target_pairs={{0,8},{2,10},{4,12},{6,14},{8,0},{10,2},{12,4},{14,6},{16,24},{18,... | collective-permute-start | bytes 884744 | tf_op jit(solution)/shard_map/ppermute | solution.py:117
  401.8 10.6 %collective-permute-start.34 = (bf16[1,48,1536]{2,1,0:T(8,128)(2,1)S(1)}, bf16[1,48,1536]{2,1,0:T(8,128)(2,1)S(1)}, u32[]{:S(2)}, u32[]{:S(2)}) collective-permute-start(bf16[1,48,1536]{2,1,0:T(8,128)(2,1)S(1)} %constant_dynamic-slice_fusion.9), channel_id=1, source_target_pairs={{0,16},{2,18},{4,20},{6,22},{8,24},{10,26},{12,28},{14,30},{16,0},... | collective-permute-start | bytes 442376 | tf_op jit(solution)/shard_map/ppermute | solution.py:117
  (115 other events, 919.8 us)

commit v2 on v1

v2 whole, which is shorter than its diff:
```python
from functools import partial

import jax
import jax.numpy as jnp
from jax import lax
from jax.experimental import pallas as pl
from jax.experimental.pallas import tpu as pltpu
from jax.sharding import PartitionSpec as P

HEAD = 64
EPS = 1e-05
F32, LOW = jnp.float32, jnp.bfloat16
TILE = 512
SCALE2 = 0.125 * 1.4426950408889634
MASKED = -1e30


def dot(a, b, contract=((1,), (0,))):
    return lax.dot_general(a, b, (contract, ((), ())), preferred_element_type=F32)


NT = ((1,), (1,))
TN = ((0,), (0,))


def params(mib):
    return pltpu.CompilerParams(vmem_limit_bytes=mib * 1024 * 1024)


def vmem(count):
    return [pl.BlockSpec(memory_space=pltpu.VMEM)] * count


def anywhere(count):
    return [pl.BlockSpec(memory_space=pl.ANY)] * count


SMEM = pl.BlockSpec(memory_space=pltpu.SMEM)


def head_slices(width):
    heads = []
    for h in range(width // HEAD):
        first = (h // 2) * 128
        last = min(first + 128, width)
        heads.append((first, last, (h % 2) if last - first == 128 else None))
    return heads


def only(values, which):
    if which is None:
        return values
    lane = lax.broadcasted_iota(jnp.int32, values.shape, 1)
    keep = (lane < HEAD) if which == 0 else (lane >= HEAD)
    return jnp.where(keep, values, jnp.zeros_like(values))


def attend_kernel(scalars, own, peer, weight, q_ref, k_ref, v_ref, out_ref, sum_ref, *, block):
    c, split = scalars[0], scalars[1]
    half, width = own.shape[0], weight.shape[0] // 3
    total = 2 * half
    for i, rows in ((0, own), (1, peer)):
        place = pl.multiple_of((c if i == 0 else 1 - c) * half, half)
        values = rows[...]
        for j, ref in enumerate((q_ref, k_ref, v_ref)):
            ref[pl.ds(place, half), :] = dot(
                values, weight[j * width : (j + 1) * width, :], NT
            ).astype(LOW)
    bias = jnp.where(split != 0, MASKED, 0.0).astype(F32)
    diagonal = lax.broadcasted_iota(jnp.int32, (block, block), 1) <= lax.broadcasted_iota(
        jnp.int32, (block, block), 0
    )
    heads = head_slices(width)
    for i in range(total // block):
        first, last = i * block, (i + 1) * block
        outs, sums = {}, []
        for h, (lo, hi, which) in enumerate(heads):
            query = only(q_ref[first:last, lo:hi], which)
            pieces = []
            if first >= half:
                pieces.append(dot(query, k_ref[:half, lo:hi], NT) * SCALE2 + bias)
                if first > half:
                    pieces.append(dot(query, k_ref[half:first, lo:hi], NT) * SCALE2)
            elif first > 0:
                pieces.append(dot(query, k_ref[:first, lo:hi], NT) * SCALE2)
            pieces.append(
                jnp.where(diagonal, dot(query, k_ref[first:last, lo:hi], NT) * SCALE2, MASKED)
            )
            scores = jnp.concatenate(pieces, axis=1) if len(pieces) > 1 else pieces[0]
            top = jnp.max(scores, axis=1, keepdims=True)
            weights = jnp.exp2(scores - top)
            totals = jnp.sum(weights, axis=1, keepdims=True)
            result = dot(weights.astype(LOW), v_ref[:last, lo:hi]) / totals
            sums.append(top + jnp.log2(totals))
            if which == 1:
                lane = lax.broadcasted_iota(jnp.int32, result.shape, 1)
                outs[lo, hi] = jnp.where(lane < HEAD, outs[lo, hi], result)
            else:
                outs[lo, hi] = result
        for (lo, hi), result in outs.items():
            out_ref[first:last, lo:hi] = result.astype(LOW)
        lane = lax.broadcasted_iota(jnp.int32, (block, 128), 1)
        packed = jnp.zeros((block, 128), F32)
        for h, value in enumerate(sums):
            packed = jnp.where(lane == h, value, packed)
        sum_ref[:, first:last] = packed.T[:8, :]


def attend(scalars, own, peer, weight):
    half, width = own.shape[0], weight.shape[0] // 3
    packed = jax.ShapeDtypeStruct((2 * half, width), LOW)
    return pl.pallas_call(
        partial(attend_kernel, block=256),
        out_shape=(packed, packed, packed, packed, jax.ShapeDtypeStruct((8, 2 * half), F32)),
        in_specs=[SMEM] + vmem(3),
        out_specs=tuple(vmem(5)),
        compiler_params=params(40),
        cost_estimate=pl.CostEstimate(
            flops=2 * 2 * half * own.shape[1] * width * 3 * 2, bytes_accessed=6 << 20, transcendentals=0
        ),
        name="attend_forward",
    )(scalars, own, peer, weight)


def attend_back_kernel(
    scalars, own, peer, weight, q_ref, k_ref, v_ref, sum_ref, grad_own, grad_peer, *rest, block, first_set
):
    if first_set:
        (partial_ref, tq, tk, tv, grad, gq, gk, gv, dk, dv, rows) = rest
        before = None
    else:
        (before, partial_ref, tq, tk, tv, grad, gq, gk, gv, dk, dv, rows) = rest
    c, split = scalars[0], scalars[1]
    half, width = own.shape[0], weight.shape[0] // 3
    total = 2 * half
    place_own = pl.multiple_of(c * half, half)
    place_peer = pl.multiple_of((1 - c) * half, half)
    grad[pl.ds(place_own, half), :] = grad_own[...]
    grad[pl.ds(place_peer, half), :] = grad_peer[...]
    bias = jnp.where(split != 0, MASKED, 0.0).astype(F32)
    diagonal = lax.broadcasted_iota(jnp.int32, (block, block), 0) <= lax.broadcasted_iota(
        jnp.int32, (block, block), 1
    )
    dk[...] = jnp.zeros_like(dk)
    dv[...] = jnp.zeros_like(dv)
    heads = head_slices(width)
    key_turned = {}
    for h, (lo, hi, which) in enumerate(heads):
        if (lo, hi) not in key_turned:
            key_turned[lo, hi] = k_ref[:, lo:hi].T
    for i in range(total // block):
        first, last = i * block, (i + 1) * block
        query_grads = {}
        for h, (lo, hi, which) in enumerate(heads):
            query = only(q_ref[first:last, lo:hi], which)
            up = only(grad[first:last, lo:hi], which)
            log_sum = sum_ref[h : h + 1, first:last]
            pieces = []
            if first >= half:
                pieces.append(dot(k_ref[:half, lo:hi], query, NT) * SCALE2 + bias)
                if first > half:
                    pieces.append(dot(k_ref[half:first, lo:hi], query, NT) * SCALE2)
            elif first > 0:
                pieces.append(dot(k_ref[:first, lo:hi], query, NT) * SCALE2)
            pieces.append(
                jnp.where(diagonal, dot(k_ref[first:last, lo:hi], query, NT) * SCALE2, MASKED)
            )
            scores = jnp.concatenate(pieces, axis=0) if len(pieces) > 1 else pieces[0]
            shares = jnp.exp2(scores - log_sum)
            share_grads = dot(v_ref[:last, lo:hi], up, NT)
            centre = jnp.sum(shares * share_grads, axis=0, keepdims=True)
            score_grads = (shares * (share_grads - centre)).astype(LOW)
            dv[:last, lo:hi] += dot(shares.astype(LOW), up)
            dk[:last, lo:hi] += dot(score_grads, query)
            turned = dot(key_turned[lo, hi][:, :last], score_grads)
            if which == 1:
                row = lax.broadcasted_iota(jnp.int32, turned.shape, 0)
                query_grads[lo, hi] = jnp.where(row < HEAD, query_grads[lo, hi], turned)
            else:
                query_grads[lo, hi] = turned
        for (lo, hi), turned in query_grads.items():
            gq[first:last, lo:hi] = (turned.T * 0.125).astype(LOW)
    gk[...] = (dk[...] * 0.125).astype(LOW)
    gv[...] = dv[...].astype(LOW)
    rows[pl.ds(place_own, half), :] = own[...]
    rows[pl.ds(place_peer, half), :] = peer[...]
    for r in range(2):
        part = pl.ds(r * half, half)
        result = dot(gq[part, :], weight[:width, :])
        result += dot(gk[part, :], weight[width : 2 * width, :])
        result += dot(gv[part, :], weight[2 * width :, :])
        if before is not None:
            result += before[part, :].astype(F32)
        partial_ref[part, :] = result.astype(partial_ref.dtype)
    turned = rows[...].T
    for ref, g in ((tq, gq), (tk, gk), (tv, gv)):
        ref[...] = dot(turned, g[...]).astype(LOW)


def attend_back(scalars, own, peer, weight, q, k, v, sums, grad_own, grad_peer, before=None):
    half, width = own.shape[0], weight.shape[0] // 3
    model = own.shape[1]
    packed = pltpu.VMEM((2 * half, width), LOW)
    extra = [] if before is None else [before]
    return pl.pallas_call(
        partial(attend_back_kernel, block=256, first_set=before is None),
        out_shape=(jax.ShapeDtypeStruct((2 * half, model), F32),)
        + (jax.ShapeDtypeStruct((model, width), LOW),) * 3,
        in_specs=[SMEM] + vmem(9 + len(extra)),
        out_specs=tuple(vmem(4)),
        scratch_shapes=[packed, packed, packed, packed]
        + [pltpu.VMEM((2 * half, width), F32)] * 2
        + [pltpu.VMEM((2 * half, model), LOW)],
        compiler_params=params(50),
        cost_estimate=pl.CostEstimate(
            flops=2 * 2 * half * model * width * 3 * 4, bytes_accessed=12 << 20, transcendentals=0
        ),
        name="attend_backward",
    )(scalars, own, peer, weight, q, k, v, sums, grad_own, grad_peer, *extra)


def norm_stats(values, axis=1):
    mean = jnp.mean(values, axis=1, keepdims=True)
    centered = values - mean
    inverse = lax.rsqrt(jnp.mean(centered * centered, axis=1, keepdims=True) + EPS)
    return centered * inverse, inverse


def load_weight(local, parts, target, sem, scalars, tile):
    half = local.shape[1]
    quarter = parts[0].shape[0]
    part = scalars[0] * 2 + scalars[1]
    loads = []
    for j in range(2 * half // tile):
        here = []
        if j * tile < half:
            columns = pl.ds(j * tile, tile)
            here.append(
                pltpu.make_async_copy(local.at[:, columns], target.at[:, columns], sem.at[j])
            )
        else:
            for i, ref in enumerate(parts):
                rows = pl.ds(pl.multiple_of((part ^ i) * quarter, quarter), quarter)
                here.append(
                    pltpu.make_async_copy(
                        ref.at[:, pl.ds(j * tile - half, tile)],
                        target.at[rows, pl.ds(j * tile, tile)],
                        sem.at[j],
                    )
                )
        loads.append(here)
    return loads


def expand_kernel(
    scalars, rows, a0, a1, a2, a3, m0, m1, m2, m3, inner_gain, inner_bias, gain, bias, local, p0, p1, p2, p3,
    middle_ref, low_ref, i0, i1, i2, i3, inner_inverse_ref, stats_ref, act_out, slope_out,
    weight, act, slope, sem, out_sem, *, tile
):
    loads = load_weight(local, (p0, p1, p2, p3), weight, sem, scalars, tile)
    for here in loads:
        for copy in here:
            copy.start()
    width = rows.shape[1]
    pieces = [ref[...].astype(F32) for ref in (a0, a1, a2, a3)]
    sub = pieces[0].shape[1]
    mean = sum(jnp.sum(p, axis=1, keepdims=True) for p in pieces) / width
    pieces = [p - mean for p in pieces]
    inverse = lax.rsqrt(
        sum(jnp.sum(p * p, axis=1, keepdims=True) for p in pieces) / width + EPS
    )
    inner_inverse_ref[...] = jnp.broadcast_to(inverse, inner_inverse_ref.shape)
    middle = rows[...].astype(F32)
    for i, (p, m, out) in enumerate(zip(pieces, (m0, m1, m2, m3), (i0, i1, i2, i3))):
        normed = p * inverse
        out[...] = normed.astype(LOW)
        inner = (normed * inner_gain[i : i + 1, :] + inner_bias[i : i + 1, :]).astype(LOW)
        middle += dot(inner, m[...], NT)
    middle_ref[...] = middle
    normed, inverse = norm_stats(middle)
    low = (normed * gain[...] + bias[...]).astype(LOW)
    low_ref[...] = low
    count = 2 * local.shape[1] // tile
    total = 0.0
    square = 0.0
    copies = []
    for j in range(count):
        for copy in loads[j]:
            copy.wait()
        columns = slice(j * tile, (j + 1) * tile)
        value = dot(low, weight[:, columns])
        cdf = 0.5 * (1.0 + lax.erf(value * 0.7071067811865476))
        active = value * cdf
        act[j] = active.astype(LOW)
        slope[j] = (cdf + value * (jnp.exp2(value * value * -0.7213475204444817) * 0.3989422804014327)).astype(LOW)
        for source, target, k in ((act, act_out, 0), (slope, slope_out, 1)):
            copy = pltpu.make_async_copy(source.at[j], target.at[j], out_sem.at[k, j])
            copy.start()
            copies.append(copy)
        here = jnp.sum(active, axis=1, keepdims=True) / tile
        off = active - here
        spread = jnp.sum(off * off, axis=1, keepdims=True)
        if j == 0:
            total, square = here, spread
        else:
            delta = here - total
            total = total + delta / (j + 1)
            square = square + spread + delta * delta * (tile * j / (j + 1))
    inverse_hidden = lax.rsqrt(square / (tile * count) + EPS)
    lane = lax.broadcasted_iota(jnp.int32, stats_ref.shape, 1)
    stats_ref[...] = jnp.where(
        lane == 0, total, jnp.where(lane == 1, inverse_hidden, jnp.where(lane == 2, inverse, 0.0))
    )
    for copy in copies:
        copy.wait()


def expand_forward(scalars, rows, pieces, merges, inner_gain, inner_bias, gain, bias, local, parts):
    count, width = rows.shape
    sub = pieces[0].shape[1]
    hidden = 2 * local.shape[1]
    tiles = hidden // TILE
    wide = jax.ShapeDtypeStruct((tiles, count, TILE), LOW)
    piece = jax.ShapeDtypeStruct((count, sub), LOW)
    return pl.pallas_call(
        partial(expand_kernel, tile=TILE),
        out_shape=(
            jax.ShapeDtypeStruct((count, width), F32),
            jax.ShapeDtypeStruct((count, width), LOW),
            piece, piece, piece, piece,
            jax.ShapeDtypeStruct((count, 128), F32),
            jax.ShapeDtypeStruct((count, 128), F32),
            wide, wide,
        ),
        in_specs=[SMEM] + vmem(13) + anywhere(5),
        out_specs=tuple(vmem(8) + anywhere(2)),
        scratch_shapes=[
            pltpu.VMEM((width, hidden), LOW),
            pltpu.VMEM((tiles, count, TILE), LOW),
            pltpu.VMEM((tiles, count, TILE), LOW),
            pltpu.SemaphoreType.DMA((tiles,)),
            pltpu.SemaphoreType.DMA((2, tiles)),
        ],
        compiler_params=params(44),
        cost_estimate=pl.CostEstimate(
            flops=2 * count * width * (hidden + width), bytes_accessed=14 << 20, transcendentals=0
        ),
        name="expand_forward",
    )(scalars, rows, *pieces, *merges, inner_gain, inner_bias, gain, bias, local, *parts)


def contract_kernel(
    scalars, middle, cot, stats, gain, bias, local, p0, p1, p2, p3, act_in,
    output_ref, sums_ref, row_ref, up_out, grad_out,
    weight, act, up, grad, sem, act_sem, up_sem, grad_sem, *, tile
):
    loads = load_weight(local, (p0, p1, p2, p3), weight, sem, scalars, tile)
    count = 2 * local.shape[1] // tile
    for j in range(count):
        loads[j].append(pltpu.make_async_copy(act_in.at[j], act.at[j], act_sem.at[j]))
        for copy in loads[j]:
            copy.start()
    mean, inverse = stats[:, 0:1], stats[:, 1:2]
    turned = cot[...].T
    out = middle[...]
    first = second = 0.0
    copies = []
    for j in range(count):
        for copy in loads[j]:
            copy.wait()
        columns = slice(j * tile, (j + 1) * tile)
        normed = (act[j].astype(F32) - mean) * inverse
        low = (normed * gain[:, columns] + bias[:, columns]).astype(LOW)
        out += dot(low, weight[:, columns], NT)
        grad[j] = dot(turned, low).astype(LOW)
        copy = pltpu.make_async_copy(grad.at[j], grad_out.at[j], grad_sem.at[j])
        copy.start()
        copies.append(copy)
        upstream = dot(cot[...], weight[:, columns])
        crossed = upstream * normed
        sums_ref[0:1, columns] = jnp.sum(crossed, axis=0, keepdims=True)
        sums_ref[1:2, columns] = jnp.sum(upstream, axis=0, keepdims=True)
        first += jnp.sum(upstream * gain[:, columns], axis=1, keepdims=True)
        second += jnp.sum(crossed * gain[:, columns], axis=1, keepdims=True)
        up[j] = (upstream * gain[:, columns]).astype(LOW)
        copy = pltpu.make_async_copy(up.at[j], up_out.at[j], up_sem.at[j])
        copy.start()
        copies.append(copy)
    output_ref[...] = out.astype(LOW)
    lane = lax.broadcasted_iota(jnp.int32, row_ref.shape, 1)
    row_ref[...] = jnp.where(
        lane == 0, first / (tile * count), jnp.where(lane == 1, second / (tile * count), 0.0)
    )
    for copy in copies:
        copy.wait()


def contract_both(scalars, middle, cot, stats, gain, bias, local, parts, act):
    count, width = cot.shape
    hidden = 2 * local.shape[1]
    tiles = hidden // TILE
    wide = pltpu.VMEM((tiles, count, TILE), LOW)
    return pl.pallas_call(
        partial(contract_kernel, tile=TILE),
        out_shape=(
            jax.ShapeDtypeStruct((count, width), LOW),
            jax.ShapeDtypeStruct((8, hidden), F32),
            jax.ShapeDtypeStruct((count, 128), F32),
            jax.ShapeDtypeStruct((tiles, count, TILE), LOW),
            jax.ShapeDtypeStruct((tiles, width, TILE), LOW),
        ),
        in_specs=[SMEM] + vmem(5) + anywhere(6),
        out_specs=tuple(vmem(3) + anywhere(2)),
        scratch_shapes=[
            pltpu.VMEM((width, hidden), LOW), wide, wide, pltpu.VMEM((tiles, width, TILE), LOW),
            pltpu.SemaphoreType.DMA((tiles,)), pltpu.SemaphoreType.DMA((tiles,)),
            pltpu.SemaphoreType.DMA((tiles,)), pltpu.SemaphoreType.DMA((tiles,)),
        ],
        compiler_params=params(44),
        cost_estimate=pl.CostEstimate(
            flops=2 * 3 * count * width * hidden, bytes_accessed=18 << 20, transcendentals=0
        ),
        name="contract_both",
    )(scalars, middle, cot, stats, gain, bias, local, *parts, act)


def expand_back_kernel(
    scalars, middle, cot, low, stats, row_sums, inner_inverse, gain, inner_gain, inner_bias,
    i0, i1, i2, i3, m0, m1, m2, m3, local, p0, p1, p2, p3, act_in, slope_in, up_in,
    middle_grad_ref, g0, g1, g2, g3, mg0, mg1, mg2, mg3, inner_sums, model_sums, grad_out,
    weight, act, slope, up, grad, sem, act_sem, slope_sem, up_sem, grad_sem, *, tile
):
    loads = load_weight(local, (p0, p1, p2, p3), weight, sem, scalars, tile)
    count = 2 * local.shape[1] // tile
    for j in range(count):
        loads[j].append(pltpu.make_async_copy(act_in.at[j], act.at[j], act_sem.at[j]))
        loads[j].append(pltpu.make_async_copy(slope_in.at[j], slope.at[j], slope_sem.at[j]))
        loads[j].append(pltpu.make_async_copy(up_in.at[j], up.at[j], up_sem.at[j]))
        for copy in loads[j]:
            copy.start()
    mean, inverse = stats[:, 0:1], stats[:, 1:2]
    first, second = row_sums[:, 0:1], row_sums[:, 1:2]
    turned = low[...].T
    total = 0.0
    copies = []
    for j in range(count):
        for copy in loads[j]:
            copy.wait()
        columns = slice(j * tile, (j + 1) * tile)
        normed = (act[j].astype(F32) - mean) * inverse
        back = inverse * (up[j].astype(F32) - first - normed * second)
        expanded_grad = (back * slope[j].astype(F32)).astype(LOW)
        total += dot(expanded_grad, weight[:, columns], NT)
        grad[j] = dot(turned, expanded_grad).astype(LOW)
        copy = pltpu.make_async_copy(grad.at[j], grad_out.at[j], grad_sem.at[j])
        copy.start()
        copies.append(copy)
    values = middle[...]
    normed = (values - jnp.mean(values, axis=1, keepdims=True)) * stats[:, 2:3]
    model_sums[0:1, :] = jnp.sum(total * normed, axis=0, keepdims=True)
    model_sums[1:2, :] = jnp.sum(total, axis=0, keepdims=True)
    scaled = total * gain[...]
    middle_grad = cot[...].astype(F32) + stats[:, 2:3] * (
        scaled
        - jnp.mean(scaled, axis=1, keepdims=True)
        - normed * jnp.mean(scaled * normed, axis=1, keepdims=True)
    )
    middle_grad_ref[...] = middle_grad
    middle_low = middle_grad.astype(LOW)
    middle_turned = middle_low.T
    width = values.shape[1]
    inner_refs = (i0, i1, i2, i3)
    ups = []
    sums = crossed = 0.0
    for i, (inner, m, out) in enumerate(zip(inner_refs, (m0, m1, m2, m3), (mg0, mg1, mg2, mg3))):
        normed = inner[...].astype(F32)
        inner_low = (normed * inner_gain[i : i + 1, :] + inner_bias[i : i + 1, :]).astype(LOW)
        out[...] = dot(middle_turned, inner_low).astype(LOW)
        upstream = dot(middle_low, m[...])
        both = upstream * normed
        inner_sums[i : i + 1, :] = jnp.sum(both, axis=0, keepdims=True)
        inner_sums[i + 4 : i + 5, :] = jnp.sum(upstream, axis=0, keepdims=True)
        scaled = upstream * inner_gain[i : i + 1, :]
        sums += jnp.sum(scaled, axis=1, keepdims=True)
        crossed += jnp.sum(both * inner_gain[i : i + 1, :], axis=1, keepdims=True)
        ups.append(scaled)
    sums, crossed = sums / width, crossed / width
    spread = inner_inverse[:, 0:1]
    for inner, scaled, out in zip(inner_refs, ups, (g0, g1, g2, g3)):
        out[...] = (spread * (scaled - sums - inner[...].astype(F32) * crossed)).astype(LOW)
    for copy in copies:
        copy.wait()


def expand_back(
    scalars, middle, cot, low, stats, row_sums, inner_inverse, gain, inner_gain, inner_bias,
    inners, merges, local, parts, act, slope, up,
):
    count, width = cot.shape
    sub = inners[0].shape[1]
    hidden = 2 * local.shape[1]
    tiles = hidden // TILE
    wide = pltpu.VMEM((tiles, count, TILE), LOW)
    sems = pltpu.SemaphoreType.DMA((tiles,))
    return pl.pallas_call(
        partial(expand_back_kernel, tile=TILE),
        out_shape=(jax.ShapeDtypeStruct((count, width), F32),)
        + (jax.ShapeDtypeStruct((count, sub), LOW),) * 4
        + (jax.ShapeDtypeStruct((width, sub), LOW),) * 4
        + (
            jax.ShapeDtypeStruct((8, sub), F32),
            jax.ShapeDtypeStruct((8, width), F32),
            jax.ShapeDtypeStruct((tiles, width, TILE), LOW),
        ),
        in_specs=[SMEM] + vmem(17) + anywhere(8),
        out_specs=tuple(vmem(11) + anywhere(1)),
        scratch_shapes=[
            pltpu.VMEM((width, hidden), LOW), wide, wide, wide, pltpu.VMEM((tiles, width, TILE), LOW),
            sems, sems, sems, sems, sems,
        ],
        compiler_params=params(50),
        cost_estimate=pl.CostEstimate(
            flops=2 * 2 * count * width * (hidden + width), bytes_accessed=24 << 20, transcendentals=0
        ),
        name="expand_backward",
    )(
        scalars, middle, cot, low, stats, row_sums, inner_inverse, gain, inner_gain, inner_bias,
        *inners, *merges, local, *parts, act, slope, up,
    )

def cross(values, bit):
    count = lax.axis_size("dp")
    return lax.ppermute(values, "dp", [(i, i ^ bit) for i in range(count)])


def cross_x(values):
    return lax.ppermute(values, "tensor", [(0, 1), (1, 0)])


def regroup(values):
    pairs = []
    for d in range(lax.axis_size("dp")):
        for t in range(2):
            here = d * 2 + t
            pairs.append((here, here if (d & 1) == t else (d ^ 1) * 2 + (t ^ 1)))
    return lax.ppermute(values, ("dp", "tensor"), pairs)


def after(values, *others):
    return lax.optimization_barrier((values, others))[0]


def ordered(flag, first, second, axis):
    return jnp.where(
        flag == 0,
        jnp.concatenate([first, second], axis=axis),
        jnp.concatenate([second, first], axis=axis),
    )


def take(values, index, axis):
    return lax.dynamic_index_in_dim(values, index, axis=axis, keepdims=False)


def add_low(a, b):
    return (a.astype(F32) + b.astype(F32)).astype(LOW)


def halve(values, bit_value, bit, axis):
    shape = values.shape
    paired = values.reshape(shape[:axis] + (shape[axis] // 2, 2) + shape[axis + 1 :])
    return take(paired, bit_value, axis + 1), cross(take(paired, 1 - bit_value, axis + 1), bit)


def blocks(values):
    count = lax.axis_size("dp")
    shape = values.shape
    return values.reshape(shape[:-2] + (count, shape[-2] // count, shape[-1]))


def finish_reduce(values, d, first_bit):
    count = lax.axis_size("dp")
    axis = values.ndim - 3
    bit = first_bit
    while bit < count:
        keep, got = halve(values, (d // bit) % 2, bit, axis)
        bit *= 2
        values = add_low(keep, got) if bit < count else keep.astype(F32) + got.astype(F32)
    return take(values, 0, axis)


def reduce_wide(gradient, d, c):
    keep, got = halve(blocks(gradient), c, 1, gradient.ndim - 2)
    low = add_low(keep, got)
    return finish_reduce(add_low(low[0], cross_x(low[1])), d, 2)


def sum_everywhere(values):
    values = values + cross_x(values)
    bit = 1
    while bit < lax.axis_size("dp"):
        values = values + cross(values, bit)
        bit *= 2
    return values


def fetch_parts(weight, c, y):
    quarter = weight.shape[0] // 4
    got = cross_x(lax.dynamic_slice_in_dim(weight, (c * 2 + y) * quarter, quarter, axis=0))
    relayed = cross(got, 2)
    return got, relayed, cross(got, 1), cross(relayed, 1)


def body(
    block_input,
    segment_index,
    output_cotangent,
    triple_weight,
    merge_weight,
    expand_weight,
    contract_weight,
    norm_gains,
    norm_biases,
    hidden_gain,
    hidden_bias,
):
    row_count, model_width = block_input.shape
    local_width = triple_weight.shape[2]
    sub_width = local_width // 2
    hidden_local = expand_weight.shape[1]
    d = lax.axis_index("dp")
    t = lax.axis_index("tensor")
    c = d % 2
    y = (d // 2) % 2
    part = t * 2 + c

    rows_in = regroup(block_input)
    triple_local = (
        lax.dynamic_slice_in_dim(triple_weight, c * sub_width, sub_width, axis=2)
        .transpose(1, 2, 0)
        .reshape(3 * sub_width, model_width)
    )
    half = 3 * sub_width // 2
    got = cross_x(lax.dynamic_slice_in_dim(triple_local, y * half, half, axis=0))
    triple_foreign = ordered(y, got, cross(got, 2), 0)
    local_c, local_o = (
        lax.dynamic_slice_in_dim(merge_weight, i * sub_width, sub_width, axis=1) for i in (c, 1 - c)
    )
    half = model_width // 2
    got = cross_x(lax.dynamic_slice_in_dim(local_c, y * half, half, axis=0))
    foreign_c = ordered(y, got, cross(got, 2), 0)
    foreign_o = cross(foreign_c, 1)
    merges = (local_c, foreign_c, local_o, foreign_o)
    expand_parts = fetch_parts(expand_weight, c, y)
    contract_parts = fetch_parts(contract_weight, c, y)
    cotangent = regroup(output_cotangent)

    split = (segment_index[:1] != segment_index[row_count : row_count + 1]).astype(jnp.int32)
    split = jnp.where(c == t, split, cross(split, 1))
    which = jnp.stack([c, split[0]])
    place = jnp.stack([c, y])

    inputs = rows_in.astype(F32)
    first_normed, first_inverse = norm_stats(inputs)
    own = (first_normed * norm_gains[0] + norm_biases[0]).astype(LOW)
    peer = cross(own, 1)

    kept = [attend(which, own, peer, weight) for weight in (triple_local, triple_foreign)]
    mine, theirs = [], []
    for packed in kept:
        halves = packed[3].reshape(2, row_count, sub_width)
        mine.append(take(halves, c, 0))
        theirs.append(cross(take(halves, 1 - c, 0), 1))
    pieces = mine + theirs
    order = (part, part ^ 2, part ^ 1, part ^ 3)
    inner_gain = jnp.stack([take(norm_gains[1].reshape(4, sub_width), p, 0) for p in order])
    inner_bias = jnp.stack([take(norm_biases[1].reshape(4, sub_width), p, 0) for p in order])

    def wide_order(vector):
        halves = vector.reshape(2, hidden_local)
        return jnp.where(t == 0, halves, halves[::-1]).reshape(-1)

    wide_gain = wide_order(hidden_gain)[None]
    wide_bias = wide_order(hidden_bias)[None]
    middle, second_low, i0, i1, i2, i3, inner_inverse, stats, act, slope = expand_forward(
        place, rows_in, pieces, merges, inner_gain, inner_bias, norm_gains[2:], norm_biases[2:],
        expand_weight, expand_parts,
    )
    output, wide_sums, row_sums, up, contract_grad = contract_both(
        place, middle, cotangent, stats, wide_gain, wide_bias, contract_weight, contract_parts, act
    )
    layer_output = regroup(output)
    tiles = act.shape[0]

    def wide_total(gradient):
        total = reduce_wide(gradient.reshape((2, tiles // 2) + gradient.shape[1:]), d, c)
        return total.transpose(1, 0, 2).reshape(total.shape[1], hidden_local)

    contract_total = wide_total(contract_grad)
    back = expand_back(
        place, middle, cotangent, second_low, stats, row_sums, inner_inverse, norm_gains[2:],
        inner_gain, inner_bias, (i0, i1, i2, i3), merges, expand_weight, expand_parts, act, slope, up,
    )
    middle_grad, g0, g1, g2, g3, m0, m1, m2, m3, inner_sums, model_sums, expand_grad = back
    expand_total = wide_total(expand_grad)
    merge_total = reduce_wide(jnp.stack([ordered(c, m0, m2, 1), ordered(c, m1, m3, 1)]), d, c)

    sums = inner_sums.reshape(2, 4, sub_width)
    places = [(part ^ p) // 2 + (part ^ p) % 2 * 2 for p in range(4)]
    inner_total = jnp.concatenate([take(sums, i, 1) for i in places], axis=1)
    early = sum_everywhere(
        jnp.concatenate(
            [
                inner_total.reshape(-1),
                model_sums[:2].reshape(-1),
                wide_order(wide_sums[0]),
                wide_order(wide_sums[1]),
            ]
        ).reshape(-1, 128)
    ).reshape(-1)

    partial_grad = None
    triple_grads = []
    for weight, packed, mine, theirs in (
        (triple_local, kept[0], g0, cross(g2, 1)),
        (triple_foreign, kept[1], g1, cross(g3, 1)),
    ):
        q, k, v, _, sums = packed
        partial_grad, *grads = attend_back(
            which, own, peer, weight, q, k, v, sums, mine, theirs, partial_grad
        )
        triple_grads.append(jnp.stack(grads))
    keep, got = halve(blocks(jnp.stack(triple_grads)), c, 1, 2)
    low = ordered(c, keep, got, 4)
    triple_total = finish_reduce(add_low(low[0], cross_x(low[1])), d, 2).transpose(1, 0, 2)

    halves = partial_grad.reshape(2, row_count, model_width)
    first_grad = take(halves, c, 0) + cross(take(halves, 1 - c, 0).astype(LOW), 1).astype(F32)
    scaled = first_grad * norm_gains[0]
    input_gradient = regroup(
        (
            middle_grad
            + first_inverse
            * (
                scaled
                - jnp.mean(scaled, axis=1, keepdims=True)
                - first_normed * jnp.mean(scaled * first_normed, axis=1, keepdims=True)
            )
        ).astype(LOW)
    )
    late = sum_everywhere(
        jnp.stack([jnp.sum(first_grad * first_normed, axis=0), jnp.sum(first_grad, axis=0)])
    )
    norms = early[: 4 * model_width].reshape(2, 2, model_width)
    wides = early[4 * model_width :].reshape(2, 2 * hidden_local)
    return (
        layer_output,
        input_gradient,
        triple_total,
        merge_total,
        expand_total,
        contract_total,
        jnp.stack([late[0], norms[0, 0], norms[1, 0]]),
        jnp.stack([late[1], norms[0, 1], norms[1, 1]]),
        wides[0],
        wides[1],
    )


def solution(mesh):
    return jax.shard_map(
        body,
        mesh=mesh,
        in_specs=(
            P(("dp", "tensor"), None),
            P("dp"),
            P(("dp", "tensor"), None),
            P(None, None, "tensor"),
            P(None, "tensor"),
            P(None, "tensor"),
            P(None, "tensor"),
            P(),
            P(),
            P(),
            P(),
        ),
        out_specs=(
            P(("dp", "tensor"), None),
            P(("dp", "tensor"), None),
            P("dp", None, "tensor"),
            P("dp", "tensor"),
            P("dp", "tensor"),
            P("dp", "tensor"),
            P(),
            P(),
            P(),
            P(),
        ),
        check_vma=False,
    )
```

time: 425 us -> 375 us (0.88)
  matrix products: 104 us -> 0 us
  Pallas kernels: 0 us -> 82.5 us
  other arithmetic: 67.8 us -> 18 us
  waiting for transfers between devices: 124 us -> 143 us
  starting transfers between devices: 70.6 us -> 88.4 us
  local copies, waits for them, and re-layouts: 50.1 us -> 34.6 us
    dot_general x35 -> x0, matrix products: 99.4 us -> none  [the longest x1 19.6 us: body(): jnp.dot(second_low, expand_all, preferred_element_type=jnp.float32)]
    pallas_call x0 -> x7, Pallas kernels: none -> 82.5 us  [the longest x2 26.1 us: attend_back(): pl.pallas_call(partial(attend_back_kernel, block=256, first_set=before is...]
    convert_element_type x26 -> x17, other arithmetic: 27.7 us -> 7.9 us  [the longest x15 6.93 us: add_low(): return (a.astype(F32) + b.astype(F32)).astype(LOW)]
    ppermute x36 -> x40, starting transfers between devices: 43.1 us -> 62.6 us  [cross(): return lax.ppermute(values, 'dp', [(i, i ^ bit) for i in range(count)])]
    select_n x9 -> x5, other arithmetic: 15.5 us -> 3.23 us  [ordered(): jnp.where(flag == 0, jnp.concatenate([first, second], axis=axis), jnp.con...]
    ppermute x10, waiting for transfers between devices: 60.5 us -> 71.4 us  [cross_x(): return lax.ppermute(values, 'tensor', [(0, 1), (1, 0)])]
    reduce_sum x11 -> x2, other arithmetic: 8.92 us -> 0.53 us  [the longest x1 0.36 us: norm_stats(): jnp.mean(centered * centered, axis=1, keepdims=True) + EPS]
    ppermute x36 -> x40, waiting for transfers between devices: 63.7 us -> 71.4 us  [cross(): return lax.ppermute(values, 'dp', [(i, i ^ bit) for i in range(count)])]
  transfers between devices with their start and end apart: 50 -> 54, of which waited for: 20 -> 22; matrix products, arithmetic and copies ran while one was open for 35% -> 9% of each run, Pallas kernels for 0% -> 14%
where the time goes in v2:
time: 375 us; the launch traced here: 371 us
  waiting for transfers between devices  143 us (38%)
  starting transfers between devices  88.4 us (24%)
  Pallas kernels  82.5 us (22%)
  local copies, waits for them, and re-layouts  34.6 us (9%)
  other arithmetic  18 us (5%)
  between operations  4.38 us (1%)
    ppermute x10, waiting for transfers between devices, cross_x(): return lax.ppermute(values, 'tensor', [(0, 1), (1, 0)])  71.4 us
    ppermute x40, waiting for transfers between devices, cross(): return lax.ppermute(values, 'dp', [(i, i ^ bit) for i in range(count)])  71.4 us
    ppermute x40, starting transfers between devices, cross(): return lax.ppermute(values, 'dp', [(i, i ^ bit) for i in range(count)])  62.6 us
    pallas_call x2, Pallas kernels, attend_back(): pl.pallas_call(partial(attend_back_kernel, block=256, first_set=before is...  26.1 us
    pallas_call x1, Pallas kernels, expand_back(): pl.pallas_call(partial(expand_back_kernel, tile=TILE), out_shape=(jax.Sha...  17.9 us
    unnamed x118, local copies, waits for them, and re-layouts  14.4 us
    pallas_call x2, Pallas kernels, attend(): pl.pallas_call(partial(attend_kernel, block=256), out_shape=(packed, pack...  14.1 us
    ppermute x10, starting transfers between devices, cross_x(): return lax.ppermute(values, 'tensor', [(0, 1), (1, 0)])  13.3 us
  transfers between devices with their start and end apart: 54, of which 22 were waited for; matrix products, arithmetic and copies ran while one was open for 9% of the time, Pallas kernels for 14%

profile of v2, /device:TPU:0, one launch (start us, length us, event | category | flops | bytes accessed | tf_op | source)
XLA Modules:
  0.0 370.7 jit_solution(2319915443038912286)
XLA Ops:
  6.7 2.5 collective-permute-start.10
  20.8 20.4 %collective-permute-start.2 = (bf16[512,768]{1,0:T(8,128)(2,1)S(1)}, bf16[512,768]{1,0:T(8,128)(2,1)}, u32[]{:S(2)}, u32[]{:S(2)}) collective-permute-start(bf16[512,768]{1,0:T(8,128)(2,1)S(1)} %fusion.12.own), channel_id=1, source_target_pairs={{0,2},{2,0},{4,6},{6,4},{8,10},{10,8},{12,14},{14,12},{16,18},{18,... | collective-permute-start | bytes 2359304 | tf_op jit(solution)/shard_map/ppermute | solution.py:533
  44.0 12.1 %collective-permute-done.3 = bf16[288,768]{1,0:T(8,128)(2,1)} collective-permute-done((bf16[288,768]{1,0:T(8,128)(2,1)}, bf16[288,768]{1,0:T(8,128)(2,1)}, u32[]{:S(2)}, u32[]{:S(2)}) %collective-permute-start.3) | collective-permute-done | bytes 442400 | tf_op jit(solution)/shard_map/ppermute | solution.py:537
  61.1 23.6 %collective-permute-done.8 = bf16[384,192]{1,0:T(8,128)(2,1)S(1)} collective-permute-done((bf16[384,192]{1,0:T(8,128)(2,1)S(1)}, bf16[384,192]{1,0:T(8,128)(2,1)S(1)}, u32[]{:S(2)}, u32[]{:S(2)}) %collective-permute-start.8) | collective-permute-done | bytes 147488 | tf_op jit(solution)/shard_map/ppermute | solution.py:533
  84.7 2.3 collective-permute-start.14
  91.8 7.0 %attend_forward.2 = (bf16[1024,192]{1,0:T(8,128)(2,1)S(1)}, bf16[1024,192]{1,0:T(8,128)(2,1)S(1)}, bf16[1024,192]{1,0:T(8,128)(2,1)S(1)}, bf16[1024,192]{1,0:T(8,128)(2,1)S(1)}, f32[8,1024]{1,0:T(8,128)S(1)}) custom-call(s32[2]{0:T(128)S(1)} %pad_add_fusion.1.scalars, bf16[512,768]{1,0:T(8,128)(2,1)S(1)} %fusion.12.own, ...), custom_call_target="tpu_custom_call" | custom-call | flops 1811939328 | bytes 6291456 | tf_op jit(solution)/shard_map/attend_forward/pallas_call | solution.py:112
  101.9 7.0 %attend_forward.3 = (bf16[1024,192]{1,0:T(8,128)(2,1)S(1)}, bf16[1024,192]{1,0:T(8,128)(2,1)S(1)}, bf16[1024,192]{1,0:T(8,128)(2,1)S(1)}, bf16[1024,192]{1,0:T(8,128)(2,1)S(1)}, f32[8,1024]{1,0:T(8,128)S(1)}) custom-call(s32[2]{0:T(128)S(1)} %pad_add_fusion.1.scalars, bf16[512,768]{1,0:T(8,128)(2,1)S(1)} %fusion.12.own, ...), custom_call_target="tpu_custom_call" | custom-call | flops 1811939328 | bytes 6291456 | tf_op jit(solution)/shard_map/attend_forward/pallas_call | solution.py:112
  113.5 11.3 %expand_forward.1 = (f32[512,768]{1,0:T(8,128)S(1)}, bf16[512,768]{1,0:T(8,128)(2,1)S(1)}, bf16[512,192]{1,0:T(8,128)(2,1)S(1)}, bf16[512,192]{1,0:T(8,128)(2,1)...) custom-call(s32[2]{0:T(128)S(1)} %pad_add_fusion.scalars, ...), custom_call_target="tpu_custom_call" | custom-call | flops 3019898880 | bytes 14680064 | tf_op jit(solution)/shard_map/expand_forward/pallas_call | solution.py:325
  125.8 13.1 %contract_both.1 = (bf16[512,768]{1,0:T(8,128)(2,1)S(1)}, f32[8,3072]{1,0:T(8,128)S(1)}, f32[512,128]{1,0:T(8,128)S(1)}, bf16[6,512,512]{2,1,0:T(8,128)(2,1)}, bf16[6,768,512]{2,1,0:T(8,128)(2,1)}) custom-call(s32[2]{0:T(128)S(1)} %pad_add_fusion.scalars, f32[512,768]{1,0:T(8,128)S(1)} %get-tuple-element.57.middle, ...), custom_call_target="tpu_custom_call" | custom-call | flops 7247757312 | bytes 18874368 | tf_op jit(solution)/shard_map/contract_both/pallas_call | solution.py:403
  139.8 17.9 %expand_backward.1 = (f32[512,768]{1,0:T(8,128)}, bf16[512,192]{1,0:T(8,128)(2,1)S(1)}, bf16[512,192]{1,0:T(8,128)(2,1)S(1)}, bf16[512,192]{1,0:T(8,128)(2,1)S(1...) custom-call(s32[2]{0:T(128)S(1)} %pad_add_fusion.scalars, ...), custom_call_target="tpu_custom_call" | custom-call | flops 6039797760 | bytes 25165824 | tf_op jit(solution)/shard_map/expand_backward/pallas_call | solution.py:505
  161.1 7.5 %collective-permute-start.19 = (bf16[512,768]{1,0:T(8,128)(2,1)}, bf16[512,768]{1,0:T(8,128)(2,1)}, u32[]{:S(2)}, u32[]{:S(2)}) collective-permute-start(bf16[512,768]{1,0:T(8,128)(2,1)} %copy-done.8), channel_id=1, source_target_pairs={{0,0},{1,2},{2,1},{3,3},{4,4},{5,6},{6,5},{7,7},{8,8},{9,10},{10,9... | collective-permute-start | bytes 2359304 | tf_op jit(solution)/shard_map/ppermute | solution.py:546
  172.6 2.8 collective-permute-done.51
  179.4 2.6 collective-permute-start.53
  188.7 12.6 %attend_backward.2 = (f32[1024,768]{1,0:T(8,128)}, bf16[768,192]{1,0:T(8,128)(2,1)S(1)}, bf16[768,192]{1,0:T(8,128)(2,1)S(1)}, bf16[768,192]{1,0:T(8,128)(2,1)S(1)}) custom-call(s32[2]{0:T(128)S(1)} %pad_add_fusion.1.scalars, bf16[512,768]{1,0:T(8,128)(2,1)S(1)} %fusion.12.own, bf16[512,768]{1,0:T(8,128)(2,1)} %collective-permute-done.2.peer, ...), custom_call_target="tpu_custom_call" | custom-call | flops 3623878656 | bytes 12582912 | tf_op jit(solution)/shard_map/attend_backward/pallas_call | solution.py:205
  201.3 13.5 %attend_backward.3 = (f32[1024,768]{1,0:T(8,128)}, bf16[768,192]{1,0:T(8,128)(2,1)S(1)}, bf16[768,192]{1,0:T(8,128)(2,1)S(1)}, bf16[768,192]{1,0:T(8,128)(2,1)S(1)}) custom-call(s32[2]{0:T(128)S(1)} %pad_add_fusion.1.scalars, bf16[512,768]{1,0:T(8,128)(2,1)S(1)} %fusion.12.own, bf16[512,768]{1,0:T(8,128)(2,1)} %collective-permute-done.2.peer, ...), custom_call_target="tpu_custom_call" | custom-call | flops 3623878656 | bytes 12582912 | tf_op jit(solution)/shard_map/attend_backward/pallas_call | solution.py:205
  222.7 6.4 %collective-permute-done.30 = bf16[8,48,384]{2,1,0:T(8,128)(2,1)S(1)} collective-permute-done((bf16[8,48,384]{2,1,0:T(8,128)(2,1)S(1)}, bf16[8,48,384]{2,1,0:T(8,128)(2,1)S(1)}, u32[]{:S(2)}, u32[]{:S(2)}) %collective-permute-start.30) | collective-permute-done | bytes 294944 | tf_op jit(solution)/shard_map/ppermute | solution.py:537
  231.5 4.3 %collective-permute-done.46 = f32[2,768]{1,0:T(2,128)S(1)} collective-permute-done((f32[2,768]{1,0:T(2,128)S(1)}, f32[2,768]{1,0:T(2,128)S(1)}, u32[]{:S(2)}, u32[]{:S(2)}) %collective-permute-start.46) | collective-permute-done | bytes 6176 | tf_op jit(solution)/shard_map/ppermute | solution.py:533
  239.4 2.6 collective-permute-start.48
  246.4 2.6 collective-permute-start.25
  254.2 2.7 collective-permute-start.33
  256.9 19.2 %collective-permute-done.25 = bf16[3,8,48,384]{3,2,1,0:T(8,128)(2,1)S(1)} collective-permute-done((bf16[3,8,48,384]{3,2,1,0:T(8,128)(2,1)S(1)}, bf16[3,8,48,384]{3,2,1,0:T(8,128)(2,1)S(1)}, u32[]{:S(2)}, u32[]{:S(2)}) %collective-permute-start.25) | collective-permute-done | bytes 884768 | tf_op jit(solution)/shard_map/ppermute | solution.py:537
  276.8 2.9 fusion
  283.0 4.7 %collective-permute-done.26 = bf16[3,4,48,384]{3,2,1,0:T(8,128)(2,1)S(1)} collective-permute-done((bf16[3,4,48,384]{3,2,1,0:T(8,128)(2,1)S(1)}, bf16[3,4,48,384]{3,2,1,0:T(8,128)(2,1)S(1)}, u32[]{:S(2)}, u32[]{:S(2)}) %collective-permute-start.26) | collective-permute-done | bytes 442400 | tf_op jit(solution)/shard_map/ppermute | solution.py:533
  290.1 3.7 collective-permute-done.27
  293.9 2.7 collective-permute-start.28
  296.6 12.2 %collective-permute-done.40 = bf16[3,8,48,512]{3,2,1,0:T(8,128)(2,1)S(1)} collective-permute-done((bf16[3,8,48,512]{3,2,1,0:T(8,128)(2,1)S(1)}, bf16[3,8,48,512]{3,2,1,0:T(8,128)(2,1)S(1)}, u32[]{:S(2)}, u32[]{:S(2)}) %collective-permute-start.40) | collective-permute-done | bytes 1179680 | tf_op jit(solution)/shard_map/ppermute | solution.py:537
  310.7 21.5 %collective-permute-done.35 = bf16[3,8,48,512]{3,2,1,0:T(8,128)(2,1)S(1)} collective-permute-done((bf16[3,8,48,512]{3,2,1,0:T(8,128)(2,1)S(1)}, bf16[3,8,48,512]{3,2,1,0:T(8,128)(2,1)S(1)}, u32[]{:S(2)}, u32[]{:S(2)}) %collective-permute-start.35) | collective-permute-done | bytes 1179680 | tf_op jit(solution)/shard_map/ppermute | solution.py:537
  336.8 10.4 %collective-permute-done.36 = bf16[3,4,48,512]{3,2,1,0:T(8,128)(2,1)S(1)} collective-permute-done((bf16[3,4,48,512]{3,2,1,0:T(8,128)(2,1)S(1)}, bf16[3,4,48,512]{3,2,1,0:T(8,128)(2,1)S(1)}, u32[]{:S(2)}, u32[]{:S(2)}) %collective-permute-start.36) | collective-permute-done | bytes 589856 | tf_op jit(solution)/shard_map/ppermute | solution.py:533
  349.4 3.0 collective-permute-start.43
  352.4 5.6 %collective-permute-done.37 = bf16[3,2,48,512]{3,2,1,0:T(8,128)(2,1)S(1)} collective-permute-done((bf16[3,2,48,512]{3,2,1,0:T(8,128)(2,1)S(1)}, bf16[3,2,48,512]{3,2,1,0:T(8,128)(2,1)S(1)}, u32[]{:S(2)}, u32[]{:S(2)}) %collective-permute-start.37) | collective-permute-done | bytes 294944 | tf_op jit(solution)/shard_map/ppermute | solution.py:533
  358.0 2.2 collective-permute-start.38
  361.1 5.6 %collective-permute-done.38 = bf16[3,1,48,512]{3,2,1,0:T(8,128)(2,1)S(1)} collective-permute-done((bf16[3,1,48,512]{3,2,1,0:T(8,128)(2,1)S(1)}, bf16[3,1,48,512]{3,2,1,0:T(8,128)(2,1)S(1)}, u32[]{:S(2)}, u32[]{:S(2)}) %collective-permute-start.38) | collective-permute-done | bytes 147488 | tf_op jit(solution)/shard_map/ppermute | solution.py:533
  (322 shorter events, 97.7 us)
Async XLA Ops:
  3.3 39.3 %collective-permute-start.1 = (s32[1]{0:T(128)}, s32[1]{0:T(128)}, u32[]{:S(2)}, u32[]{:S(2)}) collective-permute-start(s32[1]{0:T(128)} %convert_element_type.233), channel_id=1, source_target_pairs={{0,2},{2,0},{4,6},{6,4},{8,10},{10,8},{12,14},{14,12},{16,18},{18,... | collective-permute-start | bytes 20 | tf_op jit(solution)/shard_map/ppermute | solution.py:533
  6.7 51.2 %collective-permute-start.10 = (bf16[192,1536]{1,0:T(8,128)(2,1)}, bf16[192,1536]{1,0:T(8,128)(2,1)S(1)}, u32[]{:S(2)}, u32[]{:S(2)}) collective-permute-start(bf16[192,1536]{1,0:T(8,128)(2,1)} %constant_dynamic-slice_fusion.9), channel_id=1, source_target_pairs={{0,1},{1,0},{2,3},{3,2},{4,5},{5,4},{6,7},{7,6},{8,9},{9,8},{10,11... | collective-permute-start | bytes 1769480 | tf_op jit(solution)/shard_map/ppermute | solution.py:537
  12.9 74.2 %collective-permute-start.15 = (bf16[192,1536]{1,0:T(8,128)(2,1)}, bf16[192,1536]{1,0:T(8,128)(2,1)}, u32[]{:S(2)}, u32[]{:S(2)}) collective-permute-start(bf16[192,1536]{1,0:T(8,128)(2,1)} %constant_dynamic-slice_fusion.8), channel_id=1, source_target_pairs={{0,1},{1,0},{2,3},{3,2},{4,5},{5,4},{6,7},{7,6},{8,9},{9,8},{10,11... | collective-permute-start | bytes 1769480 | tf_op jit(solution)/shard_map/ppermute | solution.py:537
  19.0 37.1 %collective-permute-start.3 = (bf16[288,768]{1,0:T(8,128)(2,1)}, bf16[288,768]{1,0:T(8,128)(2,1)}, u32[]{:S(2)}, u32[]{:S(2)}) collective-permute-start(bf16[288,768]{1,0:T(8,128)(2,1)} %constant_dynamic-slice_fusion.20), channel_id=1, source_target_pairs={{0,1},{1,0},{2,3},{3,2},{4,5},{5,4},{6,7},{7,6},{8,9},{9,8},{10,11... | collective-permute-start | bytes 1327112 | tf_op jit(solution)/shard_map/ppermute | solution.py:537
  20.8 70.5 %collective-permute-start.2 = (bf16[512,768]{1,0:T(8,128)(2,1)S(1)}, bf16[512,768]{1,0:T(8,128)(2,1)}, u32[]{:S(2)}, u32[]{:S(2)}) collective-permute-start(bf16[512,768]{1,0:T(8,128)(2,1)S(1)} %fusion.12.own), channel_id=1, source_target_pairs={{0,2},{2,0},{4,6},{6,4},{8,10},{10,8},{12,14},{14,12},{16,18},{18,... | collective-permute-start | bytes 2359304 | tf_op jit(solution)/shard_map/ppermute | solution.py:533
  42.6 15.6 %collective-permute-start.7 = (bf16[384,192]{1,0:T(8,128)(2,1)S(1)}, bf16[384,192]{1,0:T(8,128)(2,1)S(1)}, u32[]{:S(2)}, u32[]{:S(2)}) collective-permute-start(bf16[384,192]{1,0:T(8,128)(2,1)S(1)} %dynamic_slice.185), channel_id=1, source_target_pairs={{0,1},{1,0},{2,3},{3,2},{4,5},{5,4},{6,7},{7,6},{8,9},{9,8},{10,11... | collective-permute-start | bytes 442376 | tf_op jit(solution)/shard_map/ppermute | solution.py:537
  56.2 31.4 %collective-permute-start.4 = (bf16[288,768]{1,0:T(8,128)(2,1)}, bf16[288,768]{1,0:T(8,128)(2,1)}, u32[]{:S(2)}, u32[]{:S(2)}) collective-permute-start(bf16[288,768]{1,0:T(8,128)(2,1)} %collective-permute-done.3), channel_id=1, source_target_pairs={{0,4},{2,6},{4,0},{6,2},{8,12},{10,14},{12,8},{14,10},{16,20},{18,... | collective-permute-start | bytes 1327112 | tf_op jit(solution)/shard_map/ppermute | solution.py:533
  57.9 33.3 %collective-permute-start.11 = (bf16[192,1536]{1,0:T(8,128)(2,1)S(1)}, bf16[192,1536]{1,0:T(8,128)(2,1)}, u32[]{:S(2)}, u32[]{:S(2)}) collective-permute-start(bf16[192,1536]{1,0:T(8,128)(2,1)S(1)} %collective-permute-done.10.p0), channel_id=1, source_target_pairs={{0,4},{2,6},{4,0},{6,2},{8,12},{10,14},{12,8},{14,10},{16,20},{18,... | collective-permute-start | bytes 1769480 | tf_op jit(solution)/shard_map/ppermute | solution.py:533
  58.2 26.5 %collective-permute-start.8 = (bf16[384,192]{1,0:T(8,128)(2,1)S(1)}, bf16[384,192]{1,0:T(8,128)(2,1)S(1)}, u32[]{:S(2)}, u32[]{:S(2)}) collective-permute-start(bf16[384,192]{1,0:T(8,128)(2,1)S(1)} %collective-permute-done.7), channel_id=1, source_target_pairs={{0,4},{2,6},{4,0},{6,2},{8,12},{10,14},{12,8},{14,10},{16,20},{18,... | collective-permute-start | bytes 442376 | tf_op jit(solution)/shard_map/ppermute | solution.py:533
  84.7 41.1 %collective-permute-start.14 = (bf16[512,768]{1,0:T(8,128)(2,1)}, bf16[512,768]{1,0:T(8,128)(2,1)S(1)}, u32[]{:S(2)}, u32[]{:S(2)}) collective-permute-start(bf16[512,768]{1,0:T(8,128)(2,1)} %param.13), channel_id=1, source_target_pairs={{0,0},{1,2},{2,1},{3,3},{4,4},{5,6},{6,5},{7,7},{8,8},{9,10},{10,9... | collective-permute-start | bytes 2359304 | tf_op jit(solution)/shard_map/ppermute | solution.py:546
  87.1 22.7 %collective-permute-start.9 = (bf16[768,192]{1,0:T(8,128)(2,1)S(1)}, bf16[768,192]{1,0:T(8,128)(2,1)S(1)}, u32[]{:S(2)}, u32[]{:S(2)}) collective-permute-start(bf16[768,192]{1,0:T(8,128)(2,1)S(1)} %maximum_select_fusion.2.m1), channel_id=1, source_target_pairs={{0,2},{2,0},{4,6},{6,4},{8,10},{10,8},{12,14},{14,12},{16,18},{18,... | collective-permute-start | bytes 884744 | tf_op jit(solution)/shard_map/ppermute | solution.py:533
  87.5 22.5 %collective-permute-start.16 = (bf16[192,1536]{1,0:T(8,128)(2,1)}, bf16[192,1536]{1,0:T(8,128)(2,1)S(1)}, u32[]{:S(2)}, u32[]{:S(2)}) collective-permute-start(bf16[192,1536]{1,0:T(8,128)(2,1)} %collective-permute-done.15.p0), channel_id=1, source_target_pairs={{0,4},{2,6},{4,0},{6,2},{8,12},{10,14},{12,8},{14,10},{16,20},{18,... | collective-permute-start | bytes 1769480 | tf_op jit(solution)/shard_map/ppermute | solution.py:533
  91.3 19.2 %collective-permute-start.12 = (bf16[192,1536]{1,0:T(8,128)(2,1)S(1)}, bf16[192,1536]{1,0:T(8,128)(2,1)S(1)}, u32[]{:S(2)}, u32[]{:S(2)}) collective-permute-start(bf16[192,1536]{1,0:T(8,128)(2,1)S(1)} %collective-permute-done.10.p0), channel_id=1, source_target_pairs={{0,2},{2,0},{4,6},{6,4},{8,10},{10,8},{12,14},{14,12},{16,18},{18,... | collective-permute-start | bytes 1769480 | tf_op jit(solution)/shard_map/ppermute | solution.py:533
  91.3 19.3 %collective-permute-start.13 = (bf16[192,1536]{1,0:T(8,128)(2,1)}, bf16[192,1536]{1,0:T(8,128)(2,1)S(1)}, u32[]{:S(2)}, u32[]{:S(2)}) collective-permute-start(bf16[192,1536]{1,0:T(8,128)(2,1)} %collective-permute-done.11.p1), channel_id=1, source_target_pairs={{0,2},{2,0},{4,6},{6,4},{8,10},{10,8},{12,14},{14,12},{16,18},{18,... | collective-permute-start | bytes 1769480 | tf_op jit(solution)/shard_map/ppermute | solution.py:533
  109.8 15.9 %collective-permute-start.17 = (bf16[192,1536]{1,0:T(8,128)(2,1)}, bf16[192,1536]{1,0:T(8,128)(2,1)S(1)}, u32[]{:S(2)}, u32[]{:S(2)}) collective-permute-start(bf16[192,1536]{1,0:T(8,128)(2,1)} %collective-permute-done.15.p0), channel_id=1, source_target_pairs={{0,2},{2,0},{4,6},{6,4},{8,10},{10,8},{12,14},{14,12},{16,18},{18,... | collective-permute-start | bytes 1769480 | tf_op jit(solution)/shard_map/ppermute | solution.py:533
  110.0 15.8 %collective-permute-start.18 = (bf16[192,1536]{1,0:T(8,128)(2,1)S(1)}, bf16[192,1536]{1,0:T(8,128)(2,1)S(1)}, u32[]{:S(2)}, u32[]{:S(2)}) collective-permute-start(bf16[192,1536]{1,0:T(8,128)(2,1)S(1)} %collective-permute-done.16.p1), channel_id=1, source_target_pairs={{0,2},{2,0},{4,6},{6,4},{8,10},{10,8},{12,14},{14,12},{16,18},{18,... | collective-permute-start | bytes 1769480 | tf_op jit(solution)/shard_map/ppermute | solution.py:533
  160.6 40.7 %collective-permute-start.20 = (bf16[512,192]{1,0:T(8,128)(2,1)S(1)}, bf16[512,192]{1,0:T(8,128)(2,1)}, u32[]{:S(2)}, u32[]{:S(2)}) collective-permute-start(bf16[512,192]{1,0:T(8,128)(2,1)S(1)} %get-tuple-element.76), channel_id=1, source_target_pairs={{0,2},{2,0},{4,6},{6,4},{8,10},{10,8},{12,14},{14,12},{16,18},{18,... | collective-permute-start | bytes 589832 | tf_op jit(solution)/shard_map/ppermute | solution.py:533
  160.6 24.4 %collective-permute-start.21 = (bf16[512,192]{1,0:T(8,128)(2,1)S(1)}, bf16[512,192]{1,0:T(8,128)(2,1)}, u32[]{:S(2)}, u32[]{:S(2)}) collective-permute-start(bf16[512,192]{1,0:T(8,128)(2,1)S(1)} %get-tuple-element.82), channel_id=1, source_target_pairs={{0,2},{2,0},{4,6},{6,4},{8,10},{10,8},{12,14},{14,12},{16,18},{18,... | collective-permute-start | bytes 589832 | tf_op jit(solution)/shard_map/ppermute | solution.py:533
  161.1 58.5 %collective-permute-start.19 = (bf16[512,768]{1,0:T(8,128)(2,1)}, bf16[512,768]{1,0:T(8,128)(2,1)}, u32[]{:S(2)}, u32[]{:S(2)}) collective-permute-start(bf16[512,768]{1,0:T(8,128)(2,1)} %copy-done.8), channel_id=1, source_target_pairs={{0,0},{1,2},{2,1},{3,3},{4,4},{5,6},{6,5},{7,7},{8,8},{9,10},{10,9... | collective-permute-start | bytes 2359304 | tf_op jit(solution)/shard_map/ppermute | solution.py:546
  172.6 44.6 %collective-permute-start.29 = (bf16[2,8,48,384]{3,2,1,0:T(8,128)(2,1)}, bf16[2,8,48,384]{3,2,1,0:T(8,128)(2,1)}, u32[]{:S(2)}, u32[]{:S(2)}) collective-permute-start(bf16[2,8,48,384]{3,2,1,0:T(8,128)(2,1)} %fusion.26), channel_id=1, source_target_pairs={{0,2},{2,0},{4,6},{6,4},{8,10},{10,8},{12,14},{14,12},{16,18},{18,... | collective-permute-start | bytes 1769480 | tf_op jit(solution)/shard_map/ppermute | solution.py:533
  184.3 92.5 %collective-permute-start.39 = (bf16[2,3,8,48,512]{4,3,2,1,0:T(8,128)(2,1)}, bf16[2,3,8,48,512]{4,3,2,1,0:T(8,128)(2,1)}, u32[]{:S(2)}, u32[]{:S(2)}) collective-permute-start(bf16[2,3,8,48,512]{4,3,2,1,0:T(8,128)(2,1)} %dynamic-slice_bitcast_fusion), channel_id=1, source_target_pairs={{0,2},{2,0},{4,6},{6,4},{8,10},{10,8},{12,14},{14,12},{16,18},{18,... | collective-permute-start | bytes 7077896 | tf_op jit(solution)/shard_map/ppermute | solution.py:533
  184.9 94.9 %collective-permute-start.34 = (bf16[2,3,8,48,512]{4,3,2,1,0:T(8,128)(2,1)}, bf16[2,3,8,48,512]{4,3,2,1,0:T(8,128)(2,1)S(1)}, u32[]{:S(2)}, u32[]{:S(2)}) collective-permute-start(bf16[2,3,8,48,512]{4,3,2,1,0:T(8,128)(2,1)} %dynamic-slice_bitcast_fusion.1), channel_id=1, source_target_pairs={{0,2},{2,0},{4,6},{6,4},{8,10},{10,8},{12,14},{14,12},{16,18},{18,... | collective-permute-start | bytes 7077896 | tf_op jit(solution)/shard_map/ppermute | solution.py:533
  217.3 27.7 %collective-permute-start.24 = (bf16[2,3,8,48,192]{4,3,2,1,0:T(8,128)(2,1)S(1)}, bf16[2,3,8,48,192]{4,3,2,1,0:T(8,128)(2,1)S(1)}, u32[]{:S(2)}, u32[]{:S(2)}) collective-permute-start(bf16[2,3,8,48,192]{4,3,2,1,0:T(8,128)(2,1)S(1)} %get-tuple-element.112), channel_id=1, source_target_pairs={{0,2},{2,0},{4,6},{6,4},{8,10},{10,8},{12,14},{14,12},{16,18},{18,... | collective-permute-start | bytes 2654216 | tf_op jit(solution)/shard_map/ppermute | solution.py:533
  229.4 20.3 %collective-permute-start.31 = (bf16[4,48,384]{2,1,0:T(8,128)(2,1)S(1)}, bf16[4,48,384]{2,1,0:T(8,128)(2,1)S(1)}, u32[]{:S(2)}, u32[]{:S(2)}) collective-permute-start(bf16[4,48,384]{2,1,0:T(8,128)(2,1)S(1)} %dynamic-slice_bitcast_fusion.15), channel_id=1, source_target_pairs={{0,4},{2,6},{4,0},{6,2},{8,12},{10,14},{12,8},{14,10},{16,20},{18,... | collective-permute-start | bytes 442376 | tf_op jit(solution)/shard_map/ppermute | solution.py:533
  244.0 46.1 %collective-permute-start.23 = (bf16[512,768]{1,0:T(8,128)(2,1)S(1)}, bf16[512,768]{1,0:T(8,128)(2,1)S(1)}, u32[]{:S(2)}, u32[]{:S(2)}) collective-permute-start(bf16[512,768]{1,0:T(8,128)(2,1)S(1)} %fusion.17), channel_id=1, source_target_pairs={{0,0},{1,2},{2,1},{3,3},{4,4},{5,6},{6,5},{7,7},{8,8},{9,10},{10,9... | collective-permute-start | bytes 2359304 | tf_op jit(solution)/shard_map/ppermute | solution.py:546
  246.4 29.8 %collective-permute-start.25 = (bf16[3,8,48,384]{3,2,1,0:T(8,128)(2,1)S(1)}, bf16[3,8,48,384]{3,2,1,0:T(8,128)(2,1)S(1)}, u32[]{:S(2)}, u32[]{:S(2)}) collective-permute-start(bf16[3,8,48,384]{3,2,1,0:T(8,128)(2,1)S(1)} %slice_bitcast_fusion.4), channel_id=1, source_target_pairs={{0,1},{1,0},{2,3},{3,2},{4,5},{5,4},{6,7},{7,6},{8,9},{9,8},{10,11... | collective-permute-start | bytes 2654216 | tf_op jit(solution)/shard_map/ppermute | solution.py:537
  254.2 35.3 %collective-permute-start.33 = (bf16[1,48,384]{2,1,0:T(8,128)(2,1)S(1)}, bf16[1,48,384]{2,1,0:T(8,128)(2,1)S(1)}, u32[]{:S(2)}, u32[]{:S(2)}) collective-permute-start(bf16[1,48,384]{2,1,0:T(8,128)(2,1)S(1)} %constant_dynamic-slice_fusion.6), channel_id=1, source_target_pairs={{0,16},{2,18},{4,20},{6,22},{8,24},{10,26},{12,28},{14,30},{16,0},... | collective-permute-start | bytes 110600 | tf_op jit(solution)/shard_map/ppermute | solution.py:533
  279.8 29.0 %collective-permute-start.40 = (bf16[3,8,48,512]{3,2,1,0:T(8,128)(2,1)S(1)}, bf16[3,8,48,512]{3,2,1,0:T(8,128)(2,1)S(1)}, u32[]{:S(2)}, u32[]{:S(2)}) collective-permute-start(bf16[3,8,48,512]{3,2,1,0:T(8,128)(2,1)S(1)} %slice_bitcast_fusion), channel_id=1, source_target_pairs={{0,1},{1,0},{2,3},{3,2},{4,5},{5,4},{6,7},{7,6},{8,9},{9,8},{10,11... | collective-permute-start | bytes 3538952 | tf_op jit(solution)/shard_map/ppermute | solution.py:537
  280.9 51.3 %collective-permute-start.35 = (bf16[3,8,48,512]{3,2,1,0:T(8,128)(2,1)S(1)}, bf16[3,8,48,512]{3,2,1,0:T(8,128)(2,1)S(1)}, u32[]{:S(2)}, u32[]{:S(2)}) collective-permute-start(bf16[3,8,48,512]{3,2,1,0:T(8,128)(2,1)S(1)} %slice_bitcast_fusion.2), channel_id=1, source_target_pairs={{0,1},{1,0},{2,3},{3,2},{4,5},{5,4},{6,7},{7,6},{8,9},{9,8},{10,11... | collective-permute-start | bytes 3538952 | tf_op jit(solution)/shard_map/ppermute | solution.py:537
  293.9 40.3 %collective-permute-start.28 = (bf16[3,1,48,384]{3,2,1,0:T(8,128)(2,1)S(1)}, bf16[3,1,48,384]{3,2,1,0:T(8,128)(2,1)S(1)}, u32[]{:S(2)}, u32[]{:S(2)}) collective-permute-start(bf16[3,1,48,384]{3,2,1,0:T(8,128)(2,1)S(1)} %constant_dynamic-slice_fusion.7), channel_id=1, source_target_pairs={{0,16},{2,18},{4,20},{6,22},{8,24},{10,26},{12,28},{14,30},{16,0},... | collective-permute-start | bytes 331784 | tf_op jit(solution)/shard_map/ppermute | solution.py:533
  309.2 25.7 %collective-permute-start.41 = (bf16[3,4,48,512]{3,2,1,0:T(8,128)(2,1)S(1)}, bf16[3,4,48,512]{3,2,1,0:T(8,128)(2,1)S(1)}, u32[]{:S(2)}, u32[]{:S(2)}) collective-permute-start(bf16[3,4,48,512]{3,2,1,0:T(8,128)(2,1)S(1)} %dynamic-slice_bitcast_fusion.5), channel_id=1, source_target_pairs={{0,4},{2,6},{4,0},{6,2},{8,12},{10,14},{12,8},{14,10},{16,20},{18,... | collective-permute-start | bytes 1769480 | tf_op jit(solution)/shard_map/ppermute | solution.py:533
  332.6 14.6 %collective-permute-start.36 = (bf16[3,4,48,512]{3,2,1,0:T(8,128)(2,1)S(1)}, bf16[3,4,48,512]{3,2,1,0:T(8,128)(2,1)S(1)}, u32[]{:S(2)}, u32[]{:S(2)}) collective-permute-start(bf16[3,4,48,512]{3,2,1,0:T(8,128)(2,1)S(1)} %dynamic-slice_bitcast_fusion.6), channel_id=1, source_target_pairs={{0,4},{2,6},{4,0},{6,2},{8,12},{10,14},{12,8},{14,10},{16,20},{18,... | collective-permute-start | bytes 1769480 | tf_op jit(solution)/shard_map/ppermute | solution.py:533
  (77 other events, 676.2 us)

commit v3 on v2

v3 whole, which is shorter than its diff:
```python
from functools import partial

import jax
import jax.numpy as jnp
from jax import lax
from jax.experimental import pallas as pl
from jax.experimental.pallas import tpu as pltpu
from jax.sharding import PartitionSpec as P

HEAD = 64
EPS = 1e-05
F32, LOW = jnp.float32, jnp.bfloat16
TILE = 512
BLOCK = 256
SCALE2 = 0.125 * 1.4426950408889634
MASKED = -1e30


def dot(a, b, contract=((1,), (0,))):
    return lax.dot_general(a, b, (contract, ((), ())), preferred_element_type=F32)


NT = ((1,), (1,))


def params(mib=60):
    return pltpu.CompilerParams(vmem_limit_bytes=mib * 1024 * 1024)


def cost(flops, mib):
    return pl.CostEstimate(flops=flops, bytes_accessed=mib << 20, transcendentals=0)


def vmem(count):
    return [pl.BlockSpec(memory_space=pltpu.VMEM)] * count


def anywhere(count):
    return [pl.BlockSpec(memory_space=pl.ANY)] * count


SMEM = pl.BlockSpec(memory_space=pltpu.SMEM)
LowRows = partial(jax.ShapeDtypeStruct, dtype=LOW)
WideRows = partial(jax.ShapeDtypeStruct, dtype=F32)


class Copies:
    def __init__(self, sems):
        self.sems, self.count = sems, 0

    def start(self, source, target):
        copy = pltpu.make_async_copy(source, target, self.sems.at[self.count])
        self.count += 1
        copy.start()
        return copy


def wait(copies):
    for copy in copies:
        copy.wait()


def head_slices(width):
    heads = []
    for h in range(width // HEAD):
        first = (h // 2) * 128
        last = min(first + 128, width)
        heads.append((first, last, (h % 2) if last - first == 128 else None))
    return heads


def only(values, which):
    if which is None:
        return values
    lane = lax.broadcasted_iota(jnp.int32, values.shape, 1)
    keep = (lane < HEAD) if which == 0 else (lane >= HEAD)
    return jnp.where(keep, values, jnp.zeros_like(values))


def attend_kernel(scalars, own_in, peer_in, *rest, parts):
    weight_in, rest = rest[:parts], rest[parts:]
    q_out, k_out, v_out, keep_out, send_out, sum_out = rest[:6]
    rest = rest[6:]
    if parts > 1:
        weight_out, rest = rest[0], rest[1:]
    own, peer, weight, q_ref, k_ref, v_ref, out_ref, sum_ref, sems = rest
    c, split = scalars[0], scalars[1]
    copies = Copies(sems)
    rows_of = weight.shape[0] // parts
    loads = []
    for i, ref in enumerate(weight_in):
        if parts == 1:
            loads.append(copies.start(ref, weight))
        else:
            place = pl.multiple_of((scalars[2] ^ i) * rows_of, rows_of)
            loads.append(copies.start(ref, weight.at[pl.ds(place, rows_of), :]))
    load_own, load_peer = copies.start(own_in, own), copies.start(peer_in, peer)
    half, width = own.shape[0], q_ref.shape[1]
    total = 2 * half
    wait(loads)
    stores = []
    if parts > 1:
        stores.append(copies.start(weight, weight_out))
    for load, place, rows in ((load_own, c, own), (load_peer, 1 - c, peer)):
        load.wait()
        place = pl.multiple_of(place * half, half)
        values = rows[...]
        for j, ref in enumerate((q_ref, k_ref, v_ref)):
            ref[pl.ds(place, half), :] = dot(
                values, weight[j * width : (j + 1) * width, :], NT
            ).astype(LOW)
    for ref, out in ((q_ref, q_out), (k_ref, k_out), (v_ref, v_out)):
        stores.append(copies.start(ref, out))
    bias = jnp.where(split != 0, MASKED, 0.0).astype(F32)
    block = BLOCK
    diagonal = lax.broadcasted_iota(jnp.int32, (block, block), 1) <= lax.broadcasted_iota(
        jnp.int32, (block, block), 0
    )
    heads = head_slices(width)
    for i in range(total // block):
        first, last = i * block, (i + 1) * block
        outs, sums = {}, []
        for lo, hi, which in heads:
            query = only(q_ref[first:last, lo:hi], which)
            pieces = []
            if first >= half:
                pieces.append(dot(query, k_ref[:half, lo:hi], NT) * SCALE2 + bias)
                if first > half:
                    pieces.append(dot(query, k_ref[half:first, lo:hi], NT) * SCALE2)
            elif first > 0:
                pieces.append(dot(query, k_ref[:first, lo:hi], NT) * SCALE2)
            pieces.append(
                jnp.where(diagonal, dot(query, k_ref[first:last, lo:hi], NT) * SCALE2, MASKED)
            )
            scores = jnp.concatenate(pieces, axis=1) if len(pieces) > 1 else pieces[0]
            top = jnp.max(scores, axis=1, keepdims=True)
            weights = jnp.exp2(scores - top)
            totals = jnp.sum(weights, axis=1, keepdims=True)
            result = dot(weights.astype(LOW), v_ref[:last, lo:hi]) / totals
            sums.append(top + jnp.log2(totals))
            if which == 1:
                lane = lax.broadcasted_iota(jnp.int32, result.shape, 1)
                outs[lo, hi] = jnp.where(lane < HEAD, outs[lo, hi], result)
            else:
                outs[lo, hi] = result
        side = c if first < half else 1 - c
        at = first % half
        for (lo, hi), result in outs.items():
            out_ref[side, at : at + block, lo:hi] = result.astype(LOW)
        lane = lax.broadcasted_iota(jnp.int32, (block, 128), 1)
        packed = jnp.zeros((block, 128), F32)
        for h, value in enumerate(sums):
            packed = jnp.where(lane == h, value, packed)
        sum_ref[:, first:last] = packed.T[:8, :]
    stores.append(copies.start(out_ref.at[0], keep_out))
    stores.append(copies.start(out_ref.at[1], send_out))
    stores.append(copies.start(sum_ref, sum_out))
    wait(stores)


def attend(scalars, own, peer, parts):
    half, model = own.shape
    width = model // 4
    packed = LowRows((2 * half, width))
    side = LowRows((half, width))
    extra = (LowRows((model, model)),) if len(parts) > 1 else ()
    outs = (packed, packed, packed, side, side, WideRows((8, 2 * half))) + extra
    return pl.pallas_call(
        partial(attend_kernel, parts=len(parts)),
        out_shape=outs,
        in_specs=[SMEM] + anywhere(2 + len(parts)),
        out_specs=tuple(anywhere(len(outs))),
        scratch_shapes=[pltpu.VMEM((half, model), LOW)] * 2
        + [pltpu.VMEM((model, model), LOW)]
        + [pltpu.VMEM((2 * half, width), LOW)] * 3
        + [pltpu.VMEM((2, half, width), LOW), pltpu.VMEM((8, 2 * half), F32)]
        + [pltpu.SemaphoreType.DMA((20,))],
        compiler_params=params(),
        cost_estimate=cost(5_000_000_000, 6),
        name="attend_forward",
    )(scalars, own, peer, *parts)


def attend_back_kernel(
    scalars, own_in, peer_in, weight_in, q_in, k_in, v_in, sum_in, grad_own, grad_peer, *rest, last_set
):
    if last_set:
        before_in, keep_out, send_out, triple_out, *rest = rest
    else:
        partial_out, triple_out, *rest = rest
    (rows, weight, q_ref, k_ref, v_ref, sum_ref, grad, packed, dk, dv, before, send, triple, sems) = rest
    c, split = scalars[0], scalars[1]
    half = grad_own.shape[0]
    width = q_ref.shape[1]
    total = 2 * half
    copies = Copies(sems)
    place_own = pl.multiple_of(c * half, half)
    place_peer = pl.multiple_of((1 - c) * half, half)
    first_loads = [
        copies.start(q_in, q_ref),
        copies.start(k_in, k_ref),
        copies.start(v_in, v_ref),
        copies.start(sum_in, sum_ref),
        copies.start(grad_own, grad.at[pl.ds(place_own, half), :]),
        copies.start(grad_peer, grad.at[pl.ds(place_peer, half), :]),
    ]
    late_loads = [
        copies.start(own_in, rows.at[pl.ds(place_own, half), :]),
        copies.start(peer_in, rows.at[pl.ds(place_peer, half), :]),
        copies.start(weight_in, weight),
    ]
    if last_set:
        late_loads.append(copies.start(before_in, before))
    wait(first_loads)
    bias = jnp.where(split != 0, MASKED, 0.0).astype(F32)
    block = BLOCK
    diagonal = lax.broadcasted_iota(jnp.int32, (block, block), 0) <= lax.broadcasted_iota(
        jnp.int32, (block, block), 1
    )
    dk[...] = jnp.zeros_like(dk)
    dv[...] = jnp.zeros_like(dv)
    heads = head_slices(width)
    key_turned = {}
    for lo, hi, which in heads:
        if (lo, hi) not in key_turned:
            key_turned[lo, hi] = k_ref[:, lo:hi].T
    for i in range(total // block):
        first, last = i * block, (i + 1) * block
        query_grads = {}
        for h, (lo, hi, which) in enumerate(heads):
            query = only(q_ref[first:last, lo:hi], which)
            up = only(grad[first:last, lo:hi], which)
            log_sum = sum_ref[h : h + 1, first:last]
            pieces = []
            if first >= half:
                pieces.append(dot(k_ref[:half, lo:hi], query, NT) * SCALE2 + bias)
                if first > half:
                    pieces.append(dot(k_ref[half:first, lo:hi], query, NT) * SCALE2)
            elif first > 0:
                pieces.append(dot(k_ref[:first, lo:hi], query, NT) * SCALE2)
            pieces.append(
                jnp.where(diagonal, dot(k_ref[first:last, lo:hi], query, NT) * SCALE2, MASKED)
            )
            scores = jnp.concatenate(pieces, axis=0) if len(pieces) > 1 else pieces[0]
            shares = jnp.exp2(scores - log_sum)
            share_grads = dot(v_ref[:last, lo:hi], up, NT)
            centre = jnp.sum(shares * share_grads, axis=0, keepdims=True)
            score_grads = (shares * (share_grads - centre)).astype(LOW)
            dv[:last, lo:hi] += dot(shares.astype(LOW), up)
            dk[:last, lo:hi] += dot(score_grads, query)
            turned = dot(key_turned[lo, hi][:, :last], score_grads)
            if which == 1:
                row = lax.broadcasted_iota(jnp.int32, turned.shape, 0)
                query_grads[lo, hi] = jnp.where(row < HEAD, query_grads[lo, hi], turned)
            else:
                query_grads[lo, hi] = turned
        for (lo, hi), turned in query_grads.items():
            packed[first:last, lo:hi] = (turned.T * 0.125).astype(LOW)
    packed[:, width : 2 * width] = (dk[...] * 0.125).astype(LOW)
    packed[:, 2 * width :] = dv[...].astype(LOW)
    wait(late_loads)
    stores = []
    turned = rows[...].T
    triple[...] = dot(turned, packed[...]).astype(LOW)
    stores.append(copies.start(triple, triple_out))
    if last_set:
        for source, mine in ((place_own, True), (place_peer, False)):
            part = pl.ds(source, half)
            result = dot(packed[part, :], weight[: 3 * width, :]) + before[part, :]
            if mine:
                before[part, :] = result
                stores.append(copies.start(before.at[part, :], keep_out))
            else:
                send[...] = result.astype(LOW)
                stores.append(copies.start(send, send_out))
    else:
        for r in range(2):
            part = pl.ds(r * half, half)
            before[part, :] = dot(packed[part, :], weight[: 3 * width, :])
        stores.append(copies.start(before, partial_out))
    wait(stores)


def attend_back(scalars, own, peer, weight, q, k, v, sums, grad_own, grad_peer, before=None):
    half, model = own.shape
    width = model // 4
    packed = pltpu.VMEM((2 * half, width), LOW)
    triple = LowRows((model, 3 * width))
    if before is None:
        outs = (WideRows((2 * half, model)), triple)
        extra = []
    else:
        outs = (WideRows((half, model)), LowRows((half, model)), triple)
        extra = [before]
    return pl.pallas_call(
        partial(attend_back_kernel, last_set=before is not None),
        out_shape=outs,
        in_specs=[SMEM] + anywhere(9 + len(extra)),
        out_specs=tuple(anywhere(len(outs))),
        scratch_shapes=[
            pltpu.VMEM((2 * half, model), LOW),
            pltpu.VMEM((model, model), LOW),
            packed, packed, packed,
            pltpu.VMEM((8, 2 * half), F32),
            packed,
            pltpu.VMEM((2 * half, 3 * width), LOW),
            pltpu.VMEM((2 * half, width), F32),
            pltpu.VMEM((2 * half, width), F32),
            pltpu.VMEM((2 * half, model), F32),
            pltpu.VMEM((half, model), LOW),
            pltpu.VMEM((model, 3 * width), LOW),
            pltpu.SemaphoreType.DMA((16,)),
        ],
        compiler_params=params(),
        cost_estimate=cost(1000, 0),
        name="attend_backward",
    )(scalars, own, peer, weight, q, k, v, sums, grad_own, grad_peer, *extra)


def norm_stats(values):
    mean = jnp.mean(values, axis=1, keepdims=True)
    centered = values - mean
    inverse = lax.rsqrt(jnp.mean(centered * centered, axis=1, keepdims=True) + EPS)
    return centered * inverse, inverse


def load_weight(copies, local, parts, target, scalars, tile):
    half = local.shape[1]
    quarter = parts[0].shape[0]
    part = scalars[0] * 2 + scalars[1]
    loads = []
    for j in range(2 * half // tile):
        here = []
        columns = pl.ds(j * tile, tile)
        if j * tile < half:
            here.append(copies.start(local.at[:, columns], target.at[:, columns]))
        else:
            for i, ref in enumerate(parts):
                rows = pl.ds(pl.multiple_of((part ^ i) * quarter, quarter), quarter)
                here.append(
                    copies.start(ref.at[:, pl.ds(j * tile - half, tile)], target.at[rows, columns])
                )
        loads.append(here)
    return loads


def load_merge(copies, merges, target):
    sub = target.shape[1]
    loads = []
    for i, ref in enumerate(merges):
        rows = ref.shape[0]
        loads.append(copies.start(ref.at[pl.ds(rows - sub, sub), :], target.at[i]))
    return loads


def expand_kernel(
    scalars, rows_in, a0, a1, a2, a3, m0, m1, m2, m3, inner_gain, inner_bias, gain, bias, local, p0, p1, p2, p3,
    middle_out, low_out, inner_out, stats_ref, act_out, slope_out,
    rows, attended, merge, middle_ref, low_ref, inner, weight, act, slope, sems, *, tile
):
    copies = Copies(sems)
    early = [copies.start(ref, attended.at[i]) for i, ref in enumerate((a0, a1, a2, a3))]
    merge_loads = load_merge(copies, (m0, m1, m2, m3), merge)
    merge_loads.append(copies.start(rows_in, rows))
    loads = load_weight(copies, local, (p0, p1, p2, p3), weight, scalars, tile)
    width = rows.shape[1]
    wait(early)
    pieces = [attended[i].astype(F32) for i in range(4)]
    mean = sum(jnp.sum(p, axis=1, keepdims=True) for p in pieces) / width
    pieces = [p - mean for p in pieces]
    inner_inverse = lax.rsqrt(
        sum(jnp.sum(p * p, axis=1, keepdims=True) for p in pieces) / width + EPS
    )
    wait(merge_loads)
    middle = rows[...].astype(F32)
    for i, p in enumerate(pieces):
        normed = p * inner_inverse
        inner[i] = normed.astype(LOW)
        low = (normed * inner_gain[i : i + 1, :] + inner_bias[i : i + 1, :]).astype(LOW)
        middle += dot(low, merge[i])
    middle_ref[...] = middle
    normed, inverse = norm_stats(middle)
    low = (normed * gain[...] + bias[...]).astype(LOW)
    low_ref[...] = low
    stores = [
        copies.start(inner, inner_out),
        copies.start(middle_ref, middle_out),
        copies.start(low_ref, low_out),
    ]
    count = 2 * local.shape[1] // tile
    total = square = 0.0
    for j in range(count):
        wait(loads[j])
        columns = slice(j * tile, (j + 1) * tile)
        value = dot(low, weight[:, columns])
        cdf = 0.5 * (1.0 + lax.erf(value * 0.7071067811865476))
        active = value * cdf
        act[j] = active.astype(LOW)
        bell = jnp.exp2(value * value * -0.7213475204444817) * 0.3989422804014327
        slope[j] = (cdf + value * bell).astype(LOW)
        stores.append(copies.start(act.at[j], act_out.at[j]))
        stores.append(copies.start(slope.at[j], slope_out.at[j]))
        here = jnp.sum(active, axis=1, keepdims=True) / tile
        off = active - here
        spread = jnp.sum(off * off, axis=1, keepdims=True)
        if j == 0:
            total, square = here, spread
        else:
            delta = here - total
            total = total + delta / (j + 1)
            square = square + spread + delta * delta * (tile * j / (j + 1))
    hidden_inverse = lax.rsqrt(square / (tile * count) + EPS)
    lane = lax.broadcasted_iota(jnp.int32, stats_ref.shape, 1)
    stats = jnp.zeros(stats_ref.shape, F32)
    for i, value in enumerate((total, hidden_inverse, inverse, inner_inverse)):
        stats = jnp.where(lane == i, value, stats)
    stats_ref[...] = stats
    wait(stores)


def expand_forward(scalars, rows, pieces, merges, inner_gain, inner_bias, gain, bias, local, parts):
    count, width = rows.shape
    sub = pieces[0].shape[1]
    hidden = 2 * local.shape[1]
    tiles = hidden // TILE
    wide = (tiles, count, TILE)
    return pl.pallas_call(
        partial(expand_kernel, tile=TILE),
        out_shape=(
            WideRows((count, width)), LowRows((count, width)), LowRows((4, count, sub)),
            WideRows((count, 128)), LowRows(wide), LowRows(wide),
        ),
        in_specs=[SMEM] + anywhere(9) + vmem(4) + anywhere(5),
        out_specs=tuple(anywhere(3) + vmem(1) + anywhere(2)),
        scratch_shapes=[
            pltpu.VMEM((count, width), LOW),
            pltpu.VMEM((4, count, sub), LOW),
            pltpu.VMEM((4, sub, width), LOW),
            pltpu.VMEM((count, width), F32),
            pltpu.VMEM((count, width), LOW),
            pltpu.VMEM((4, count, sub), LOW),
            pltpu.VMEM((width, hidden), LOW),
            pltpu.VMEM(wide, LOW),
            pltpu.VMEM(wide, LOW),
            pltpu.SemaphoreType.DMA((48,)),
        ],
        compiler_params=params(),
        cost_estimate=cost(10_000_000_000, 14),
        name="expand_forward",
    )(scalars, rows, *pieces, *merges, inner_gain, inner_bias, gain, bias, local, *parts)


def store_split(copies, grad, place, value, outs, c):
    if len(outs) == 1:
        grad[place] = value
        return [copies.start(grad.at[place], outs[0].at[place])]
    grad[place] = value.reshape(grad.shape[1:])
    return [
        copies.start(grad.at[place, :, c], outs[0].at[place]),
        copies.start(grad.at[place, :, 1 - c], outs[1].at[place]),
    ]


def split_shapes(tiles, width, blocks):
    rows = width // blocks
    if rows % 16:
        return (tiles, width, TILE), [LowRows((tiles, width, TILE))]
    return (tiles, blocks // 2, 2, rows, TILE), [LowRows((tiles, blocks // 2, rows, TILE))] * 2


def contract_kernel(
    scalars, stats, gain, bias, middle_in, cot_in, local, p0, p1, p2, p3, act_in, *rest, tile, outs
):
    sums_ref, row_ref, output_out, up_out, *rest = rest
    grad_outs, (middle, cot, output, weight, act, up, grad, sems) = rest[:outs], rest[outs:]
    copies = Copies(sems)
    early = [copies.start(cot_in, cot), copies.start(middle_in, middle)]
    loads = load_weight(copies, local, (p0, p1, p2, p3), weight, scalars, tile)
    count = 2 * local.shape[1] // tile
    for j in range(count):
        loads[j].append(copies.start(act_in.at[j], act.at[j]))
    mean, inverse = stats[:, 0:1], stats[:, 1:2]
    wait(early)
    turned = cot[...].T
    out = middle[...]
    first = second = 0.0
    stores = []
    for j in range(count):
        wait(loads[j])
        columns = slice(j * tile, (j + 1) * tile)
        normed = (act[j].astype(F32) - mean) * inverse
        low = (normed * gain[:, columns] + bias[:, columns]).astype(LOW)
        out += dot(low, weight[:, columns], NT)
        stores += store_split(copies, grad, j, dot(turned, low).astype(LOW), grad_outs, scalars[0])
        upstream = dot(cot[...], weight[:, columns])
        crossed = upstream * normed
        sums_ref[0:1, columns] = jnp.sum(crossed, axis=0, keepdims=True)
        sums_ref[1:2, columns] = jnp.sum(upstream, axis=0, keepdims=True)
        scaled = upstream * gain[:, columns]
        first += jnp.sum(scaled, axis=1, keepdims=True)
        second += jnp.sum(scaled * normed, axis=1, keepdims=True)
        up[j] = scaled.astype(LOW)
        stores.append(copies.start(up.at[j], up_out.at[j]))
    output[...] = out.astype(LOW)
    stores.append(copies.start(output, output_out))
    lane = lax.broadcasted_iota(jnp.int32, row_ref.shape, 1)
    row_ref[...] = jnp.where(
        lane == 0, first / (tile * count), jnp.where(lane == 1, second / (tile * count), 0.0)
    )
    wait(stores)


def contract_both(scalars, stats, gain, bias, middle, cot, local, parts, act, blocks):
    count, width = cot.shape
    hidden = 2 * local.shape[1]
    tiles = hidden // TILE
    wide = (tiles, count, TILE)
    scratch, grads = split_shapes(tiles, width, blocks)
    return pl.pallas_call(
        partial(contract_kernel, tile=TILE, outs=len(grads)),
        out_shape=(WideRows((8, hidden)), WideRows((count, 128)), LowRows((count, width)), LowRows(wide), *grads),
        in_specs=[SMEM] + vmem(3) + anywhere(8),
        out_specs=tuple(vmem(2) + anywhere(2 + len(grads))),
        scratch_shapes=[
            pltpu.VMEM((count, width), F32),
            pltpu.VMEM((count, width), LOW),
            pltpu.VMEM((count, width), LOW),
            pltpu.VMEM((width, hidden), LOW),
            pltpu.VMEM(wide, LOW),
            pltpu.VMEM(wide, LOW),
            pltpu.VMEM(scratch, LOW),
            pltpu.SemaphoreType.DMA((64,)),
        ],
        compiler_params=params(),
        cost_estimate=cost(1000, 0),
        name="contract_both",
    )(scalars, stats, gain, bias, middle, cot, local, *parts, act)


def expand_back_kernel(
    scalars, stats, row_sums, gain, inner_gain, inner_bias,
    middle_in, cot_in, low_in, inner_in, m0, m1, m2, m3, local, p0, p1, p2, p3, act_in, slope_in, up_in,
    *rest, tile, outs
):
    inner_sums, model_sums, middle_out, g0, g1, g2, g3, *rest = rest
    grad_outs = rest[:outs]
    (middle, cot, low, inner, merge, inner_grad, weight, act, slope, up, grad, sems) = rest[outs:]
    copies = Copies(sems)
    early = [copies.start(low_in, low)]
    loads = load_weight(copies, local, (p0, p1, p2, p3), weight, scalars, tile)
    count = 2 * local.shape[1] // tile
    for j in range(count):
        loads[j].append(copies.start(act_in.at[j], act.at[j]))
        loads[j].append(copies.start(slope_in.at[j], slope.at[j]))
        loads[j].append(copies.start(up_in.at[j], up.at[j]))
    late = [
        copies.start(middle_in, middle),
        copies.start(cot_in, cot),
        copies.start(inner_in, inner),
    ] + load_merge(copies, (m0, m1, m2, m3), merge)
    mean, inverse = stats[:, 0:1], stats[:, 1:2]
    first, second = row_sums[:, 0:1], row_sums[:, 1:2]
    wait(early)
    turned = low[...].T
    total = 0.0
    stores = []
    for j in range(count):
        wait(loads[j])
        columns = slice(j * tile, (j + 1) * tile)
        normed = (act[j].astype(F32) - mean) * inverse
        back = inverse * (up[j].astype(F32) - first - normed * second)
        expanded_grad = (back * slope[j].astype(F32)).astype(LOW)
        total += dot(expanded_grad, weight[:, columns], NT)
        stores += store_split(
            copies, grad, j + j // (count // 2), dot(turned, expanded_grad).astype(LOW), grad_outs, scalars[0]
        )
    wait(late)
    values = middle[...]
    spread = stats[:, 2:3]
    normed = (values - jnp.mean(values, axis=1, keepdims=True)) * spread
    model_sums[0:1, :] = jnp.sum(total * normed, axis=0, keepdims=True)
    model_sums[1:2, :] = jnp.sum(total, axis=0, keepdims=True)
    scaled = total * gain[...]
    middle_grad = cot[...].astype(F32) + spread * (
        scaled
        - jnp.mean(scaled, axis=1, keepdims=True)
        - normed * jnp.mean(scaled * normed, axis=1, keepdims=True)
    )
    middle[...] = middle_grad
    stores.append(copies.start(middle, middle_out))
    middle_low = middle_grad.astype(LOW)
    width = values.shape[1]
    ups = []
    sums = crossed = 0.0
    for i in range(4):
        normed = inner[i].astype(F32)
        upstream = dot(middle_low, merge[i], NT)
        both = upstream * normed
        inner_sums[i : i + 1, :] = jnp.sum(both, axis=0, keepdims=True)
        inner_sums[i + 4 : i + 5, :] = jnp.sum(upstream, axis=0, keepdims=True)
        scaled = upstream * inner_gain[i : i + 1, :]
        sums += jnp.sum(scaled, axis=1, keepdims=True)
        crossed += jnp.sum(both * inner_gain[i : i + 1, :], axis=1, keepdims=True)
        ups.append(scaled)
    sums, crossed = sums / width, crossed / width
    spread = stats[:, 3:4]
    for i, out in enumerate((g0, g1, g2, g3)):
        inner_grad[i] = (spread * (ups[i] - sums - inner[i].astype(F32) * crossed)).astype(LOW)
        stores.append(copies.start(inner_grad.at[i], out))
    middle_turned = middle_low.T
    merge_grads = []
    for i in range(4):
        inner_low = inner[i].astype(F32) * inner_gain[i : i + 1, :] + inner_bias[i : i + 1, :]
        merge_grads.append(dot(middle_turned, inner_low.astype(LOW)))
    for i in range(2):
        value = jnp.concatenate(
            [
                jnp.where(scalars[0] == 0, merge_grads[i], merge_grads[i + 2]),
                jnp.where(scalars[0] == 0, merge_grads[i + 2], merge_grads[i]),
                jnp.zeros((width, tile - width // 2), F32),
            ],
            axis=1,
        ).astype(LOW)
        stores += store_split(copies, grad, (i + 1) * (count // 2) + i, value, grad_outs, scalars[0])
    wait(stores)


def expand_back(
    scalars, stats, row_sums, gain, inner_gain, inner_bias, middle, cot, low, inner, merges, local, parts,
    act, slope, up, blocks
):
    count, width = cot.shape
    sub = inner.shape[2]
    hidden = 2 * local.shape[1]
    tiles = hidden // TILE
    wide = pltpu.VMEM((tiles, count, TILE), LOW)
    scratch, grads = split_shapes(tiles + 2, width, blocks)
    return pl.pallas_call(
        partial(expand_back_kernel, tile=TILE, outs=len(grads)),
        out_shape=(
            WideRows((8, sub)), WideRows((8, width)), WideRows((count, width)),
            *[LowRows((count, sub))] * 4, *grads,
        ),
        in_specs=[SMEM] + vmem(5) + anywhere(16),
        out_specs=tuple(vmem(2) + anywhere(5 + len(grads))),
        scratch_shapes=[
            pltpu.VMEM((count, width), F32),
            pltpu.VMEM((count, width), LOW),
            pltpu.VMEM((count, width), LOW),
            pltpu.VMEM((4, count, sub), LOW),
            pltpu.VMEM((4, sub, width), LOW),
            pltpu.VMEM((4, count, sub), LOW),
            pltpu.VMEM((width, hidden), LOW),
            wide, wide, wide,
            pltpu.VMEM(scratch, LOW),
            pltpu.SemaphoreType.DMA((80,)),
        ],
        compiler_params=params(),
        cost_estimate=cost(1000, 0),
        name="expand_backward",
    )(
        scalars, stats, row_sums, gain, inner_gain, inner_bias, middle, cot, low, inner, *merges, local, *parts,
        act, slope, up,
    )


def cross(values, bit):
    count = lax.axis_size("dp")
    return lax.ppermute(values, "dp", [(i, i ^ bit) for i in range(count)])


def cross_x(values):
    return lax.ppermute(values, "tensor", [(0, 1), (1, 0)])


def regroup(values):
    pairs = []
    for d in range(lax.axis_size("dp")):
        for t in range(2):
            here = d * 2 + t
            pairs.append((here, here if (d & 1) == t else (d ^ 1) * 2 + (t ^ 1)))
    return lax.ppermute(values, ("dp", "tensor"), pairs)


def after(values, *others):
    return lax.optimization_barrier((values, others))[0]


def ordered(flag, first, second, axis):
    return jnp.where(
        flag == 0,
        jnp.concatenate([first, second], axis=axis),
        jnp.concatenate([second, first], axis=axis),
    )


def take(values, index, axis):
    return lax.dynamic_index_in_dim(values, index, axis=axis, keepdims=False)


def add_kernel(scalars, keep, got, keep_out, send_out):
    mine = scalars[0]
    for index, out in ((mine, keep_out), (1 - mine, send_out)):
        out[...] = (keep[:, index].astype(F32) + got[:, index].astype(F32)).astype(LOW)


def add_split(keep, got, mine):
    outer, _, count, rows, columns = keep.shape
    if rows % 16:
        total = (keep.astype(F32) + got.astype(F32)).astype(LOW)
        return take(total, mine, 1), take(total, 1 - mine, 1)
    step = max(n for n in range(1, count + 1) if count % n == 0 and n * rows <= 400)
    many = 1
    if step == count:
        many = max(n for n in range(1, outer + 1) if outer % n == 0 and n * step * rows <= 400)
    source = pl.BlockSpec((many, 2, step, rows, columns), lambda i, j: (i, 0, j, 0, 0))
    target = pl.BlockSpec((many, step, rows, columns), lambda i, j: (i, j, 0, 0))
    return pl.pallas_call(
        add_kernel,
        grid=(outer // many, count // step),
        out_shape=(LowRows((outer, count, rows, columns)),) * 2,
        in_specs=[SMEM, source, source],
        out_specs=(target, target),
        compiler_params=params(),
        cost_estimate=cost(1000, 7),
        name="add_split",
    )(mine[None].astype(jnp.int32), keep, got)


class Reduction:
    def __init__(self, d, lead, bits):
        self.d, self.lead, self.bits = d, lead, bits

    def places(self, bit):
        place = self.bits.index(bit)
        return (self.lead << place, 2, 1 << (len(self.bits) - place - 1)), (self.d // bit) % 2

    def give(self, keep, got):
        self.keep, self.got = keep, got

    def next(self, stage, *others):
        rows, columns = self.keep.shape[-2:]
        got = after(self.got, *others) if others else self.got
        if stage == "x":
            self.lead //= 2
            shape, mine = (1, 2, self.lead << len(self.bits)), jnp.zeros((), jnp.int32)
        else:
            shape, mine = self.places(stage)
            self.bits = [bit for bit in self.bits if bit != stage]
        shape = shape + (rows, columns)
        self.keep, send = add_split(self.keep.reshape(shape), got.reshape(shape), mine)
        self.got = cross_x(send) if stage == "x" else cross(send, stage)

    def result(self):
        rows, columns = self.keep.shape[-2:]
        total = self.keep.astype(F32) + self.got.astype(F32)
        return total.reshape(-1, rows, columns)


def sum_everywhere(values):
    bits = [1 << i for i in range(lax.axis_size("dp").bit_length() - 1)]
    for bit in bits[:1] + bits[3:] + bits[1:3]:
        values = values + cross(values, bit)
    return values + cross_x(values)


def body(
    block_input,
    segment_index,
    output_cotangent,
    triple_weight,
    merge_weight,
    expand_weight,
    contract_weight,
    norm_gains,
    norm_biases,
    hidden_gain,
    hidden_bias,
):
    row_count, model_width = block_input.shape
    local_width = triple_weight.shape[2]
    sub_width = local_width // 2
    hidden_local = expand_weight.shape[1]
    dp = lax.axis_size("dp")
    d = lax.axis_index("dp")
    t = lax.axis_index("tensor")
    c = d % 2
    y = (d // 2) % 2
    z = (d // 4) % 2
    part = t * 2 + c

    rows_in = regroup(block_input)
    merge_turned = merge_weight.T
    merge_c, merge_o = (
        lax.dynamic_slice_in_dim(merge_turned, i * sub_width, sub_width, axis=0) for i in (c, 1 - c)
    )
    triple_c = (
        lax.dynamic_slice_in_dim(triple_weight, c * sub_width, sub_width, axis=2)
        .transpose(1, 2, 0)
        .reshape(3 * sub_width, model_width)
    )
    heads_local = jnp.concatenate([triple_c, merge_c], axis=0)
    heads_got = cross_x(
        lax.dynamic_slice_in_dim(heads_local, (y * 2 + z) * sub_width, sub_width, axis=0)
    )
    quarter = model_width // 4

    def quarter_of(weight):
        return lax.dynamic_slice_in_dim(weight, (c * 2 + y) * quarter, quarter, axis=0)

    split = (segment_index[:1] != segment_index[row_count : row_count + 1]).astype(jnp.int32)
    split = jnp.where(c == t, split, cross(split, 1))
    which = jnp.stack([c, split[0], y * 2 + z])
    place = jnp.stack([c, y])

    inputs = rows_in.astype(F32)
    first_normed, first_inverse = norm_stats(inputs)
    own = (first_normed * norm_gains[0] + norm_biases[0]).astype(LOW)
    peer = cross(own, 1)
    expand_got = cross_x(after(quarter_of(expand_weight), own))

    heads_y = cross(heads_got, 2)
    heads_z = cross(heads_got, 4)
    own = after(own, heads_got)
    packed_local = attend(which, own, peer, (heads_local,))
    heads_y, heads_z = after((heads_y, heads_z), packed_local[5])
    heads_yz = cross(heads_y, 4)
    contract_got = cross_x(after(quarter_of(contract_weight), packed_local[5]))
    expand_got = after(expand_got, packed_local[5])
    expand_relayed = cross(expand_got, 2)
    cotangent = regroup(after(output_cotangent, expand_got))
    *packed_foreign, heads_foreign = attend(
        which, after(own, expand_got), peer, (heads_got, heads_z, heads_y, heads_yz)
    )
    theirs = [cross(packed[4], 1) for packed in (packed_local, packed_foreign)]
    merges = (
        heads_local, heads_foreign, merge_o,
        cross(lax.slice_in_dim(heads_foreign, 3 * sub_width, 4 * sub_width, axis=0), 1),
    )

    def four(got, relayed):
        return got, relayed, cross(got, 1), cross(relayed, 1)

    expand_parts = four(expand_got, after(expand_relayed, packed_foreign[5]))
    pieces = (packed_local[3], packed_foreign[3], *theirs)
    order = (part, part ^ 2, part ^ 1, part ^ 3)
    inner_gain = jnp.stack([take(norm_gains[1].reshape(4, sub_width), p, 0) for p in order])
    inner_bias = jnp.stack([take(norm_biases[1].reshape(4, sub_width), p, 0) for p in order])

    def wide_order(vector):
        halves = vector.reshape(2, hidden_local)
        return jnp.where(t == 0, halves, halves[::-1]).reshape(-1)

    wide_gain = wide_order(hidden_gain)[None]
    wide_bias = wide_order(hidden_bias)[None]

    contract_relayed = cross(after(contract_got, packed_foreign[5]), 2)
    middle, second_low, inner, stats, act, slope = expand_forward(
        place, rows_in, pieces, merges, inner_gain, inner_bias, norm_gains[2:], norm_biases[2:],
        expand_weight, expand_parts,
    )
    contract_parts = four(contract_got, after(contract_relayed, stats))
    wide_sums, row_sums, output, up, *contract_grad = contract_both(
        place, stats, wide_gain, wide_bias, middle, cotangent, contract_weight, contract_parts, act, dp
    )
    bits = [1 << i for i in reversed(range(1, dp.bit_length() - 1))]

    def first_exchange(grads):
        tiles = grads[0].shape[0]
        if len(grads) == 1:
            blocks = grads[0].reshape(tiles, dp // 2, 2, model_width // dp, TILE)
            grads = take(blocks, c, 2), take(blocks, 1 - c, 2)
        reduction = Reduction(d, tiles, bits)
        reduction.give(grads[0], cross(grads[1], 1))
        return reduction

    contract_sum = first_exchange(contract_grad)
    layer_output = regroup(output)
    back = expand_back(
        place, stats, row_sums, norm_gains[2:], inner_gain, inner_bias, middle, cotangent, second_low, inner,
        merges, expand_weight, expand_parts, act, slope, up, dp,
    )

    back, layer_output, contract_sum.got = lax.optimization_barrier(
        (back, layer_output, contract_sum.got)
    )
    inner_sums, model_sums, middle_grad, g0, g1, g2, g3, *expand_grad = back

    expand_sum = first_exchange(expand_grad)
    contract_sum.next("x")
    g3, g2 = cross(g3, 1), cross(g2, 1)
    expand_sum.next(2, contract_sum.keep)
    g1 = after(g1, expand_sum.keep)
    q, k, v, _, _, sums = packed_foreign
    partial_grad, foreign_grad = attend_back(which, own, peer, heads_foreign, q, k, v, sums, g1, g3)
    triple_got = cross_x(foreign_grad)
    contract_sum.next(4, partial_grad)
    g0 = after(g0, contract_sum.keep)
    q, k, v, _, _, sums = packed_local
    back = attend_back(which, own, peer, heads_local, q, k, v, sums, g0, g2, partial_grad)
    back, triple_got, contract_sum.got, expand_sum.got = lax.optimization_barrier(
        (back, triple_got, contract_sum.got, expand_sum.got)
    )
    keep, send, local_grad = back
    expand_sum.next(4)
    contract_sum.next(2)

    first_grad = keep + cross(send, 1).astype(F32)
    scaled = first_grad * norm_gains[0]
    input_gradient = regroup(
        (
            middle_grad
            + first_inverse
            * (
                scaled
                - jnp.mean(scaled, axis=1, keepdims=True)
                - first_normed * jnp.mean(scaled * first_normed, axis=1, keepdims=True)
            )
        ).astype(LOW)
    )
    sums = inner_sums.reshape(2, 4, sub_width)
    places = [(part ^ p) // 2 + (part ^ p) % 2 * 2 for p in range(4)]
    inner_total = jnp.concatenate([take(sums, i, 1) for i in places], axis=1)
    vectors = sum_everywhere(
        jnp.concatenate(
            [
                jnp.sum(first_grad * first_normed, axis=0),
                jnp.sum(first_grad, axis=0),
                inner_total.reshape(-1),
                model_sums[:2].reshape(-1),
                wide_order(wide_sums[0]),
                wide_order(wide_sums[1]),
            ]
        ).reshape(-1, 128)
    ).reshape(-1)

    triple_sum = Reduction(d, 1, bits + [1])
    rows = model_width // dp
    triple_sum.give(local_grad.reshape(dp, rows, -1), triple_got.reshape(dp, rows, -1))
    triple_sum.next(2)
    expand_sum.next("x")
    triple_sum.next(4)
    for bit in bits:
        for total in (contract_sum, expand_sum, triple_sum):
            if bit in total.bits:
                total.next(bit)

    def tiled(total):
        return total.transpose(1, 0, 2).reshape(total.shape[1], -1)

    both = triple_sum.result()
    mine = take(both, c, 0)
    other = cross(take(both, 1 - c, 0), 1)
    triple_total = ordered(
        c, mine.reshape(rows, 3, sub_width), other.reshape(rows, 3, sub_width), 2
    )
    expand_all = expand_sum.result()
    merge_total = expand_all[-1, :, :local_width]
    expand_total = tiled(expand_all[:-1])
    contract_total = tiled(contract_sum.result())
    norms = vectors[: 6 * model_width].reshape(3, 2, model_width)
    wides = vectors[6 * model_width :].reshape(2, 2 * hidden_local)
    return (
        layer_output,
        input_gradient,
        triple_total,
        merge_total,
        expand_total,
        contract_total,
        norms[:, 0],
        norms[:, 1],
        wides[0],
        wides[1],
    )


def solution(mesh):
    return jax.shard_map(
        body,
        mesh=mesh,
        in_specs=(
            P(("dp", "tensor"), None),
            P("dp"),
            P(("dp", "tensor"), None),
            P(None, None, "tensor"),
            P(None, "tensor"),
            P(None, "tensor"),
            P(None, "tensor"),
            P(),
            P(),
            P(),
            P(),
        ),
        out_specs=(
            P(("dp", "tensor"), None),
            P(("dp", "tensor"), None),
            P("dp", None, "tensor"),
            P("dp", "tensor"),
            P("dp", "tensor"),
            P("dp", "tensor"),
            P(),
            P(),
            P(),
            P(),
        ),
        check_vma=False,
    )
```

time: 375 us -> 296 us (0.79)
  waiting for transfers between devices: 143 us -> 53.4 us
  Pallas kernels: 82.5 us -> 125 us
  starting transfers between devices: 88.4 us -> 56.4 us
  local copies, waits for them, and re-layouts: 34.6 us -> 40.3 us
  other arithmetic: 18 us -> 13.2 us
    ppermute x10 -> x7, waiting for transfers between devices: 71.4 us -> 11.6 us  [cross_x(): return lax.ppermute(values, 'tensor', [(0, 1), (1, 0)])]
    pallas_call x7 -> x18, Pallas kernels: 82.5 us -> 125 us  [the longest x11 30.1 us: add_split(): pl.pallas_call(add_kernel, grid=(outer // many, count // step), out_shape...]
    ppermute x40 -> x33, waiting for transfers between devices: 71.4 us -> 41.8 us  [cross(): return lax.ppermute(values, 'dp', [(i, i ^ bit) for i in range(count)])]
    ppermute x40 -> x33, starting transfers between devices: 62.6 us -> 42.4 us  [cross(): return lax.ppermute(values, 'dp', [(i, i ^ bit) for i in range(count)])]
    convert_element_type x15 -> x0, other arithmetic: 6.93 us -> none  [add_low(): return (a.astype(F32) + b.astype(F32)).astype(LOW)]
    ppermute x10 -> x7, starting transfers between devices: 13.3 us -> 6.67 us  [cross_x(): return lax.ppermute(values, 'tensor', [(0, 1), (1, 0)])]
    ppermute x4, starting transfers between devices: 12.6 us -> 7.42 us  [regroup(): return lax.ppermute(values, ('dp', 'tensor'), pairs)]
    unnamed x118 -> x119, local copies, waits for them, and re-layouts: 14.4 us -> 16.1 us
  transfers between devices with their start and end apart: 54 -> 44, of which waited for: 22 -> 13; matrix products, arithmetic and copies ran while one was open for 9% -> 14% of each run, Pallas kernels for 14% -> 37%
where the time goes in v3:
time: 296 us; the launch traced here: 292 us
  Pallas kernels  125 us (42%)
  starting transfers between devices  56.4 us (19%)
  waiting for transfers between devices  53.4 us (18%)
  local copies, waits for them, and re-layouts  40.3 us (14%)
  other arithmetic  13.2 us (4%)
  between operations  4.03 us (1%)
    ppermute x33, starting transfers between devices, cross(): return lax.ppermute(values, 'dp', [(i, i ^ bit) for i in range(count)])  42.4 us
    ppermute x33, waiting for transfers between devices, cross(): return lax.ppermute(values, 'dp', [(i, i ^ bit) for i in range(count)])  41.8 us
    pallas_call x11, Pallas kernels, add_split(): pl.pallas_call(add_kernel, grid=(outer // many, count // step), out_shape...  30.1 us
    pallas_call x2, Pallas kernels, attend_back(): pl.pallas_call(partial(attend_back_kernel, last_set=before is not None),...  27.8 us
    pallas_call x2, Pallas kernels, attend(): pl.pallas_call(partial(attend_kernel, parts=len(parts)), out_shape=outs,...  19 us
    pallas_call x1, Pallas kernels, expand_back(): pl.pallas_call(partial(expand_back_kernel, tile=TILE, outs=len(grads)), o...  17.4 us
    pallas_call x1, Pallas kernels, contract_both(): pl.pallas_call(partial(contract_kernel, tile=TILE, outs=len(grads)), out_...  16.9 us
    unnamed x119, local copies, waits for them, and re-layouts  16.1 us
  transfers between devices with their start and end apart: 44, of which 13 were waited for; matrix products, arithmetic and copies ran while one was open for 14% of the time, Pallas kernels for 37%

profile of v3, /device:TPU:0, one launch (start us, length us, event | category | flops | bytes accessed | tf_op | source)
XLA Modules:
  0.0 292.0 jit_solution(1968036261054296748)
XLA Ops:
  5.9 10.9 %collective-permute-start.3 = (bf16[512,768]{1,0:T(8,128)(2,1)S(1)}, bf16[512,768]{1,0:T(8,128)(2,1)S(1)}, u32[]{:S(2)}, u32[]{:S(2)}) collective-permute-start(bf16[512,768]{1,0:T(8,128)(2,1)S(1)} %fusion.7.own_in), channel_id=1, source_target_pairs={{0,2},{2,0},{4,6},{6,4},{8,10},{10,8},{12,14},{14,12},{16,18},{18,... | collective-permute-start | bytes 2359304 | tf_op jit(solution)/shard_map/ppermute | solution.py:669
  36.1 9.4 %attend_forward.2 = (bf16[1024,192]{1,0:T(8,128)(2,1)}, bf16[1024,192]{1,0:T(8,128)(2,1)}, bf16[1024,192]{1,0:T(8,128)(2,1)}, bf16[512,192]{1,0:T(8,128)(2,1)}, ...) custom-call(s32[3]{0:T(128)} %pad_add_fusion.1.scalars, bf16[512,768]{1,0:T(8,128)(2,1)} %copy-done.4, ...), custom_call_target="tpu_custom_call" | custom-call | flops 5000000000 | bytes 6291456 | tf_op jit(solution)/shard_map/attend_forward/pallas_call | solution.py:168
  50.8 3.3 %collective-permute-done.7.rest_3_ = bf16[192,768]{1,0:T(8,128)(2,1)S(1)} collective-permute-done((bf16[192,768]{1,0:T(8,128)(2,1)S(1)}, bf16[192,768]{1,0:T(8,128)(2,1)S(1)}, u32[]{:S(2)}, u32[]{:S(2)}) %collective-permute-start.7) | collective-permute-done | bytes 294944 | tf_op jit(solution)/shard_map/ppermute | solution.py:669
  54.8 9.6 %attend_forward.3 = (bf16[1024,192]{1,0:T(8,128)(2,1)}, bf16[1024,192]{1,0:T(8,128)(2,1)}, bf16[1024,192]{1,0:T(8,128)(2,1)}, bf16[512,192]{1,0:T(8,128)(2,1)}, ...) custom-call(s32[3]{0:T(128)} %pad_add_fusion.1.scalars, bf16[512,768]{1,0:T(8,128)(2,1)} %copy-done.4, ...), custom_call_target="tpu_custom_call" | custom-call | flops 5000000000 | bytes 6291456 | tf_op jit(solution)/shard_map/attend_forward/pallas_call | solution.py:168
  74.5 13.4 %expand_forward.1 = (f32[512,768]{1,0:T(8,128)}, bf16[512,768]{1,0:T(8,128)(2,1)}, bf16[4,512,192]{2,1,0:T(8,128)(2,1)}, f32[512,128]{1,0:T(8,128)}, bf16[6,512,...) custom-call(s32[2]{0:T(128)} %pad_add_fusion.scalars, bf16[512,768]{1,0:T(8,128)(2,1)} %copy-done.2, ...), custom_call_target="tpu_custom_call" | custom-call | flops 10000000000 | bytes 14680064 | tf_op jit(solution)/shard_map/expand_forward/pallas_call | solution.py:427
  91.6 16.9 %contract_both.1 = (f32[8,3072]{1,0:T(8,128)}, f32[512,128]{1,0:T(8,128)}, bf16[512,768]{1,0:T(8,128)(2,1)}, bf16[6,512,512]{2,1,0:T(8,128)(2,1)}, bf16[6,8,48,5...) custom-call(s32[2]{0:T(128)} %pad_add_fusion.scalars, f32[512,128]{1,0:T(8,128)} %get-tuple-element.117.stats, ...), custom_call_target="tpu_custom_call" | custom-call | flops 1000 | tf_op jit(solution)/shard_map/contract_both/pallas_call | solution.py:519
  111.0 17.4 %expand_backward.1 = (f32[8,192]{1,0:T(8,128)}, f32[8,768]{1,0:T(8,128)}, f32[512,768]{1,0:T(8,128)}, bf16[512,192]{1,0:T(8,128)(2,1)}, bf16[512,192]{1,0:T(8,12...) custom-call(s32[2]{0:T(128)} %pad_add_fusion.scalars, ...), custom_call_target="tpu_custom_call" | custom-call | flops 1000 | tf_op jit(solution)/shard_map/expand_backward/pallas_call | solution.py:638
  129.9 4.7 %add_split.11 = (bf16[1,24,48,512]{3,2,1,0:T(8,128)(2,1)}, bf16[1,24,48,512]{3,2,1,0:T(8,128)(2,1)}) custom-call(s32[1]{0:T(128)} %constant.197.clone.1.scalars, bf16[1,2,24,48,512]{4,3,2,1,0:T(8,128)(2,1)} %bitcast.93, bf16[1,2,24,48,512]{4,3,2,1,0:T(8,128)(2,1)} %bitcast.94), custom_call_target="tpu_custom_call" | custom-call | flops 1000 | bytes 7340032 | tf_op jit(solution)/shard_map/add_split/pallas_call | solution.py:718
  136.5 5.0 %add_split.12 = (bf16[32,1,48,512]{3,2,1,0:T(8,128)(2,1)}, bf16[32,1,48,512]{3,2,1,0:T(8,128)(2,1)}) custom-call(s32[1]{0:T(128)} %bitcast.1.scalars, bf16[32,2,1,48,512]{4,3,2,1,0:T(8,128)(2,1)} %bitcast.90, bf16[32,2,1,48,512]{4,3,2,1,0:T(8,128)(2,1)} %bitcast.13.got), custom_call_target="tpu_custom_call" | custom-call | flops 1000 | bytes 7340032 | tf_op jit(solution)/shard_map/add_split/pallas_call | solution.py:718
  145.2 14.2 %attend_backward.2 = (f32[1024,768]{1,0:T(8,128)}, bf16[768,576]{1,0:T(8,128)(2,1)}) custom-call(s32[3]{0:T(128)} %pad_add_fusion.1.scalars, bf16[512,768]{1,0:T(8,128)(2,1)} %copy-done.4, bf16[512,768]{1,0:T(8,128)(2,1)} %copy-done.7, bf16[768,768]{1,0:T(8,128)(2,1)} %get-tuple-element.114.m1.weight_in, bf16[1024,192]{1,0:T(8,128)(2,1)} %get-tuple-element.150.q_in, ...), custom_call_target="tpu_custom_call" | custom-call | flops 1000 | tf_op jit(solution)/shard_map/attend_backward/pallas_call | solution.py:295
  159.5 2.2 copy.33
  164.6 2.5 add_split.13
  171.3 13.6 %attend_backward.3 = (f32[512,768]{1,0:T(8,128)}, bf16[512,768]{1,0:T(8,128)(2,1)}, bf16[768,576]{1,0:T(8,128)(2,1)}) custom-call(s32[3]{0:T(128)} %pad_add_fusion.1.scalars, bf16[512,768]{1,0:T(8,128)(2,1)} %copy-done.4, bf16[512,768]{1,0:T(8,128)(2,1)} %copy-done.7, bf16[768,768]{1,0:T(8,128)(2,1)} %pad_maximum_fusion.rest_0_.m0.weight_in, ...), custom_call_target="tpu_custom_call" | custom-call | flops 1000 | tf_op jit(solution)/shard_map/attend_backward/pallas_call | solution.py:295
  185.7 2.1 add_split.20
  189.2 2.2 copy.34
  191.4 2.6 add_split.14
  194.7 2.9 collective-permute-done.37
  200.1 2.6 collective-permute-start.38
  202.7 5.0 %collective-permute-done.30 = bf16[4,2,48,576]{3,2,1,0:T(8,128)(2,1)S(1)} collective-permute-done((bf16[4,2,48,576]{3,2,1,0:T(8,128)(2,1)}, bf16[4,2,48,576]{3,2,1,0:T(8,128)(2,1)S(1)}, u32[]{:S(2)}, u32[]{:S(2)}) %collective-permute-start.30) | collective-permute-done | bytes 442400 | tf_op jit(solution)/shard_map/ppermute | solution.py:669
  208.4 2.0 add_split.15
  212.9 3.2 %add_split.17 = (bf16[16,1,48,512]{3,2,1,0:T(8,128)(2,1)}, bf16[16,1,48,512]{3,2,1,0:T(8,128)(2,1)}) custom-call(s32[1]{0:T(128)} %bitcast.8.scalars, bf16[16,2,1,48,512]{4,3,2,1,0:T(8,128)(2,1)} %bitcast.95, bf16[16,2,1,48,512]{4,3,2,1,0:T(8,128)(2,1)} %bitcast.96), custom_call_target="tpu_custom_call" | custom-call | flops 1000 | bytes 7340032 | tf_op jit(solution)/shard_map/add_split/pallas_call | solution.py:718
  220.0 2.5 collective-permute-start.32
  224.2 12.5 %collective-permute-done.32 = bf16[1,2,48,576]{3,2,1,0:T(8,128)(2,1)S(1)} collective-permute-done((bf16[1,2,48,576]{3,2,1,0:T(8,128)(2,1)}, bf16[1,2,48,576]{3,2,1,0:T(8,128)(2,1)S(1)}, u32[]{:S(2)}, u32[]{:S(2)}) %collective-permute-start.32) | collective-permute-done | bytes 110624 | tf_op jit(solution)/shard_map/ppermute | solution.py:669
  240.6 2.4 add_split.18
  243.3 3.3 %collective-permute-start.40 = (f32[84,128]{1,0:T(8,128)S(1)}, f32[84,128]{1,0:T(8,128)S(1)}, u32[]{:S(2)}, u32[]{:S(2)}) collective-permute-start(f32[84,128]{1,0:T(8,128)S(1)} %bitcast_add_fusion), channel_id=1, source_target_pairs={{0,16},{2,18},{4,20},{6,22},{8,24},{10,26},{12,28},{14,30},{16,0},... | collective-permute-start | bytes 129032 | tf_op jit(solution)/shard_map/ppermute | solution.py:669
  246.6 2.0 collective-permute-done.40
  249.9 2.9 collective-permute-done.41
  252.8 3.5 %collective-permute-start.42 = (f32[84,128]{1,0:T(8,128)S(1)}, f32[84,128]{1,0:T(8,128)S(1)}, u32[]{:S(2)}, u32[]{:S(2)}) collective-permute-start(f32[84,128]{1,0:T(8,128)S(1)} %add.207), channel_id=1, source_target_pairs={{0,8},{2,10},{4,12},{6,14},{8,0},{10,2},{12,4},{14,6},{16,24},{18,... | collective-permute-start | bytes 129032 | tf_op jit(solution)/shard_map/ppermute | solution.py:669
  256.3 2.9 %fusion.12 = bf16[512,768]{1,0:T(8,128)(2,1)} fusion(f32[512,768]{1,0:T(8,128)} %get-tuple-element.141, bf16[512,768]{1,0:T(8,128)(2,1)S(1)} %copy-done.3, f32[512]{0:T(512)S(1)} %broadcast_multiply_fusion, f32[512]{0:T(512)S(1)} %broadcast_multiply_fusion.1, f32[768]{0:T(1024)S(1)} %copy-done.29, f32[512]{0:T(512)S(1)} %copy-done.35, f32[512]{0:T(512)S(1)} %copy-done.32, ...), kind=kLoop, calls=%fused_computation.14 | loop fusion | flops 4718592 | bytes 5516288 | tf_op jit(solution)/shard_map/convert_element_type | solution.py:919
  265.0 9.0 %collective-permute-done.43 = f32[84,128]{1,0:T(8,128)S(1)} collective-permute-done((f32[84,128]{1,0:T(8,128)S(1)}, f32[84,128]{1,0:T(8,128)S(1)}, u32[]{:S(2)}, u32[]{:S(2)}) %collective-permute-start.43) | collective-permute-done | bytes 43040 | tf_op jit(solution)/shard_map/ppermute | solution.py:673
  274.7 2.0 add_split.19
  278.1 9.3 %collective-permute-done.36 = bf16[4,1,48,512]{3,2,1,0:T(8,128)(2,1)S(1)} collective-permute-done((bf16[4,1,48,512]{3,2,1,0:T(8,128)(2,1)}, bf16[4,1,48,512]{3,2,1,0:T(8,128)(2,1)S(1)}, u32[]{:S(2)}, u32[]{:S(2)}) %collective-permute-start.36) | collective-permute-done | bytes 196640 | tf_op jit(solution)/shard_map/ppermute | solution.py:669
  (263 shorter events, 90.0 us)
Async XLA Ops:
  5.9 29.3 %collective-permute-start.3 = (bf16[512,768]{1,0:T(8,128)(2,1)S(1)}, bf16[512,768]{1,0:T(8,128)(2,1)S(1)}, u32[]{:S(2)}, u32[]{:S(2)}) collective-permute-start(bf16[512,768]{1,0:T(8,128)(2,1)S(1)} %fusion.7.own_in), channel_id=1, source_target_pairs={{0,2},{2,0},{4,6},{6,4},{8,10},{10,8},{12,14},{14,12},{16,18},{18,... | collective-permute-start | bytes 2359304 | tf_op jit(solution)/shard_map/ppermute | solution.py:669
  22.0 10.2 %collective-permute-start.2 = (bf16[192,768]{1,0:T(8,128)(2,1)}, bf16[192,768]{1,0:T(8,128)(2,1)}, u32[]{:S(2)}, u32[]{:S(2)}) collective-permute-start(bf16[192,768]{1,0:T(8,128)(2,1)} %fusion.15), channel_id=1, source_target_pairs={{0,1},{1,0},{2,3},{3,2},{4,5},{5,4},{6,7},{7,6},{8,9},{9,8},{10,11... | collective-permute-start | bytes 884744 | tf_op jit(solution)/shard_map/ppermute | solution.py:673
  31.1 15.8 %collective-permute-start.4 = (bf16[192,1536]{1,0:T(8,128)(2,1)}, bf16[192,1536]{1,0:T(8,128)(2,1)S(1)}, u32[]{:S(2)}, u32[]{:S(2)}) collective-permute-start(bf16[192,1536]{1,0:T(8,128)(2,1)} %constant_dynamic-slice_fusion.15), channel_id=1, source_target_pairs={{0,1},{1,0},{2,3},{3,2},{4,5},{5,4},{6,7},{7,6},{8,9},{9,8},{10,11... | collective-permute-start | bytes 1769480 | tf_op jit(solution)/shard_map/ppermute | solution.py:673
  32.1 13.4 %collective-permute-start.5 = (bf16[192,768]{1,0:T(8,128)(2,1)}, bf16[192,768]{1,0:T(8,128)(2,1)S(1)}, u32[]{:S(2)}, u32[]{:S(2)}) collective-permute-start(bf16[192,768]{1,0:T(8,128)(2,1)} %collective-permute-done.2.rest_0_), channel_id=1, source_target_pairs={{0,4},{2,6},{4,0},{6,2},{8,12},{10,14},{12,8},{14,10},{16,20},{18,... | collective-permute-start | bytes 884744 | tf_op jit(solution)/shard_map/ppermute | solution.py:669
  33.7 11.9 %collective-permute-start.6 = (bf16[192,768]{1,0:T(8,128)(2,1)}, bf16[192,768]{1,0:T(8,128)(2,1)S(1)}, u32[]{:S(2)}, u32[]{:S(2)}) collective-permute-start(bf16[192,768]{1,0:T(8,128)(2,1)} %collective-permute-done.2.rest_0_), channel_id=1, source_target_pairs={{0,8},{2,10},{4,12},{6,14},{8,0},{10,2},{12,4},{14,6},{16,24},{18,... | collective-permute-start | bytes 884744 | tf_op jit(solution)/shard_map/ppermute | solution.py:669
  45.5 8.6 %collective-permute-start.7 = (bf16[192,768]{1,0:T(8,128)(2,1)S(1)}, bf16[192,768]{1,0:T(8,128)(2,1)S(1)}, u32[]{:S(2)}, u32[]{:S(2)}) collective-permute-start(bf16[192,768]{1,0:T(8,128)(2,1)S(1)} %collective-permute-done.5.rest_2_), channel_id=1, source_target_pairs={{0,8},{2,10},{4,12},{6,14},{8,0},{10,2},{12,4},{14,6},{16,24},{18,... | collective-permute-start | bytes 884744 | tf_op jit(solution)/shard_map/ppermute | solution.py:669
  46.9 17.5 %collective-permute-start.11 = (bf16[192,1536]{1,0:T(8,128)(2,1)S(1)}, bf16[192,1536]{1,0:T(8,128)(2,1)S(1)}, u32[]{:S(2)}, u32[]{:S(2)}) collective-permute-start(bf16[192,1536]{1,0:T(8,128)(2,1)S(1)} %collective-permute-done.4.p0), channel_id=1, source_target_pairs={{0,4},{2,6},{4,0},{6,2},{8,12},{10,14},{12,8},{14,10},{16,20},{18,... | collective-permute-start | bytes 1769480 | tf_op jit(solution)/shard_map/ppermute | solution.py:669
  50.4 23.1 %collective-permute-start.12 = (bf16[192,1536]{1,0:T(8,128)(2,1)S(1)}, bf16[192,1536]{1,0:T(8,128)(2,1)S(1)}, u32[]{:S(2)}, u32[]{:S(2)}) collective-permute-start(bf16[192,1536]{1,0:T(8,128)(2,1)S(1)} %collective-permute-done.4.p0), channel_id=1, source_target_pairs={{0,2},{2,0},{4,6},{6,4},{8,10},{10,8},{12,14},{14,12},{16,18},{18,... | collective-permute-start | bytes 1769480 | tf_op jit(solution)/shard_map/ppermute | solution.py:669
  50.4 17.4 %collective-permute-start.15 = (bf16[192,1536]{1,0:T(8,128)(2,1)}, bf16[192,1536]{1,0:T(8,128)(2,1)S(1)}, u32[]{:S(2)}, u32[]{:S(2)}) collective-permute-start(bf16[192,1536]{1,0:T(8,128)(2,1)} %constant_dynamic-slice_fusion.5), channel_id=1, source_target_pairs={{0,1},{1,0},{2,3},{3,2},{4,5},{5,4},{6,7},{7,6},{8,9},{9,8},{10,11... | collective-permute-start | bytes 1769480 | tf_op jit(solution)/shard_map/ppermute | solution.py:673
  64.5 9.0 %collective-permute-start.13 = (bf16[192,1536]{1,0:T(8,128)(2,1)S(1)}, bf16[192,1536]{1,0:T(8,128)(2,1)S(1)}, u32[]{:S(2)}, u32[]{:S(2)}) collective-permute-start(bf16[192,1536]{1,0:T(8,128)(2,1)S(1)} %collective-permute-done.11.p1), channel_id=1, source_target_pairs={{0,2},{2,0},{4,6},{6,4},{8,10},{10,8},{12,14},{14,12},{16,18},{18,... | collective-permute-start | bytes 1769480 | tf_op jit(solution)/shard_map/ppermute | solution.py:669
  69.5 20.9 %collective-permute-start.14 = (bf16[512,768]{1,0:T(8,128)(2,1)}, bf16[512,768]{1,0:T(8,128)(2,1)S(1)}, u32[]{:S(2)}, u32[]{:S(2)}) collective-permute-start(bf16[512,768]{1,0:T(8,128)(2,1)} %param.13), channel_id=1, source_target_pairs={{0,0},{1,2},{2,1},{3,3},{4,4},{5,6},{6,5},{7,7},{8,8},{9,10},{10,9... | collective-permute-start | bytes 2359304 | tf_op jit(solution)/shard_map/ppermute | solution.py:682
  71.3 16.6 %collective-permute-start.16 = (bf16[192,1536]{1,0:T(8,128)(2,1)}, bf16[192,1536]{1,0:T(8,128)(2,1)}, u32[]{:S(2)}, u32[]{:S(2)}) collective-permute-start(bf16[192,1536]{1,0:T(8,128)(2,1)} %copy-done.18), channel_id=1, source_target_pairs={{0,4},{2,6},{4,0},{6,2},{8,12},{10,14},{12,8},{14,10},{16,20},{18,... | collective-permute-start | bytes 1769480 | tf_op jit(solution)/shard_map/ppermute | solution.py:669
  71.8 18.6 %collective-permute-start.17 = (bf16[192,1536]{1,0:T(8,128)(2,1)}, bf16[192,1536]{1,0:T(8,128)(2,1)}, u32[]{:S(2)}, u32[]{:S(2)}) collective-permute-start(bf16[192,1536]{1,0:T(8,128)(2,1)} %copy-done.18), channel_id=1, source_target_pairs={{0,2},{2,0},{4,6},{6,4},{8,10},{10,8},{12,14},{14,12},{16,18},{18,... | collective-permute-start | bytes 1769480 | tf_op jit(solution)/shard_map/ppermute | solution.py:669
  108.5 19.9 %collective-permute-start.20 = (bf16[6,8,48,512]{3,2,1,0:T(8,128)(2,1)}, bf16[6,8,48,512]{3,2,1,0:T(8,128)(2,1)S(1)}, u32[]{:S(2)}, u32[]{:S(2)}) collective-permute-start(bf16[6,8,48,512]{3,2,1,0:T(8,128)(2,1)} %get-tuple-element.139), channel_id=1, source_target_pairs={{0,2},{2,0},{4,6},{6,4},{8,10},{10,8},{12,14},{14,12},{16,18},{18,... | collective-permute-start | bytes 7077896 | tf_op jit(solution)/shard_map/ppermute | solution.py:669
  109.0 19.4 %collective-permute-start.19 = (bf16[512,768]{1,0:T(8,128)(2,1)}, bf16[512,768]{1,0:T(8,128)(2,1)S(1)}, u32[]{:S(2)}, u32[]{:S(2)}) collective-permute-start(bf16[512,768]{1,0:T(8,128)(2,1)} %get-tuple-element.138), channel_id=1, source_target_pairs={{0,0},{1,2},{2,1},{3,3},{4,4},{5,6},{6,5},{7,7},{8,8},{9,10},{10,9... | collective-permute-start | bytes 2359304 | tf_op jit(solution)/shard_map/ppermute | solution.py:682
  128.4 8.0 %collective-permute-start.22 = (bf16[8,8,48,512]{3,2,1,0:T(8,128)(2,1)}, bf16[8,8,48,512]{3,2,1,0:T(8,128)(2,1)}, u32[]{:S(2)}, u32[]{:S(2)}) collective-permute-start(bf16[8,8,48,512]{3,2,1,0:T(8,128)(2,1)} %get-tuple-element.155), channel_id=1, source_target_pairs={{0,2},{2,0},{4,6},{6,4},{8,10},{10,8},{12,14},{14,12},{16,18},{18,... | collective-permute-start | bytes 9437192 | tf_op jit(solution)/shard_map/ppermute | solution.py:669
  134.6 29.0 %collective-permute-start.21 = (bf16[1,24,48,512]{3,2,1,0:T(8,128)(2,1)}, bf16[1,24,48,512]{3,2,1,0:T(8,128)(2,1)S(1)}, u32[]{:S(2)}, u32[]{:S(2)}) collective-permute-start(bf16[1,24,48,512]{3,2,1,0:T(8,128)(2,1)} %get-tuple-element.149), channel_id=1, source_target_pairs={{0,1},{1,0},{2,3},{3,2},{4,5},{5,4},{6,7},{7,6},{8,9},{9,8},{10,11... | collective-permute-start | bytes 3538952 | tf_op jit(solution)/shard_map/ppermute | solution.py:673
  141.5 43.5 %collective-permute-start.27 = (bf16[32,1,48,512]{3,2,1,0:T(8,128)(2,1)}, bf16[32,1,48,512]{3,2,1,0:T(8,128)(2,1)S(1)}, u32[]{:S(2)}, u32[]{:S(2)}) collective-permute-start(bf16[32,1,48,512]{3,2,1,0:T(8,128)(2,1)} %get-tuple-element.170), channel_id=1, source_target_pairs={{0,4},{2,6},{4,0},{6,2},{8,12},{10,14},{12,8},{14,10},{16,20},{18,... | collective-permute-start | bytes 4718600 | tf_op jit(solution)/shard_map/ppermute | solution.py:669
  161.7 23.2 %collective-permute-start.25 = (bf16[768,576]{0,1:T(8,128)(2,1)}, bf16[768,576]{0,1:T(8,128)(2,1)}, u32[]{:S(2)}, u32[]{:S(2)}) collective-permute-start(bf16[768,576]{0,1:T(8,128)(2,1)} %copy.33), channel_id=1, source_target_pairs={{0,1},{1,0},{2,3},{3,2},{4,5},{5,4},{6,7},{7,6},{8,9},{9,8},{10,11... | collective-permute-start | bytes 2654216 | tf_op jit(solution)/shard_map/ppermute | solution.py:673
  167.2 17.8 %collective-permute-start.26 = (bf16[6,2,48,512]{3,2,1,0:T(8,128)(2,1)}, bf16[6,2,48,512]{3,2,1,0:T(8,128)(2,1)S(1)}, u32[]{:S(2)}, u32[]{:S(2)}) collective-permute-start(bf16[6,2,48,512]{3,2,1,0:T(8,128)(2,1)} %get-tuple-element.169), channel_id=1, source_target_pairs={{0,8},{2,10},{4,12},{6,14},{8,0},{10,2},{12,4},{14,6},{16,24},{18,... | collective-permute-start | bytes 1769480 | tf_op jit(solution)/shard_map/ppermute | solution.py:669
  185.0 52.7 %collective-permute-start.28 = (bf16[512,768]{1,0:T(8,128)(2,1)}, bf16[512,768]{1,0:T(8,128)(2,1)S(1)}, u32[]{:S(2)}, u32[]{:S(2)}) collective-permute-start(bf16[512,768]{1,0:T(8,128)(2,1)} %get-tuple-element.172), channel_id=1, source_target_pairs={{0,2},{2,0},{4,6},{6,4},{8,10},{10,8},{12,14},{14,12},{16,18},{18,... | collective-permute-start | bytes 2359304 | tf_op jit(solution)/shard_map/ppermute | solution.py:669
  187.9 9.7 %collective-permute-start.37 = (bf16[6,1,48,512]{3,2,1,0:T(8,128)(2,1)}, bf16[6,1,48,512]{3,2,1,0:T(8,128)(2,1)S(1)}, u32[]{:S(2)}, u32[]{:S(2)}) collective-permute-start(bf16[6,1,48,512]{3,2,1,0:T(8,128)(2,1)} %get-tuple-element.190), channel_id=1, source_target_pairs={{0,4},{2,6},{4,0},{6,2},{8,12},{10,14},{12,8},{14,10},{16,20},{18,... | collective-permute-start | bytes 884744 | tf_op jit(solution)/shard_map/ppermute | solution.py:669
  194.0 13.7 %collective-permute-start.30 = (bf16[4,2,48,576]{3,2,1,0:T(8,128)(2,1)}, bf16[4,2,48,576]{3,2,1,0:T(8,128)(2,1)S(1)}, u32[]{:S(2)}, u32[]{:S(2)}) collective-permute-start(bf16[4,2,48,576]{3,2,1,0:T(8,128)(2,1)} %get-tuple-element.176), channel_id=1, source_target_pairs={{0,4},{2,6},{4,0},{6,2},{8,12},{10,14},{12,8},{14,10},{16,20},{18,... | collective-permute-start | bytes 1327112 | tf_op jit(solution)/shard_map/ppermute | solution.py:669
  200.1 22.4 %collective-permute-start.38 = (bf16[3,1,48,512]{3,2,1,0:T(8,128)(2,1)}, bf16[3,1,48,512]{3,2,1,0:T(8,128)(2,1)}, u32[]{:S(2)}, u32[]{:S(2)}) collective-permute-start(bf16[3,1,48,512]{3,2,1,0:T(8,128)(2,1)} %get-tuple-element.192), channel_id=1, source_target_pairs={{0,16},{2,18},{4,20},{6,22},{8,24},{10,26},{12,28},{14,30},{16,0},... | collective-permute-start | bytes 442376 | tf_op jit(solution)/shard_map/ppermute | solution.py:669
  216.2 24.4 %collective-permute-start.34 = (bf16[16,1,48,512]{3,2,1,0:T(8,128)(2,1)}, bf16[16,1,48,512]{3,2,1,0:T(8,128)(2,1)}, u32[]{:S(2)}, u32[]{:S(2)}) collective-permute-start(bf16[16,1,48,512]{3,2,1,0:T(8,128)(2,1)} %get-tuple-element.183), channel_id=1, source_target_pairs={{0,8},{2,10},{4,12},{6,14},{8,0},{10,2},{12,4},{14,6},{16,24},{18,... | collective-permute-start | bytes 2359304 | tf_op jit(solution)/shard_map/ppermute | solution.py:669
  220.0 16.7 %collective-permute-start.32 = (bf16[1,2,48,576]{3,2,1,0:T(8,128)(2,1)}, bf16[1,2,48,576]{3,2,1,0:T(8,128)(2,1)S(1)}, u32[]{:S(2)}, u32[]{:S(2)}) collective-permute-start(bf16[1,2,48,576]{3,2,1,0:T(8,128)(2,1)} %get-tuple-element.180), channel_id=1, source_target_pairs={{0,16},{2,18},{4,20},{6,22},{8,24},{10,26},{12,28},{14,30},{16,0},... | collective-permute-start | bytes 331784 | tf_op jit(solution)/shard_map/ppermute | solution.py:669
  239.9 21.1 %collective-permute-start.33 = (f32[48,576]{1,0:T(8,128)}, f32[48,576]{1,0:T(8,128)}, u32[]{:S(2)}, u32[]{:S(2)}) collective-permute-start(f32[48,576]{1,0:T(8,128)} %get-tuple-element.231), channel_id=1, source_target_pairs={{0,2},{2,0},{4,6},{6,4},{8,10},{10,8},{12,14},{14,12},{16,18},{18,... | collective-permute-start | bytes 331784 | tf_op jit(solution)/shard_map/ppermute | solution.py:669
  243.0 31.7 %collective-permute-start.35 = (bf16[1,8,48,512]{3,2,1,0:T(8,128)(2,1)}, bf16[1,8,48,512]{3,2,1,0:T(8,128)(2,1)}, u32[]{:S(2)}, u32[]{:S(2)}) collective-permute-start(bf16[1,8,48,512]{3,2,1,0:T(8,128)(2,1)} %get-tuple-element.185), channel_id=1, source_target_pairs={{0,1},{1,0},{2,3},{3,2},{4,5},{5,4},{6,7},{7,6},{8,9},{9,8},{10,11... | collective-permute-start | bytes 1179656 | tf_op jit(solution)/shard_map/ppermute | solution.py:673
  252.8 9.3 %collective-permute-start.42 = (f32[84,128]{1,0:T(8,128)S(1)}, f32[84,128]{1,0:T(8,128)S(1)}, u32[]{:S(2)}, u32[]{:S(2)}) collective-permute-start(f32[84,128]{1,0:T(8,128)S(1)} %add.207), channel_id=1, source_target_pairs={{0,8},{2,10},{4,12},{6,14},{8,0},{10,2},{12,4},{14,6},{16,24},{18,... | collective-permute-start | bytes 129032 | tf_op jit(solution)/shard_map/ppermute | solution.py:669
  259.2 30.5 %collective-permute-start.29 = (bf16[512,768]{1,0:T(8,128)(2,1)}, bf16[512,768]{1,0:T(8,128)(2,1)S(1)}, u32[]{:S(2)}, u32[]{:S(2)}) collective-permute-start(bf16[512,768]{1,0:T(8,128)(2,1)} %fusion.12), channel_id=1, source_target_pairs={{0,0},{1,2},{2,1},{3,3},{4,4},{5,6},{6,5},{7,7},{8,8},{9,10},{10,9... | collective-permute-start | bytes 2359304 | tf_op jit(solution)/shard_map/ppermute | solution.py:682
  262.1 11.9 %collective-permute-start.43 = (f32[84,128]{1,0:T(8,128)S(1)}, f32[84,128]{1,0:T(8,128)S(1)}, u32[]{:S(2)}, u32[]{:S(2)}) collective-permute-start(f32[84,128]{1,0:T(8,128)S(1)} %add.208), channel_id=1, source_target_pairs={{0,1},{1,0},{2,3},{3,2},{4,5},{5,4},{6,7},{7,6},{8,9},{9,8},{10,11... | collective-permute-start | bytes 129032 | tf_op jit(solution)/shard_map/ppermute | solution.py:673
  276.6 10.7 %collective-permute-start.36 = (bf16[4,1,48,512]{3,2,1,0:T(8,128)(2,1)}, bf16[4,1,48,512]{3,2,1,0:T(8,128)(2,1)S(1)}, u32[]{:S(2)}, u32[]{:S(2)}) collective-permute-start(bf16[4,1,48,512]{3,2,1,0:T(8,128)(2,1)} %get-tuple-element.187), channel_id=1, source_target_pairs={{0,16},{2,18},{4,20},{6,22},{8,24},{10,26},{12,28},{14,30},{16,0},... | collective-permute-start | bytes 589832 | tf_op jit(solution)/shard_map/ppermute | solution.py:669
  (62 other events, 419.2 us)
